TPU v7x, 32 devices: a whole 2x2x4 slice. The times are simulated.
32 devices in a mesh: groups: 2 (over y), row: 4 (over z), col: 2 (over x), sub: 2 (over core).
Axes of the slice: x: 2, y: 2, z: 4, core: 2. Of those that a mesh axis runs over, the one named last changes fastest.
Arguments:
- query_acts: bfloat16 [64, 128, 4096], P(('groups', 'col', 'sub'), None, 'row'), parts along dimension 0, may hold values from -6 to 6
- query_grads: bfloat16 [64, 128, 4096], P(('groups', 'col', 'sub'), None, 'row'), parts along dimension 0, may hold values from -0.5390625 to 0.5390625
- proj_in: bfloat16 [4096, 128], P('row'), may hold values from -0.09375 to 0.09375
- proj_out: bfloat16 [4096, 128], P('row'), may hold values from -0.09375 to 0.09375
- inverse_gram: float32 [16384, 16384], P('row', ('col', 'sub')), may hold values from -0.01 to 2.01, as said below
- store_slab: bfloat16 [2048, 16384], P(('groups', 'col'), ('row', 'sub')), parts along dimension 0, may hold values from -0.046875 to 0.046875
Outputs:
- scores: float32 [64, 1024], P('groups', 'col'), parts along dimension 0
There are 2 independent parts, one for each index of `groups`. A program takes and returns all parts, laid end to end along the dimension named above; an argument that names none is the same for every part. Nothing has to cross between parts.
Inputs may be any that keep to these rules, and one draw needn't show every extreme that they name: inverse_gram is symmetric.
All inputs are finite; a program needn't handle non-finite values.
Results may differ from a plain program's by a relative error of at most 0.0029.
Values may be sent and summed in bfloat16 or wider, within the bound.
No kernel may reach another device: no remote copies, remote signals or barrier semaphores. Data moves between devices by JAX's collectives and lax.ppermute only.
A program may use at most 128 MiB of HBM per device.

v0:
```python
import functools

import jax
import jax.numpy as jnp
from jax import lax
from jax.experimental import pallas as pl
from jax.experimental.pallas import tpu as pltpu
from jax.sharding import PartitionSpec as P

HIGHEST = lax.Precision.HIGHEST


def plain_body(query_acts, query_grads, proj_in, proj_out, inverse_gram, store_slab):
    row_count = lax.axis_size("row")
    row_index = lax.axis_index("row")
    sub_index = lax.axis_index("sub")
    in_width = proj_in.shape[1]
    act_part = jnp.einsum("qtd,dk->qtk", query_acts, proj_in, preferred_element_type=jnp.float32)
    grad_part = jnp.einsum("qtd,dk->qtk", query_grads, proj_out, preferred_element_type=jnp.float32)
    store_width = store_slab.shape[1]
    row_block = in_width // row_count
    act_whole, grad_proj = lax.psum((act_part, grad_part), "row")
    act_proj = lax.dynamic_slice_in_dim(act_whole, row_index * row_block, row_block, 2)
    kron_part = jnp.einsum("qta,qtb->qab", act_proj, grad_proj, precision=HIGHEST)
    kron_feats = lax.all_gather(kron_part, ("col", "sub"), axis=0, tiled=True)
    features_flat = kron_feats.reshape(kron_feats.shape[0], -1)
    precond_part = jnp.dot(features_flat, inverse_gram, precision=HIGHEST)
    precond_block = lax.psum(precond_part, "row").astype(jnp.bfloat16)
    precond_full = lax.all_gather(precond_block, ("col", "sub"), axis=1, tiled=True)
    store_start = (row_index * lax.axis_size("sub") + sub_index) * store_width
    precond_mine = lax.dynamic_slice_in_dim(precond_full, store_start, store_width, 1)
    score_part = lax.dot_general(
        precond_mine, store_slab, (((1,), (1,)), ((), ())), preferred_element_type=jnp.float32
    )
    return lax.psum(score_part, ("row", "sub"))


PAD = 8
SHIFT = 13.0
LOG2E = 1.4426950408889634
WHOLE = pl.BlockSpec(memory_space=pltpu.VMEM)
MIB = 2**20


def exponents(part):
    top = jnp.max(jnp.abs(part), axis=0, keepdims=True)
    return jnp.ceil(jnp.log(jnp.clip(top, 1e-30, 1e30)) * LOG2E)


def scaled(part, k):
    return part * jnp.exp2(SHIFT - k)


def restored(part, k):
    return part * jnp.exp2(k - SHIFT)


def project_kernel(place_ref, *refs, targets):
    inputs, outs, (inputs_buf, weights_buf, sems, weights_sems) = refs[:4], refs[4:-4], refs[-4:]
    own, tokens, width = inputs_buf.shape[2:]
    count = own * tokens
    row = place_ref[1]
    weights = [pltpu.make_async_copy(inputs[2 + i], weights_buf.at[i], weights_sems.at[i]) for i in range(2)]
    copies = {}
    for k in range(len(targets)):
        for i in range(2):
            if k == 0:
                weights[i].start()
            rows = pl.ds((row ^ targets[k]) * own, own)
            copies[k, i] = pltpu.make_async_copy(inputs[i].at[rows], inputs_buf.at[i, k], sems.at[i, k])
            copies[k, i].start()
    for k in range(len(targets)):
        for i in range(2):
            if k == 0:
                weights[i].wait()
            copies[k, i].wait()
            x = inputs_buf[i, k].reshape(count, width)
            part = jnp.dot(x, weights_buf[i], preferred_element_type=jnp.float32)
            e = exponents(part)
            outs[k][i * count : (i + 1) * count] = scaled(part, e)
            outs[k][2 * count + i * PAD : 2 * count + (i + 1) * PAD] = jnp.broadcast_to(e, (PAD, e.shape[1]))


def project(targets, row_count, place, query_acts, query_grads, proj_in, proj_out):
    queries, tokens, width = query_acts.shape
    own = queries // row_count
    out_width = proj_in.shape[1]
    height = 2 * own * tokens + 2 * PAD
    far = pl.BlockSpec(memory_space=pltpu.HBM)
    return pl.pallas_call(
        functools.partial(project_kernel, targets=targets),
        in_specs=[pl.BlockSpec(memory_space=pltpu.SMEM)] + [far] * 4,
        out_specs=[WHOLE] * len(targets),
        out_shape=[jax.ShapeDtypeStruct((height, out_width), jnp.float32)] * len(targets),
        scratch_shapes=[
            pltpu.VMEM((2, len(targets), own, tokens, width), query_acts.dtype),
            pltpu.VMEM((2,) + proj_in.shape, proj_in.dtype),
            pltpu.SemaphoreType.DMA((2, len(targets))),
            pltpu.SemaphoreType.DMA((2,)),
        ],
        compiler_params=pltpu.CompilerParams(vmem_limit_bytes=8 * MIB),
        name="project",
    )(place, *[pltpu.with_memory_space_constraint(x, pltpu.HBM) for x in (query_acts, query_grads, proj_in, proj_out)])


def kron_kernel(place_ref, after_ref, own_ref, *refs, tokens):
    del after_ref
    refs, outs, scratch = refs[:-5], refs[-5:-1], refs[-1]
    count = (own_ref.shape[0] - 2 * PAD) // 2
    sums = []
    for i in range(2):
        total = None
        for ref in (own_ref,) + refs:
            k = 2 * count + i * PAD
            part = restored(ref[i * count : (i + 1) * count], ref[k : k + 1])
            total = part if total is None else total + part
        sums.append(total)
    acts, grads = sums
    height = acts.shape[1] // 8
    group, col, sub = place_ref[0], place_ref[2], place_ref[3]
    for j in range(count // tokens):
        rows = slice(j * tokens, (j + 1) * tokens)
        scratch[j] = lax.dot_general(
            acts[rows], grads[rows], (((0,), (0,)), ((), ())), precision=HIGHEST, preferred_element_type=jnp.float32
        )
        for k in range(4):
            for s in range(2):
                start = (((col ^ (k % 2)) * 2 + (sub ^ s)) * 2 + (group ^ (k // 2))) * height
                outs[k][s, j * height : (j + 1) * height] = scratch[j, pl.ds(pl.multiple_of(start, height), height)]


def pack_kernel(*refs):
    kept, got_ref, out_ref = refs[:-2], refs[-2], refs[-1]
    lanes = got_ref.shape[-1]
    parts = jnp.concatenate([ref[0] for ref in kept] + [got_ref[...].reshape(-1, lanes)], 0)
    k = exponents(parts)
    out_ref[: parts.shape[0]] = scaled(parts, k)
    out_ref[parts.shape[0] :] = jnp.broadcast_to(k, (PAD, lanes))


def pack_scores_kernel(scores_ref, out_ref):
    scores = scores_ref[...]
    k = exponents(scores)
    out_ref[: scores.shape[0]] = scaled(scores, k)
    out_ref[scores.shape[0] :] = jnp.broadcast_to(k, (PAD, scores.shape[1]))


def sum_scores_kernel(*refs):
    out_ref = refs[-1]
    count = out_ref.shape[0]
    out_ref[...] = tree_sum([restored(ref[:count], ref[count : count + 1]) for ref in refs[:-1]])


def split(block):
    high = block.astype(jnp.bfloat16)
    return high, (block - high.astype(jnp.float32)).astype(jnp.bfloat16)


def gram_split_kernel(place_ref, after_ref, gram_ref, *refs, first):
    del after_ref
    outs, (mark_ref, buffer, sems) = refs[:-3], refs[-3:]
    slots, tile, width = buffer.shape
    quarter = outs[0].shape[0] // 2
    steps = quarter // tile
    total = steps * len(outs)
    column = pl.multiple_of(place_ref[0] * width, width)
    sub = place_ref[3]

    def copy(i):
        part = first + i // steps
        start = (lax.rem(part // 2 + 1 + sub, 2) * 2 + lax.rem(part, 2)) * quarter + lax.rem(i, steps) * tile
        rows = pl.ds(pl.multiple_of(start, tile), tile)
        slot = lax.rem(i, slots)
        return pltpu.make_async_copy(gram_ref.at[rows, pl.ds(column, width)], buffer.at[slot], sems.at[slot])

    for i in range(min(slots - 1, total)):
        copy(i).start()

    for part, out_ref in enumerate(outs):

        @pl.loop(0, steps)
        def _(j):
            i = part * steps + j

            @pl.when(i + slots - 1 < total)
            def _():
                copy(i + slots - 1).start()

            copy(i).wait()
            high, low = split(buffer[lax.rem(i, slots)])
            start = pl.multiple_of(j * tile, tile)
            out_ref[pl.ds(start, tile)] = high
            out_ref[pl.ds(start + quarter, tile)] = low

    mark_ref[...] = jnp.zeros_like(mark_ref)


def gram_split(place, after, inverse_gram, first, count, tile=256, slots=4):
    rows, width = inverse_gram.shape
    half, quarter = width // 2, rows // 4
    tile = min(tile, quarter)
    *quarters, mark = pl.pallas_call(
        functools.partial(gram_split_kernel, first=first),
        in_specs=[pl.BlockSpec(memory_space=pltpu.SMEM), WHOLE, pl.BlockSpec(memory_space=pltpu.HBM)],
        out_specs=[WHOLE] * (count + 1),
        out_shape=[pltpu.VMEM((2 * quarter, half), jnp.bfloat16)] * count
        + [jax.ShapeDtypeStruct((8, 128), jnp.float32)],
        scratch_shapes=[pltpu.VMEM((slots, tile, half), jnp.float32), pltpu.SemaphoreType.DMA((slots,))],
        compiler_params=pltpu.CompilerParams(vmem_limit_bytes=12 * MIB),
        cost_estimate=pl.CostEstimate(flops=0, bytes_accessed=count * 4 * quarter * half, transcendentals=0),
        name="gram_split",
    )(place, after, inverse_gram)
    return [pltpu.with_memory_space_constraint(x, pltpu.VMEM) for x in quarters], mark


def gram_rows(group, gram_ref, terms, write):
    quarter = gram_ref.shape[0] // 2
    queries = terms.shape[1] // 2
    part = jnp.dot(gram_ref[...], terms[...], preferred_element_type=jnp.float32)
    part = part[:quarter] + part[quarter:]
    done = (part[:, :queries] + part[:, queries:]).T
    for g in range(2):
        write(g ^ group, done[g * (queries // 2) : (g + 1) * (queries // 2)])


def away_kernel(place_ref, after_ref, *refs, row_count, own):
    del after_ref
    grams, sources, (out_ref, terms, natural) = refs[:2], refs[2 : 2 + row_count], refs[2 + row_count :]
    group, row, col, sub = (place_ref[i] for i in range(4))
    height, queries, lanes = natural.shape
    for z in range(row_count):
        count = sources[z].shape[0] - PAD
        piece = restored(sources[z][:count], sources[z][count : count + 1])
        for place in range(8):
            s, g, c = place // 4, place // 2 % 2, place % 2
            first = ((((g ^ group) * 2 + (c ^ col)) * 2 + (s ^ sub)) * row_count + (z ^ row)) * own
            for j in range(own):
                start = (place * own + j) * height
                natural[:, pl.ds(first + j, 1), :] = piece[start : start + height].reshape(height, 1, lanes)
    for a in range(height):
        block = natural[a]
        high = block.astype(jnp.bfloat16).astype(jnp.float32)
        both = jnp.concatenate([high, block - high], 0).T
        terms[a * lanes : (a + 1) * lanes] = both.astype(jnp.bfloat16)
    for i in range(2):

        def write(g, value):
            out_ref[i, g] = value

        gram_rows(group, grams[i], terms, write)


def home_kernel(place_ref, gram_ref, terms_ref, *refs):
    out_ref = refs[-1]

    def write(g, value):
        out_ref[g] = value

    gram_rows(place_ref[0], gram_ref, terms_ref, write)


def join_kernel(early_ref, early_got_ref, late_ref, late_got_ref, early_out, early_wire, late_out, late_wire):
    early = early_ref[...] + early_got_ref[...].astype(jnp.float32)
    early_out[...] = early
    early_wire[...] = early.astype(jnp.bfloat16)
    late_out[...] = late_ref[0] + late_got_ref[0]
    late_wire[...] = (late_ref[1] + late_got_ref[1]).astype(jnp.bfloat16)


def gram_product(place, after, quarters, sources, own, lanes):
    quarter, half = quarters[0].shape[0] // 2, quarters[0].shape[1]
    row_count = len(sources)
    queries = 8 * row_count * own
    index = pl.BlockSpec(memory_space=pltpu.SMEM)

    def common(count):
        return dict(
            compiler_params=pltpu.CompilerParams(vmem_limit_bytes=8 * MIB),
            cost_estimate=pl.CostEstimate(
                flops=8 * count * queries * quarter * half, bytes_accessed=count * quarter * half, transcendentals=0
            ),
        )

    away, terms = pl.pallas_call(
        functools.partial(away_kernel, row_count=row_count, own=own),
        in_specs=[index] + [WHOLE] * (3 + row_count),
        out_specs=[WHOLE, WHOLE],
        out_shape=[
            jax.ShapeDtypeStruct((2, 2, queries // 2, quarter), jnp.float32),
            jax.ShapeDtypeStruct((half, 2 * queries), jnp.bfloat16),
        ],
        scratch_shapes=[pltpu.VMEM((half // lanes, queries, lanes), jnp.float32)],
        name="away",
        **common(2),
    )(place, after, *quarters[:2], *sources)
    got = swapped(away, "sub")

    def home(i, *after):
        return pl.pallas_call(
            home_kernel,
            in_specs=[index] + [WHOLE] * (2 + len(after)),
            out_specs=WHOLE,
            out_shape=jax.ShapeDtypeStruct((2, queries // 2, quarter), jnp.float32),
            name="home",
            **common(1),
        )(place, quarters[2 + i], terms, *after)

    early = home(0) + got[0]
    wire = early[1].astype(jnp.bfloat16)
    late = home(1, wire)
    shape = (queries // 2, quarter)
    early, early_wire, late, late_wire = pl.pallas_call(
        join_kernel,
        in_specs=[WHOLE] * 4,
        out_specs=[WHOLE] * 4,
        out_shape=[jax.ShapeDtypeStruct(shape, kind) for kind in (jnp.float32, jnp.bfloat16) * 2],
        compiler_params=pltpu.CompilerParams(vmem_limit_bytes=4 * MIB),
        name="join",
    )(early[0], swapped(wire, "groups"), late, got[1])
    late = late + swapped(late_wire, "groups").astype(jnp.float32)
    early = early + swapped(early_wire, "col").astype(jnp.float32)
    late = late + swapped(late.astype(jnp.bfloat16), "col").astype(jnp.float32)
    return jnp.concatenate([early, late], 1)


def others(pick, axis):
    size = lax.axis_size(axis)
    index = lax.axis_index(axis)
    return [lax.ppermute(pick(index ^ k), axis, [(i, i ^ k) for i in range(size)]) for k in range(1, size)]


def tree_sum(terms):
    while len(terms) > 1:
        terms = [terms[i] + terms[i + 1] for i in range(0, len(terms), 2)]
    return terms[0]


def swapped(array, axis):
    return others(lambda d: array, axis)[0]


def peers(pick):
    return [lax.ppermute(pick(k), ("groups", "col"), [(i, i ^ k) for i in range(4)]) for k in (1, 2, 3)]


def call(kernel, shapes, name, *args, specs=None, scratch=()):
    specs = specs or [pl.BlockSpec(memory_space=pltpu.SMEM) if a.dtype == jnp.int32 else WHOLE for a in args]
    many = isinstance(shapes, list)
    shapes = [jax.ShapeDtypeStruct(shape, jnp.float32) for shape in (shapes if many else [shapes])]
    outs = pl.pallas_call(
        kernel,
        in_specs=specs,
        out_specs=[WHOLE] * len(shapes),
        out_shape=shapes,
        scratch_shapes=list(scratch),
        compiler_params=pltpu.CompilerParams(vmem_limit_bytes=4 * MIB),
        name=name,
    )(*args)
    return outs if many else outs[0]


def body(query_acts, query_grads, proj_in, proj_out, inverse_gram, store_slab):
    row_count = lax.axis_size("row")
    place = jnp.stack([lax.axis_index(axis) for axis in ("groups", "row", "col", "sub")])
    queries, tokens = query_acts.shape[:2]
    own = queries // row_count
    in_width, out_width = proj_in.shape[1], proj_out.shape[1]
    got = []
    for targets in (range(row_count)[: row_count // 2 - 1 : -1], range(row_count)[: row_count // 2][::-1]):
        parts = project(targets, row_count, place, query_acts, query_grads, proj_in, proj_out)
        for k, part in zip(targets, parts):
            if k:
                got.append(lax.ppermute(part.astype(jnp.float16), "row", [(i, i ^ k) for i in range(row_count)]))
    first, mark = gram_split(place, parts[-1], inverse_gram, 0, 3)
    height = own * in_width // 8
    near = call(
        functools.partial(kron_kernel, tokens=tokens),
        [(2, height, out_width)] * 4,
        "kron",
        place,
        mark,
        parts[-1],
        *[x.astype(jnp.float32) for x in got],
        scratch=[pltpu.VMEM((own, in_width, out_width), jnp.float32)],
    )
    near = [near[0]] + peers(lambda k: near[k])
    got = swapped(jnp.stack([x[1] for x in near]), "sub")
    packed = call(pack_kernel, (8 * height + PAD, out_width), "pack", *near, got)
    wire = packed.astype(jnp.float16)
    sources = [packed] + [got.astype(jnp.float32) for got in others(lambda d: wire, "row")]
    last, mark = gram_split(place, packed, inverse_gram, 3, 1)
    total = gram_product(place, mark, first + last, sources, own, out_width)
    high = lax.reduce_precision(total, 8, 7)
    terms = jnp.concatenate([high, total - high], 0).astype(jnp.bfloat16)
    scores = lax.dot_general(
        terms, store_slab, (((1,), (1,)), ((), ())), preferred_element_type=jnp.float32
    )
    scores = scores[: total.shape[0]] + scores[total.shape[0] :]
    scores = scores + swapped(scores, "sub")
    packed = call(pack_scores_kernel, (scores.shape[0] + PAD, scores.shape[1]), "pack_scores", scores)
    packed = lax.reduce_precision(packed, 5, 10)
    wire = packed.astype(jnp.float16)
    sources = [packed] + [got.astype(jnp.float32) for got in others(lambda d: wire, "row")]
    return call(sum_scores_kernel, scores.shape, "sum_scores", *sources)


def solution(mesh):
    shape = mesh.shape
    rows = shape["row"]
    paired = shape["groups"] == shape["col"] == shape["sub"] == 2 and rows & (rows - 1) == 0

    def chosen(query_acts, query_grads, proj_in, proj_out, *rest):
        queries = query_acts.shape[0] // (shape["groups"] * shape["col"] * shape["sub"])
        square = proj_in.shape[1] == proj_out.shape[1] == 128
        chosen_body = body if paired and square and queries % rows == 0 else plain_body
        return jax.shard_map(
            chosen_body,
            mesh=mesh,
            in_specs=(
                P(("groups", "col", "sub"), None, "row"),
                P(("groups", "col", "sub"), None, "row"),
                P("row", None),
                P("row", None),
                P("row", ("col", "sub")),
                P(("groups", "col"), ("row", "sub")),
            ),
            out_specs=P("groups", "col"),
            check_vma=False,
        )(query_acts, query_grads, proj_in, proj_out, *rest)

    return chosen
```

profile of v0, /device:TPU:0, one launch (start us, length us, event | category | flops | bytes accessed | tf_op | source)
XLA Modules:
  0.0 74.9 jit_solution(7629627561353559197)
XLA Ops:
  0.1 3.1 %project.3 = (f32[528,128]{1,0:T(8,128)S(1)}, f32[528,128]{1,0:T(8,128)S(1)}) custom-call(s32[4]{0:T(128)S(1)} %pad_add_fusion.place_ref, bf16[8,128,1024]{2,1,0:T(8,128)(2,1)} %refs_0_.3, bf16[8,128,1024]{2,1,0:T(8,128)(2,1)} %refs_1_.3, bf16[1024,128]{1,0:T(8,128)(2,1)} %refs_2_.3, bf16[1024,128]{1,0:T(8,128)(2,1)} %refs_3_.3), custom_call_target="tpu_custom_call" | custom-call | tf_op jit(solution)/shard_map/project/pallas_call | solution.py:90
  3.2 4.1 %collective-permute-start.1 = (f16[528,128]{1,0:T(8,128)(2,1)S(1)}, f16[528,128]{1,0:T(8,128)(2,1)S(1)}, u32[]{:S(2)}, u32[]{:S(2)}) collective-permute-start(f16[528,128]{1,0:T(8,128)(2,1)S(1)} %convert_element_type.60), channel_id=1, source_target_pairs={{0,8},{4,12},{8,0},{12,4},{1,9},{5,13},{9,1},{13,5},{2,10},{6,14},... | collective-permute-start | bytes 405512 | tf_op jit(solution)/shard_map/ppermute | solution.py:373
  7.3 1.4 %collective-permute-start = (f16[528,128]{1,0:T(8,128)(2,1)S(1)}, f16[528,128]{1,0:T(8,128)(2,1)S(1)}, u32[]{:S(2)}, u32[]{:S(2)}) collective-permute-start(f16[528,128]{1,0:T(8,128)(2,1)S(1)} %convert_element_type.58), channel_id=1, source_target_pairs={{0,12},{4,8},{8,4},{12,0},{1,13},{5,9},{9,5},{13,1},{2,14},{6,10},... | collective-permute-start | bytes 405512 | tf_op jit(solution)/shard_map/ppermute | solution.py:373
  8.8 3.1 %project.2 = (f32[528,128]{1,0:T(8,128)S(1)}, f32[528,128]{1,0:T(8,128)S(1)}) custom-call(s32[4]{0:T(128)S(1)} %pad_add_fusion.place_ref, bf16[8,128,1024]{2,1,0:T(8,128)(2,1)} %refs_0_.3, bf16[8,128,1024]{2,1,0:T(8,128)(2,1)} %refs_1_.3, bf16[1024,128]{1,0:T(8,128)(2,1)} %refs_2_.3, bf16[1024,128]{1,0:T(8,128)(2,1)} %refs_3_.3), custom_call_target="tpu_custom_call" | custom-call | tf_op jit(solution)/shard_map/project/pallas_call | solution.py:90
  12.2 9.4 %gram_split.2 = (bf16[2048,2048]{1,0:T(8,128)(2,1)S(1)}, bf16[2048,2048]{1,0:T(8,128)(2,1)S(1)}, bf16[2048,2048]{1,0:T(8,128)(2,1)S(1)}, f32[8,128]{1,0:T(8,128)S(1)}) custom-call(s32[4]{0:T(128)S(1)} %pad_add_fusion.place_ref, f32[528,128]{1,0:T(8,128)S(1)} %get-tuple-element.25.after_ref.own_ref, f32[4096,4096]{1,0:T(8,128)} %gram_ref.3), custom_call_target="tpu_custom_call" | custom-call | bytes 25165824 | tf_op jit(solution)/shard_map/gram_split/pallas_call | solution.py:202
  22.6 1.6 %collective-permute-start.3 = (f32[2,32,128]{2,1,0:T(8,128)S(1)}, f32[2,32,128]{2,1,0:T(8,128)S(1)}, u32[]{:S(2)}, u32[]{:S(2)}) collective-permute-start(f32[2,32,128]{2,1,0:T(8,128)S(1)} %get-tuple-element.32), channel_id=1, source_target_pairs={{0,2},{2,0},{16,18},{18,16},{1,3},{3,1},{17,19},{19,17},{4,6},{6,4... | collective-permute-start | bytes 98312 | tf_op jit(solution)/shard_map/ppermute | solution.py:343
  24.1 1.5 %collective-permute-start.4 = (f32[2,32,128]{2,1,0:T(8,128)S(1)}, f32[2,32,128]{2,1,0:T(8,128)S(1)}, u32[]{:S(2)}, u32[]{:S(2)}) collective-permute-start(f32[2,32,128]{2,1,0:T(8,128)S(1)} %get-tuple-element.33), channel_id=1, source_target_pairs={{0,16},{2,18},{16,0},{18,2},{1,17},{3,19},{17,1},{19,3},{4,20},{6,... | collective-permute-start | bytes 98312 | tf_op jit(solution)/shard_map/ppermute | solution.py:343
  26.5 1.8 %collective-permute-done.4.refs_2_ = f32[2,32,128]{2,1,0:T(8,128)S(1)} collective-permute-done((f32[2,32,128]{2,1,0:T(8,128)S(1)}, f32[2,32,128]{2,1,0:T(8,128)S(1)}, u32[]{:S(2)}, u32[]{:S(2)}) %collective-permute-start.4) | collective-permute-done | bytes 32800 | tf_op jit(solution)/shard_map/ppermute | solution.py:343
  28.4 2.1 %collective-permute-done.5.refs_3_ = f32[2,32,128]{2,1,0:T(8,128)S(1)} collective-permute-done((f32[2,32,128]{2,1,0:T(8,128)S(1)}, f32[2,32,128]{2,1,0:T(8,128)S(1)}, u32[]{:S(2)}, u32[]{:S(2)}) %collective-permute-start.5) | collective-permute-done | bytes 32800 | tf_op jit(solution)/shard_map/ppermute | solution.py:343
  30.6 1.2 %collective-permute-done.6.refs_4_ = f32[4,32,128]{2,1,0:T(8,128)S(1)} collective-permute-done((f32[4,32,128]{2,1,0:T(8,128)S(1)}, f32[4,32,128]{2,1,0:T(8,128)S(1)}, u32[]{:S(2)}, u32[]{:S(2)}) %collective-permute-start.6) | collective-permute-done | bytes 65568 | tf_op jit(solution)/shard_map/ppermute | solution.py:329
  31.9 3.0 %collective-permute-start.9 = (f16[264,128]{1,0:T(8,128)(2,1)S(1)}, f16[264,128]{1,0:T(8,128)(2,1)S(1)}, u32[]{:S(2)}, u32[]{:S(2)}) collective-permute-start(f16[264,128]{1,0:T(8,128)(2,1)S(1)} %convert_element_type.64), channel_id=1, source_target_pairs={{0,12},{4,8},{8,4},{12,0},{1,13},{5,9},{9,5},{13,1},{2,14},{6,10},... | collective-permute-start | bytes 202760 | tf_op jit(solution)/shard_map/ppermute | solution.py:329
  35.2 1.1 %collective-permute-start.7 = (f16[264,128]{1,0:T(8,128)(2,1)S(1)}, f16[264,128]{1,0:T(8,128)(2,1)S(1)}, u32[]{:S(2)}, u32[]{:S(2)}) collective-permute-start(f16[264,128]{1,0:T(8,128)(2,1)S(1)} %convert_element_type.64), channel_id=1, source_target_pairs={{0,4},{4,0},{8,12},{12,8},{1,5},{5,1},{9,13},{13,9},{2,6},{6,2},{1... | collective-permute-start | bytes 202760 | tf_op jit(solution)/shard_map/ppermute | solution.py:329
  36.3 4.4 %gram_split.3 = (bf16[2048,2048]{1,0:T(8,128)(2,1)S(1)}, f32[8,128]{1,0:T(8,128)S(1)}) custom-call(s32[4]{0:T(128)S(1)} %pad_add_fusion.place_ref, f32[264,128]{1,0:T(8,128)S(1)} %pack.1.after_ref.refs_2_, f32[4096,4096]{1,0:T(8,128)} %gram_ref.3), custom_call_target="tpu_custom_call" | custom-call | bytes 8388608 | tf_op jit(solution)/shard_map/gram_split/pallas_call | solution.py:202
  40.7 1.0 %collective-permute-done.8 = f16[264,128]{1,0:T(8,128)(2,1)S(1)} collective-permute-done((f16[264,128]{1,0:T(8,128)(2,1)S(1)}, f16[264,128]{1,0:T(8,128)(2,1)S(1)}, u32[]{:S(2)}, u32[]{:S(2)}) %collective-permute-start.8) | collective-permute-done | bytes 67616 | tf_op jit(solution)/shard_map/ppermute | solution.py:329
  41.7 6.1 %away.1 = (f32[2,2,32,1024]{3,2,1,0:T(8,128)S(1)}, bf16[2048,128]{1,0:T(8,128)(2,1)S(1)}) custom-call(s32[4]{0:T(128)S(1)} %pad_add_fusion.place_ref, f32[8,128]{1,0:T(8,128)S(1)} %get-tuple-element.35.after_ref, bf16[2048,2048]{1,0:T(8,128)(2,1)S(1)} %get-tuple-element.36.refs_0_, bf16[2048,2048]{1,0:T(8,128)(2,1)S(1)} %get-tuple-element.37.refs_1_, ...), custom_call_target="tpu_custom_call" | custom-call | flops 2147483648 | bytes 4194304 | tf_op jit(solution)/shard_map/away/pallas_call | solution.py:284
  47.9 3.1 %home.2 = f32[2,32,1024]{2,1,0:T(8,128)S(1)} custom-call(s32[4]{0:T(128)S(1)} %pad_add_fusion.place_ref, bf16[2048,2048]{1,0:T(8,128)(2,1)S(1)} %get-tuple-element.26.gram_ref, bf16[2048,128]{1,0:T(8,128)(2,1)S(1)} %get-tuple-element.38.terms_ref), custom_call_target="tpu_custom_call" | custom-call | flops 1073741824 | bytes 2097152 | tf_op jit(solution)/shard_map/home/pallas_call | solution.py:299
  51.7 3.1 %home.3.late_ref = f32[2,32,1024]{2,1,0:T(8,128)S(1)} custom-call(s32[4]{0:T(128)S(1)} %pad_add_fusion.place_ref, bf16[2048,2048]{1,0:T(8,128)(2,1)S(1)} %get-tuple-element.40.gram_ref, bf16[2048,128]{1,0:T(8,128)(2,1)S(1)} %get-tuple-element.38.terms_ref, bf16[32,1024]{1,0:T(8,128)(2,1)S(1)} %fusion.7.refs_0_), custom_call_target="tpu_custom_call" | custom-call | flops 1073741824 | bytes 2097152 | tf_op jit(solution)/shard_map/home/pallas_call | solution.py:299
  57.0 3.0 %collective-permute-done.13 = bf16[32,1024]{1,0:T(8,128)(2,1)S(1)} collective-permute-done((bf16[32,1024]{1,0:T(8,128)(2,1)S(1)}, bf16[32,1024]{1,0:T(8,128)(2,1)S(1)}, u32[]{:S(2)}, u32[]{:S(2)}) %collective-permute-start.13) | collective-permute-done | bytes 65568 | tf_op jit(solution)/shard_map/ppermute | solution.py:329
  60.8 3.6 %collective-permute-done.14 = bf16[32,1024]{1,0:T(8,128)(2,1)S(1)} collective-permute-done((bf16[32,1024]{1,0:T(8,128)(2,1)S(1)}, bf16[32,1024]{1,0:T(8,128)(2,1)S(1)}, u32[]{:S(2)}, u32[]{:S(2)}) %collective-permute-start.14) | collective-permute-done | bytes 65568 | tf_op jit(solution)/shard_map/ppermute | solution.py:329
  65.3 1.2 %collective-permute-done.15 = f32[32,512]{1,0:T(8,128)S(1)} collective-permute-done((f32[32,512]{1,0:T(8,128)S(1)}, f32[32,512]{1,0:T(8,128)S(1)}, u32[]{:S(2)}, u32[]{:S(2)}) %collective-permute-start.15) | collective-permute-done | bytes 65568 | tf_op jit(solution)/shard_map/ppermute | solution.py:329
  66.7 2.6 %collective-permute-start.18 = (f16[40,512]{1,0:T(8,128)(2,1)S(1)}, f16[40,512]{1,0:T(8,128)(2,1)S(1)}, u32[]{:S(2)}, u32[]{:S(2)}) collective-permute-start(f16[40,512]{1,0:T(8,128)(2,1)S(1)} %get-tuple-element.47), channel_id=1, source_target_pairs={{0,12},{4,8},{8,4},{12,0},{1,13},{5,9},{9,5},{13,1},{2,14},{6,10},... | collective-permute-start | bytes 122888 | tf_op jit(solution)/shard_map/ppermute | solution.py:329
  69.3 1.9 %collective-permute-start.16 = (f16[40,512]{1,0:T(8,128)(2,1)S(1)}, f16[40,512]{1,0:T(8,128)(2,1)S(1)}, u32[]{:S(2)}, u32[]{:S(2)}) collective-permute-start(f16[40,512]{1,0:T(8,128)(2,1)S(1)} %get-tuple-element.47), channel_id=1, source_target_pairs={{0,4},{4,0},{8,12},{12,8},{1,5},{5,1},{9,13},{13,9},{2,6},{6,2},{1... | collective-permute-start | bytes 122888 | tf_op jit(solution)/shard_map/ppermute | solution.py:329
  71.1 1.5 %collective-permute-done.18 = f16[40,512]{1,0:T(8,128)(2,1)S(1)} collective-permute-done((f16[40,512]{1,0:T(8,128)(2,1)S(1)}, f16[40,512]{1,0:T(8,128)(2,1)S(1)}, u32[]{:S(2)}, u32[]{:S(2)}) %collective-permute-start.18) | collective-permute-done | bytes 40992 | tf_op jit(solution)/shard_map/ppermute | solution.py:329
  72.6 1.5 %collective-permute-done.17 = f16[40,512]{1,0:T(8,128)(2,1)S(1)} collective-permute-done((f16[40,512]{1,0:T(8,128)(2,1)S(1)}, f16[40,512]{1,0:T(8,128)(2,1)S(1)}, u32[]{:S(2)}, u32[]{:S(2)}) %collective-permute-start.17) | collective-permute-done | bytes 40992 | tf_op jit(solution)/shard_map/ppermute | solution.py:329
  (59 shorter events, 8.1 us)
Async XLA Ops:
  0.0 64.5 %copy-start = (bf16[512,2048]{1,0:T(8,128)(2,1)S(1)}, bf16[512,2048]{1,0:T(8,128)(2,1)}, u32[]{:S(2)}) copy-start(bf16[512,2048]{1,0:T(8,128)(2,1)} %param.11) | copy-start | bytes 6291460
  3.2 18.3 %collective-permute-start.1 = (f16[528,128]{1,0:T(8,128)(2,1)S(1)}, f16[528,128]{1,0:T(8,128)(2,1)S(1)}, u32[]{:S(2)}, u32[]{:S(2)}) collective-permute-start(f16[528,128]{1,0:T(8,128)(2,1)S(1)} %convert_element_type.60), channel_id=1, source_target_pairs={{0,8},{4,12},{8,0},{12,4},{1,9},{5,13},{9,1},{13,5},{2,10},{6,14},... | collective-permute-start | bytes 405512 | tf_op jit(solution)/shard_map/ppermute | solution.py:373
  7.3 14.3 %collective-permute-start = (f16[528,128]{1,0:T(8,128)(2,1)S(1)}, f16[528,128]{1,0:T(8,128)(2,1)S(1)}, u32[]{:S(2)}, u32[]{:S(2)}) collective-permute-start(f16[528,128]{1,0:T(8,128)(2,1)S(1)} %convert_element_type.58), channel_id=1, source_target_pairs={{0,12},{4,8},{8,4},{12,0},{1,13},{5,9},{9,5},{13,1},{2,14},{6,10},... | collective-permute-start | bytes 405512 | tf_op jit(solution)/shard_map/ppermute | solution.py:373
  11.9 9.8 %collective-permute-start.2 = (f16[528,128]{1,0:T(8,128)(2,1)S(1)}, f16[528,128]{1,0:T(8,128)(2,1)S(1)}, u32[]{:S(2)}, u32[]{:S(2)}) collective-permute-start(f16[528,128]{1,0:T(8,128)(2,1)S(1)} %convert_element_type.62), channel_id=1, source_target_pairs={{0,4},{4,0},{8,12},{12,8},{1,5},{5,1},{9,13},{13,9},{2,6},{6,2},{1... | collective-permute-start | bytes 405512 | tf_op jit(solution)/shard_map/ppermute | solution.py:373
  22.6 4.0 %collective-permute-start.3 = (f32[2,32,128]{2,1,0:T(8,128)S(1)}, f32[2,32,128]{2,1,0:T(8,128)S(1)}, u32[]{:S(2)}, u32[]{:S(2)}) collective-permute-start(f32[2,32,128]{2,1,0:T(8,128)S(1)} %get-tuple-element.32), channel_id=1, source_target_pairs={{0,2},{2,0},{16,18},{18,16},{1,3},{3,1},{17,19},{19,17},{4,6},{6,4... | collective-permute-start | bytes 98312 | tf_op jit(solution)/shard_map/ppermute | solution.py:343
  24.1 4.3 %collective-permute-start.4 = (f32[2,32,128]{2,1,0:T(8,128)S(1)}, f32[2,32,128]{2,1,0:T(8,128)S(1)}, u32[]{:S(2)}, u32[]{:S(2)}) collective-permute-start(f32[2,32,128]{2,1,0:T(8,128)S(1)} %get-tuple-element.33), channel_id=1, source_target_pairs={{0,16},{2,18},{16,0},{18,2},{1,17},{3,19},{17,1},{19,3},{4,20},{6,... | collective-permute-start | bytes 98312 | tf_op jit(solution)/shard_map/ppermute | solution.py:343
  25.6 4.8 %collective-permute-start.5 = (f32[2,32,128]{2,1,0:T(8,128)S(1)}, f32[2,32,128]{2,1,0:T(8,128)S(1)}, u32[]{:S(2)}, u32[]{:S(2)}) collective-permute-start(f32[2,32,128]{2,1,0:T(8,128)S(1)} %get-tuple-element.34), channel_id=1, source_target_pairs={{0,18},{2,16},{16,2},{18,0},{1,19},{3,17},{17,3},{19,1},{4,22},{6,... | collective-permute-start | bytes 98312 | tf_op jit(solution)/shard_map/ppermute | solution.py:343
  30.5 1.3 %collective-permute-start.6 = (f32[4,32,128]{2,1,0:T(8,128)S(1)}, f32[4,32,128]{2,1,0:T(8,128)S(1)}, u32[]{:S(2)}, u32[]{:S(2)}) collective-permute-start(f32[4,32,128]{2,1,0:T(8,128)S(1)} %pad_maximum_fusion.1), channel_id=1, source_target_pairs={{0,1},{1,0},{2,3},{3,2},{4,5},{5,4},{6,7},{7,6},{8,9},{9,8},{10,11... | collective-permute-start | bytes 196616 | tf_op jit(solution)/shard_map/ppermute | solution.py:329
  31.9 8.8 %collective-permute-start.9 = (f16[264,128]{1,0:T(8,128)(2,1)S(1)}, f16[264,128]{1,0:T(8,128)(2,1)S(1)}, u32[]{:S(2)}, u32[]{:S(2)}) collective-permute-start(f16[264,128]{1,0:T(8,128)(2,1)S(1)} %convert_element_type.64), channel_id=1, source_target_pairs={{0,12},{4,8},{8,4},{12,0},{1,13},{5,9},{9,5},{13,1},{2,14},{6,10},... | collective-permute-start | bytes 202760 | tf_op jit(solution)/shard_map/ppermute | solution.py:329
  34.8 6.9 %collective-permute-start.8 = (f16[264,128]{1,0:T(8,128)(2,1)S(1)}, f16[264,128]{1,0:T(8,128)(2,1)S(1)}, u32[]{:S(2)}, u32[]{:S(2)}) collective-permute-start(f16[264,128]{1,0:T(8,128)(2,1)S(1)} %convert_element_type.64), channel_id=1, source_target_pairs={{0,8},{4,12},{8,0},{12,4},{1,9},{5,13},{9,1},{13,5},{2,10},{6,14},... | collective-permute-start | bytes 202760 | tf_op jit(solution)/shard_map/ppermute | solution.py:329
  35.2 6.5 %collective-permute-start.7 = (f16[264,128]{1,0:T(8,128)(2,1)S(1)}, f16[264,128]{1,0:T(8,128)(2,1)S(1)}, u32[]{:S(2)}, u32[]{:S(2)}) collective-permute-start(f16[264,128]{1,0:T(8,128)(2,1)S(1)} %convert_element_type.64), channel_id=1, source_target_pairs={{0,4},{4,0},{8,12},{12,8},{1,5},{5,1},{9,13},{13,9},{2,6},{6,2},{1... | collective-permute-start | bytes 202760 | tf_op jit(solution)/shard_map/ppermute | solution.py:329
  47.8 3.2 %collective-permute-start.10 = (f32[2,2,32,1024]{3,2,1,0:T(8,128)S(1)}, f32[2,2,32,1024]{3,2,1,0:T(8,128)S(1)}, u32[]{:S(2)}, u32[]{:S(2)}) collective-permute-start(f32[2,2,32,1024]{3,2,1,0:T(8,128)S(1)} %get-tuple-element.39), channel_id=1, source_target_pairs={{0,1},{1,0},{2,3},{3,2},{4,5},{5,4},{6,7},{7,6},{8,9},{9,8},{10,11... | collective-permute-start | bytes 1572872 | tf_op jit(solution)/shard_map/ppermute | solution.py:329
  51.1 4.6 %collective-permute-start.11 = (bf16[32,1024]{1,0:T(8,128)(2,1)S(1)}, bf16[32,1024]{1,0:T(8,128)(2,1)S(1)}, u32[]{:S(2)}, u32[]{:S(2)}) collective-permute-start(bf16[32,1024]{1,0:T(8,128)(2,1)S(1)} %fusion.7.refs_0_), channel_id=1, source_target_pairs={{0,16},{16,0},{1,17},{17,1},{2,18},{18,2},{3,19},{19,3},{4,20},{20... | collective-permute-start | bytes 196616 | tf_op jit(solution)/shard_map/ppermute | solution.py:329
  55.7 4.3 %collective-permute-start.13 = (bf16[32,1024]{1,0:T(8,128)(2,1)S(1)}, bf16[32,1024]{1,0:T(8,128)(2,1)S(1)}, u32[]{:S(2)}, u32[]{:S(2)}) collective-permute-start(bf16[32,1024]{1,0:T(8,128)(2,1)S(1)} %get-tuple-element.44), channel_id=1, source_target_pairs={{0,16},{16,0},{1,17},{17,1},{2,18},{18,2},{3,19},{19,3},{4,20},{20... | collective-permute-start | bytes 196616 | tf_op jit(solution)/shard_map/ppermute | solution.py:329
  56.5 4.3 %collective-permute-start.12 = (bf16[32,1024]{1,0:T(8,128)(2,1)S(1)}, bf16[32,1024]{1,0:T(8,128)(2,1)S(1)}, u32[]{:S(2)}, u32[]{:S(2)}) collective-permute-start(bf16[32,1024]{1,0:T(8,128)(2,1)S(1)} %get-tuple-element.42), channel_id=1, source_target_pairs={{0,2},{2,0},{1,3},{3,1},{4,6},{6,4},{5,7},{7,5},{8,10},{10,8},{9,1... | collective-permute-start | bytes 196616 | tf_op jit(solution)/shard_map/ppermute | solution.py:329
  60.1 4.3 %collective-permute-start.14 = (bf16[32,1024]{1,0:T(8,128)(2,1)S(1)}, bf16[32,1024]{1,0:T(8,128)(2,1)S(1)}, u32[]{:S(2)}, u32[]{:S(2)}) collective-permute-start(bf16[32,1024]{1,0:T(8,128)(2,1)S(1)} %fusion.6), channel_id=1, source_target_pairs={{0,2},{2,0},{1,3},{3,1},{4,6},{6,4},{5,7},{7,5},{8,10},{10,8},{9,1... | collective-permute-start | bytes 196616 | tf_op jit(solution)/shard_map/ppermute | solution.py:329
  65.3 1.3 %collective-permute-start.15 = (f32[32,512]{1,0:T(8,128)S(1)}, f32[32,512]{1,0:T(8,128)S(1)}, u32[]{:S(2)}, u32[]{:S(2)}) collective-permute-start(f32[32,512]{1,0:T(8,128)S(1)} %slice_add_fusion), channel_id=1, source_target_pairs={{0,1},{1,0},{2,3},{3,2},{4,5},{5,4},{6,7},{7,6},{8,9},{9,8},{10,11... | collective-permute-start | bytes 196616 | tf_op jit(solution)/shard_map/ppermute | solution.py:329
  66.7 5.9 %collective-permute-start.18 = (f16[40,512]{1,0:T(8,128)(2,1)S(1)}, f16[40,512]{1,0:T(8,128)(2,1)S(1)}, u32[]{:S(2)}, u32[]{:S(2)}) collective-permute-start(f16[40,512]{1,0:T(8,128)(2,1)S(1)} %get-tuple-element.47), channel_id=1, source_target_pairs={{0,12},{4,8},{8,4},{12,0},{1,13},{5,9},{9,5},{13,1},{2,14},{6,10},... | collective-permute-start | bytes 122888 | tf_op jit(solution)/shard_map/ppermute | solution.py:329
  69.3 4.9 %collective-permute-start.17 = (f16[40,512]{1,0:T(8,128)(2,1)S(1)}, f16[40,512]{1,0:T(8,128)(2,1)S(1)}, u32[]{:S(2)}, u32[]{:S(2)}) collective-permute-start(f16[40,512]{1,0:T(8,128)(2,1)S(1)} %get-tuple-element.47), channel_id=1, source_target_pairs={{0,8},{4,12},{8,0},{12,4},{1,9},{5,13},{9,1},{13,5},{2,10},{6,14},... | collective-permute-start | bytes 122888 | tf_op jit(solution)/shard_map/ppermute | solution.py:329
  69.3 4.9 %collective-permute-start.16 = (f16[40,512]{1,0:T(8,128)(2,1)S(1)}, f16[40,512]{1,0:T(8,128)(2,1)S(1)}, u32[]{:S(2)}, u32[]{:S(2)}) collective-permute-start(f16[40,512]{1,0:T(8,128)(2,1)S(1)} %get-tuple-element.47), channel_id=1, source_target_pairs={{0,4},{4,0},{8,12},{12,8},{1,5},{5,1},{9,13},{13,9},{2,6},{6,2},{1... | collective-permute-start | bytes 122888 | tf_op jit(solution)/shard_map/ppermute | solution.py:329
where the time goes:
time: 75 us; the launch traced here: 74.9 us
  Pallas kernels  33.9 us (45%)
  starting transfers between devices  21 us (28%)
  waiting for transfers between devices  18.4 us (25%)
  matrix products  0.76 us (1%)
    ppermute x13, waiting for transfers between devices, others(): lax.ppermute(pick(index ^ k), axis, [(i, i ^ k) for i in range(size)])  14 us
    pallas_call x2, Pallas kernels, gram_split(): pl.pallas_call(functools.partial(gram_split_kernel, first=first), in_spec...  13.8 us
    ppermute x13, starting transfers between devices, others(): lax.ppermute(pick(index ^ k), axis, [(i, i ^ k) for i in range(size)])  11.6 us
    pallas_call x2, Pallas kernels, home(): pl.pallas_call(home_kernel, in_specs=[index] + [WHOLE] * (2 + len(after))...  6.23 us
    pallas_call x2, Pallas kernels, project(): pl.pallas_call(functools.partial(project_kernel, targets=targets), in_spe...  6.16 us
    pallas_call x1, Pallas kernels, gram_product(): pl.pallas_call(functools.partial(away_kernel, row_count=row_count, own=ow...  6.09 us
    ppermute x3, starting transfers between devices, body(): lax.ppermute(part.astype(jnp.float16), 'row', [(i, i ^ k) for i in range(...  5.82 us
    ppermute x3, waiting for transfers between devices, peers(): lax.ppermute(pick(k), ('groups', 'col'), [(i, i ^ k) for i in range(4)])  4.33 us
  transfers between devices with their start and end apart: 19, of which 12 were waited for; matrix products, arithmetic and copies ran while one was open for 0% of the time, Pallas kernels for 31%

commit v1 on v0

--- a/solution.py
+++ b/solution.py
@@ -129,13 +129,20 @@
                 outs[k][s, j * height : (j + 1) * height] = scratch[j, pl.ds(pl.multiple_of(start, height), height)]
 
 
-def pack_kernel(*refs):
-    kept, got_ref, out_ref = refs[:-2], refs[-2], refs[-1]
-    lanes = got_ref.shape[-1]
-    parts = jnp.concatenate([ref[0] for ref in kept] + [got_ref[...].reshape(-1, lanes)], 0)
+def pack_kernel(after_ref, *refs):
+    del after_ref
+    kept, out_ref = refs[:-1], refs[-1]
+    lanes = out_ref.shape[1]
+    parts = jnp.concatenate([ref[i] for ref in kept for i in range(4 // len(kept))], 0)
     k = exponents(parts)
     out_ref[: parts.shape[0]] = scaled(parts, k)
     out_ref[parts.shape[0] :] = jnp.broadcast_to(k, (PAD, lanes))
+
+
+def gather_kernel(after_ref, *refs):
+    del after_ref
+    for i, ref in enumerate(refs[:-1]):
+        refs[-1][i] = ref[1]
 
 
 def pack_scores_kernel(scores_ref, out_ref):
@@ -195,7 +202,7 @@
     mark_ref[...] = jnp.zeros_like(mark_ref)
 
 
-def gram_split(place, after, inverse_gram, first, count, tile=256, slots=4):
+def gram_split(place, after, inverse_gram, first, count, tile=128, slots=8):
     rows, width = inverse_gram.shape
     half, quarter = width // 2, rows // 4
     tile = min(tile, quarter)
@@ -223,19 +230,19 @@
         write(g ^ group, done[g * (queries // 2) : (g + 1) * (queries // 2)])
 
 
-def away_kernel(place_ref, after_ref, *refs, row_count, own):
-    del after_ref
-    grams, sources, (out_ref, terms, natural) = refs[:2], refs[2 : 2 + row_count], refs[2 + row_count :]
+def away_kernel(place_ref, *refs, row_count, own):
+    grams, sources, (out_ref, terms, natural) = refs[:2], refs[2:-3], refs[-3:]
     group, row, col, sub = (place_ref[i] for i in range(4))
     height, queries, lanes = natural.shape
-    for z in range(row_count):
-        count = sources[z].shape[0] - PAD
-        piece = restored(sources[z][:count], sources[z][count : count + 1])
-        for place in range(8):
-            s, g, c = place // 4, place // 2 % 2, place % 2
+    for i, ref in enumerate(sources):
+        s, z = i // row_count, i % row_count
+        count = ref.shape[0] - PAD
+        piece = restored(ref[:count], ref[count : count + 1])
+        for k in range(4):
+            g, c = k // 2, k % 2
             first = ((((g ^ group) * 2 + (c ^ col)) * 2 + (s ^ sub)) * row_count + (z ^ row)) * own
             for j in range(own):
-                start = (place * own + j) * height
+                start = (k * own + j) * height
                 natural[:, pl.ds(first + j, 1), :] = piece[start : start + height].reshape(height, 1, lanes)
     for a in range(height):
         block = natural[a]
@@ -267,9 +274,9 @@
     late_wire[...] = (late_ref[1] + late_got_ref[1]).astype(jnp.bfloat16)
 
 
-def gram_product(place, after, quarters, sources, own, lanes):
+def gram_product(place, quarters, sources, own, lanes):
     quarter, half = quarters[0].shape[0] // 2, quarters[0].shape[1]
-    row_count = len(sources)
+    row_count = len(sources) // 2
     queries = 8 * row_count * own
     index = pl.BlockSpec(memory_space=pltpu.SMEM)
 
@@ -283,7 +290,7 @@
 
     away, terms = pl.pallas_call(
         functools.partial(away_kernel, row_count=row_count, own=own),
-        in_specs=[index] + [WHOLE] * (3 + row_count),
+        in_specs=[index] + [WHOLE] * (2 + len(sources)),
         out_specs=[WHOLE, WHOLE],
         out_shape=[
             jax.ShapeDtypeStruct((2, 2, queries // 2, quarter), jnp.float32),
@@ -292,7 +299,7 @@
         scratch_shapes=[pltpu.VMEM((half // lanes, queries, lanes), jnp.float32)],
         name="away",
         **common(2),
-    )(place, after, *quarters[:2], *sources)
+    )(place, *quarters[:2], *sources)
     got = swapped(away, "sub")
 
     def home(i, *after):
@@ -366,7 +373,7 @@
     own = queries // row_count
     in_width, out_width = proj_in.shape[1], proj_out.shape[1]
     got = []
-    for targets in (range(row_count)[: row_count // 2 - 1 : -1], range(row_count)[: row_count // 2][::-1]):
+    for targets in [(k,) for k in range(row_count - 1, row_count // 2 - 1, -1)] + [range(row_count // 2)[::-1]]:
         parts = project(targets, row_count, place, query_acts, query_grads, proj_in, proj_out)
         for k, part in zip(targets, parts):
             if k:
@@ -383,13 +390,15 @@
         *[x.astype(jnp.float32) for x in got],
         scratch=[pltpu.VMEM((own, in_width, out_width), jnp.float32)],
     )
+    last, mark = gram_split(place, near[0], inverse_gram, 3, 1)
     near = [near[0]] + peers(lambda k: near[k])
-    got = swapped(jnp.stack([x[1] for x in near]), "sub")
-    packed = call(pack_kernel, (8 * height + PAD, out_width), "pack", *near, got)
-    wire = packed.astype(jnp.float16)
-    sources = [packed] + [got.astype(jnp.float32) for got in others(lambda d: wire, "row")]
-    last, mark = gram_split(place, packed, inverse_gram, 3, 1)
-    total = gram_product(place, mark, first + last, sources, own, out_width)
+    sources = []
+    away = call(gather_kernel, (4, height, out_width), "gather", mark, *near)
+    for kept in (near, [swapped(away, "sub")]):
+        packed = call(pack_kernel, (4 * height + PAD, out_width), "pack", mark, *kept)
+        wire = packed.astype(jnp.float16)
+        sources += [packed] + [got.astype(jnp.float32) for got in others(lambda d: wire, "row")]
+    total = gram_product(place, first + last, sources, own, out_width)
     high = lax.reduce_precision(total, 8, 7)
     terms = jnp.concatenate([high, total - high], 0).astype(jnp.bfloat16)
     scores = lax.dot_general(

time: 75 us -> 77.7 us (1.036)
  starting transfers between devices: 21 us -> 28.9 us
  waiting for transfers between devices: 18.4 us -> 11.8 us
  Pallas kernels: 33.9 us -> 35.2 us
    ppermute x13 -> x16, starting transfers between devices: 11.6 us -> 19.5 us  [others(): lax.ppermute(pick(index ^ k), axis, [(i, i ^ k) for i in range(size)])]
    ppermute x3, waiting for transfers between devices: 4.33 us -> 0.13 us  [peers(): lax.ppermute(pick(k), ('groups', 'col'), [(i, i ^ k) for i in range(4)])]
    ppermute x13 -> x16, waiting for transfers between devices: 14 us -> 11.6 us  [others(): lax.ppermute(pick(index ^ k), axis, [(i, i ^ k) for i in range(size)])]
    pallas_call x2 -> x3, Pallas kernels: 6.16 us -> 7.78 us  [project(): pl.pallas_call(functools.partial(project_kernel, targets=targets), in_spe...]
    pallas_call x4 -> x6, Pallas kernels: 1.63 us -> 1.65 us  [call(): pl.pallas_call(kernel, in_specs=specs, out_specs=[WHOLE] * len(shapes), o...]
  transfers between devices with their start and end apart: 19 -> 22, of which waited for: 12 -> 8; matrix products, arithmetic and copies ran while one was open for 0% -> 0% of each run, Pallas kernels for 31% -> 32%
where the time goes in v1:
time: 77.7 us; the launch traced here: 77.5 us
  Pallas kernels  35.2 us (45%)
  starting transfers between devices  28.9 us (37%)
  waiting for transfers between devices  11.8 us (15%)
    ppermute x16, starting transfers between devices, others(): lax.ppermute(pick(index ^ k), axis, [(i, i ^ k) for i in range(size)])  19.5 us
    pallas_call x2, Pallas kernels, gram_split(): pl.pallas_call(functools.partial(gram_split_kernel, first=first), in_spec...  13.4 us
    ppermute x16, waiting for transfers between devices, others(): lax.ppermute(pick(index ^ k), axis, [(i, i ^ k) for i in range(size)])  11.6 us
    pallas_call x3, Pallas kernels, project(): pl.pallas_call(functools.partial(project_kernel, targets=targets), in_spe...  7.78 us
    pallas_call x2, Pallas kernels, home(): pl.pallas_call(home_kernel, in_specs=[index] + [WHOLE] * (2 + len(after))...  6.22 us
    pallas_call x1, Pallas kernels, gram_product(): pl.pallas_call(functools.partial(away_kernel, row_count=row_count, own=ow...  6.1 us
    ppermute x3, starting transfers between devices, body(): lax.ppermute(part.astype(jnp.float16), 'row', [(i, i ^ k) for i in range(...  5.83 us
    ppermute x3, starting transfers between devices, peers(): lax.ppermute(pick(k), ('groups', 'col'), [(i, i ^ k) for i in range(4)])  3.55 us
  transfers between devices with their start and end apart: 22, of which 8 were waited for; matrix products, arithmetic and copies ran while one was open for 0% of the time, Pallas kernels for 32%

profile of v1, /device:TPU:0, one launch (start us, length us, event | category | flops | bytes accessed | tf_op | source)
XLA Modules:
  0.0 77.5 jit_solution(16939726259671058239)
XLA Ops:
  0.1 2.4 %project.5 = f32[528,128]{1,0:T(8,128)S(1)} custom-call(s32[4]{0:T(128)S(1)} %pad_add_fusion.place_ref, bf16[8,128,1024]{2,1,0:T(8,128)(2,1)} %refs_0_.5, bf16[8,128,1024]{2,1,0:T(8,128)(2,1)} %refs_1_.5, bf16[1024,128]{1,0:T(8,128)(2,1)} %refs_2_.5, bf16[1024,128]{1,0:T(8,128)(2,1)} %refs_3_.5), custom_call_target="tpu_custom_call" | custom-call | tf_op jit(solution)/shard_map/project/pallas_call | solution.py:90
  2.5 4.1 %collective-permute-start.1 = (f16[528,128]{1,0:T(8,128)(2,1)S(1)}, f16[528,128]{1,0:T(8,128)(2,1)S(1)}, u32[]{:S(2)}, u32[]{:S(2)}) collective-permute-start(f16[528,128]{1,0:T(8,128)(2,1)S(1)} %convert_element_type.72), channel_id=1, source_target_pairs={{0,8},{4,12},{8,0},{12,4},{1,9},{5,13},{9,1},{13,5},{2,10},{6,14},... | collective-permute-start | bytes 405512 | tf_op jit(solution)/shard_map/ppermute | solution.py:380
  6.6 2.3 %project.4 = f32[528,128]{1,0:T(8,128)S(1)} custom-call(s32[4]{0:T(128)S(1)} %pad_add_fusion.place_ref, bf16[8,128,1024]{2,1,0:T(8,128)(2,1)} %refs_0_.5, bf16[8,128,1024]{2,1,0:T(8,128)(2,1)} %refs_1_.5, bf16[1024,128]{1,0:T(8,128)(2,1)} %refs_2_.5, bf16[1024,128]{1,0:T(8,128)(2,1)} %refs_3_.5), custom_call_target="tpu_custom_call" | custom-call | tf_op jit(solution)/shard_map/project/pallas_call | solution.py:90
  9.0 1.4 %collective-permute-start = (f16[528,128]{1,0:T(8,128)(2,1)S(1)}, f16[528,128]{1,0:T(8,128)(2,1)S(1)}, u32[]{:S(2)}, u32[]{:S(2)}) collective-permute-start(f16[528,128]{1,0:T(8,128)(2,1)S(1)} %convert_element_type.70), channel_id=1, source_target_pairs={{0,12},{4,8},{8,4},{12,0},{1,13},{5,9},{9,5},{13,1},{2,14},{6,10},... | collective-permute-start | bytes 405512 | tf_op jit(solution)/shard_map/ppermute | solution.py:380
  10.4 3.1 %project.3 = (f32[528,128]{1,0:T(8,128)S(1)}, f32[528,128]{1,0:T(8,128)S(1)}) custom-call(s32[4]{0:T(128)S(1)} %pad_add_fusion.place_ref, bf16[8,128,1024]{2,1,0:T(8,128)(2,1)} %refs_0_.5, bf16[8,128,1024]{2,1,0:T(8,128)(2,1)} %refs_1_.5, bf16[1024,128]{1,0:T(8,128)(2,1)} %refs_2_.5, bf16[1024,128]{1,0:T(8,128)(2,1)} %refs_3_.5), custom_call_target="tpu_custom_call" | custom-call | tf_op jit(solution)/shard_map/project/pallas_call | solution.py:90
  13.8 9.2 %gram_split.2 = (bf16[2048,2048]{1,0:T(8,128)(2,1)S(1)}, bf16[2048,2048]{1,0:T(8,128)(2,1)S(1)}, bf16[2048,2048]{1,0:T(8,128)(2,1)S(1)}, f32[8,128]{1,0:T(8,128)S(1)}) custom-call(s32[4]{0:T(128)S(1)} %pad_add_fusion.place_ref, f32[528,128]{1,0:T(8,128)S(1)} %get-tuple-element.23.after_ref.own_ref, f32[4096,4096]{1,0:T(8,128)} %gram_ref.3), custom_call_target="tpu_custom_call" | custom-call | bytes 25165824 | tf_op jit(solution)/shard_map/gram_split/pallas_call | solution.py:209
  24.0 1.6 %collective-permute-start.3 = (f32[2,32,128]{2,1,0:T(8,128)S(1)}, f32[2,32,128]{2,1,0:T(8,128)S(1)}, u32[]{:S(2)}, u32[]{:S(2)}) collective-permute-start(f32[2,32,128]{2,1,0:T(8,128)S(1)} %get-tuple-element.31), channel_id=1, source_target_pairs={{0,2},{2,0},{16,18},{18,16},{1,3},{3,1},{17,19},{19,17},{4,6},{6,4... | collective-permute-start | bytes 98312 | tf_op jit(solution)/shard_map/ppermute | solution.py:350
  25.6 1.5 %collective-permute-start.4 = (f32[2,32,128]{2,1,0:T(8,128)S(1)}, f32[2,32,128]{2,1,0:T(8,128)S(1)}, u32[]{:S(2)}, u32[]{:S(2)}) collective-permute-start(f32[2,32,128]{2,1,0:T(8,128)S(1)} %get-tuple-element.32), channel_id=1, source_target_pairs={{0,16},{2,18},{16,0},{18,2},{1,17},{3,19},{17,1},{19,3},{4,20},{6,... | collective-permute-start | bytes 98312 | tf_op jit(solution)/shard_map/ppermute | solution.py:350
  27.6 4.2 %gram_split.3 = (bf16[2048,2048]{1,0:T(8,128)(2,1)S(1)}, f32[8,128]{1,0:T(8,128)S(1)}) custom-call(s32[4]{0:T(128)S(1)} %pad_add_fusion.place_ref, f32[2,32,128]{2,1,0:T(8,128)S(1)} %get-tuple-element.29.after_ref.refs_0_, f32[4096,4096]{1,0:T(8,128)} %gram_ref.3), custom_call_target="tpu_custom_call" | custom-call | bytes 8388608 | tf_op jit(solution)/shard_map/gram_split/pallas_call | solution.py:209
  32.0 3.0 %collective-permute-start.8 = (f16[136,128]{1,0:T(8,128)(2,1)S(1)}, f16[136,128]{1,0:T(8,128)(2,1)S(1)}, u32[]{:S(2)}, u32[]{:S(2)}) collective-permute-start(f16[136,128]{1,0:T(8,128)(2,1)S(1)} %convert_element_type.76), channel_id=1, source_target_pairs={{0,12},{4,8},{8,4},{12,0},{1,13},{5,9},{9,5},{13,1},{2,14},{6,10},... | collective-permute-start | bytes 104456 | tf_op jit(solution)/shard_map/ppermute | solution.py:336
  36.5 3.0 %collective-permute-start.12 = (f16[136,128]{1,0:T(8,128)(2,1)S(1)}, f16[136,128]{1,0:T(8,128)(2,1)S(1)}, u32[]{:S(2)}, u32[]{:S(2)}) collective-permute-start(f16[136,128]{1,0:T(8,128)(2,1)S(1)} %convert_element_type.80), channel_id=1, source_target_pairs={{0,12},{4,8},{8,4},{12,0},{1,13},{5,9},{9,5},{13,1},{2,14},{6,10},... | collective-permute-start | bytes 104456 | tf_op jit(solution)/shard_map/ppermute | solution.py:336
  39.5 1.5 %collective-permute-start.10 = (f16[136,128]{1,0:T(8,128)(2,1)S(1)}, f16[136,128]{1,0:T(8,128)(2,1)S(1)}, u32[]{:S(2)}, u32[]{:S(2)}) collective-permute-start(f16[136,128]{1,0:T(8,128)(2,1)S(1)} %convert_element_type.80), channel_id=1, source_target_pairs={{0,4},{4,0},{8,12},{12,8},{1,5},{5,1},{9,13},{13,9},{2,6},{6,2},{1... | collective-permute-start | bytes 104456 | tf_op jit(solution)/shard_map/ppermute | solution.py:336
  42.3 2.0 %collective-permute-done.11 = f16[136,128]{1,0:T(8,128)(2,1)S(1)} collective-permute-done((f16[136,128]{1,0:T(8,128)(2,1)S(1)}, f16[136,128]{1,0:T(8,128)(2,1)S(1)}, u32[]{:S(2)}, u32[]{:S(2)}) %collective-permute-start.11) | collective-permute-done | bytes 34848 | tf_op jit(solution)/shard_map/ppermute | solution.py:336
  44.3 6.1 %away.1 = (f32[2,2,32,1024]{3,2,1,0:T(8,128)S(1)}, bf16[2048,128]{1,0:T(8,128)(2,1)S(1)}) custom-call(s32[4]{0:T(128)S(1)} %pad_add_fusion.place_ref, bf16[2048,2048]{1,0:T(8,128)(2,1)S(1)} %get-tuple-element.25.refs_0_, bf16[2048,2048]{1,0:T(8,128)(2,1)S(1)} %get-tuple-element.26.refs_1_, f32[136,128]{1,0:T(8,128)S(1)} %pack.2.refs_2_, ...), custom_call_target="tpu_custom_call" | custom-call | flops 2147483648 | bytes 4194304 | tf_op jit(solution)/shard_map/away/pallas_call | solution.py:291
  50.5 3.1 %home.2 = f32[2,32,1024]{2,1,0:T(8,128)S(1)} custom-call(s32[4]{0:T(128)S(1)} %pad_add_fusion.place_ref, bf16[2048,2048]{1,0:T(8,128)(2,1)S(1)} %get-tuple-element.24.gram_ref, bf16[2048,128]{1,0:T(8,128)(2,1)S(1)} %get-tuple-element.34.terms_ref), custom_call_target="tpu_custom_call" | custom-call | flops 1073741824 | bytes 2097152 | tf_op jit(solution)/shard_map/home/pallas_call | solution.py:306
  53.7 1.6 %collective-permute-start.14 = (bf16[32,1024]{1,0:T(8,128)(2,1)S(1)}, bf16[32,1024]{1,0:T(8,128)(2,1)S(1)}, u32[]{:S(2)}, u32[]{:S(2)}) collective-permute-start(bf16[32,1024]{1,0:T(8,128)(2,1)S(1)} %fusion.7.refs_0_), channel_id=1, source_target_pairs={{0,16},{16,0},{1,17},{17,1},{2,18},{18,2},{3,19},{19,3},{4,20},{20... | collective-permute-start | bytes 196616 | tf_op jit(solution)/shard_map/ppermute | solution.py:336
  55.3 3.1 %home.3.late_ref = f32[2,32,1024]{2,1,0:T(8,128)S(1)} custom-call(s32[4]{0:T(128)S(1)} %pad_add_fusion.place_ref, bf16[2048,2048]{1,0:T(8,128)(2,1)S(1)} %get-tuple-element.36.gram_ref, bf16[2048,128]{1,0:T(8,128)(2,1)S(1)} %get-tuple-element.34.terms_ref, bf16[32,1024]{1,0:T(8,128)(2,1)S(1)} %fusion.7.refs_0_), custom_call_target="tpu_custom_call" | custom-call | flops 1073741824 | bytes 2097152 | tf_op jit(solution)/shard_map/home/pallas_call | solution.py:306
  59.8 1.5 %collective-permute-start.15 = (bf16[32,1024]{1,0:T(8,128)(2,1)S(1)}, bf16[32,1024]{1,0:T(8,128)(2,1)S(1)}, u32[]{:S(2)}, u32[]{:S(2)}) collective-permute-start(bf16[32,1024]{1,0:T(8,128)(2,1)S(1)} %get-tuple-element.38), channel_id=1, source_target_pairs={{0,2},{2,0},{1,3},{3,1},{4,6},{6,4},{5,7},{7,5},{8,10},{10,8},{9,1... | collective-permute-start | bytes 196616 | tf_op jit(solution)/shard_map/ppermute | solution.py:336
  61.4 1.4 %collective-permute-done.16 = bf16[32,1024]{1,0:T(8,128)(2,1)S(1)} collective-permute-done((bf16[32,1024]{1,0:T(8,128)(2,1)S(1)}, bf16[32,1024]{1,0:T(8,128)(2,1)S(1)}, u32[]{:S(2)}, u32[]{:S(2)}) %collective-permute-start.16) | collective-permute-done | bytes 65568 | tf_op jit(solution)/shard_map/ppermute | solution.py:336
  62.8 1.6 %collective-permute-start.17 = (bf16[32,1024]{1,0:T(8,128)(2,1)S(1)}, bf16[32,1024]{1,0:T(8,128)(2,1)S(1)}, u32[]{:S(2)}, u32[]{:S(2)}) collective-permute-start(bf16[32,1024]{1,0:T(8,128)(2,1)S(1)} %fusion.6), channel_id=1, source_target_pairs={{0,2},{2,0},{1,3},{3,1},{4,6},{6,4},{5,7},{7,5},{8,10},{10,8},{9,1... | collective-permute-start | bytes 196616 | tf_op jit(solution)/shard_map/ppermute | solution.py:336
  64.4 2.7 %collective-permute-done.17 = bf16[32,1024]{1,0:T(8,128)(2,1)S(1)} collective-permute-done((bf16[32,1024]{1,0:T(8,128)(2,1)S(1)}, bf16[32,1024]{1,0:T(8,128)(2,1)S(1)}, u32[]{:S(2)}, u32[]{:S(2)}) %collective-permute-start.17) | collective-permute-done | bytes 65568 | tf_op jit(solution)/shard_map/ppermute | solution.py:336
  69.4 1.8 %collective-permute-start.21 = (f16[40,512]{1,0:T(8,128)(2,1)S(1)}, f16[40,512]{1,0:T(8,128)(2,1)S(1)}, u32[]{:S(2)}, u32[]{:S(2)}) collective-permute-start(f16[40,512]{1,0:T(8,128)(2,1)S(1)} %get-tuple-element.43), channel_id=1, source_target_pairs={{0,12},{4,8},{8,4},{12,0},{1,13},{5,9},{9,5},{13,1},{2,14},{6,10},... | collective-permute-start | bytes 122888 | tf_op jit(solution)/shard_map/ppermute | solution.py:336
  71.6 2.3 %collective-permute-start.19 = (f16[40,512]{1,0:T(8,128)(2,1)S(1)}, f16[40,512]{1,0:T(8,128)(2,1)S(1)}, u32[]{:S(2)}, u32[]{:S(2)}) collective-permute-start(f16[40,512]{1,0:T(8,128)(2,1)S(1)} %get-tuple-element.43), channel_id=1, source_target_pairs={{0,4},{4,0},{8,12},{12,8},{1,5},{5,1},{9,13},{13,9},{2,6},{6,2},{1... | collective-permute-start | bytes 122888 | tf_op jit(solution)/shard_map/ppermute | solution.py:336
  73.9 1.9 %collective-permute-done.21 = f16[40,512]{1,0:T(8,128)(2,1)S(1)} collective-permute-done((f16[40,512]{1,0:T(8,128)(2,1)S(1)}, f16[40,512]{1,0:T(8,128)(2,1)S(1)}, u32[]{:S(2)}, u32[]{:S(2)}) %collective-permute-start.21) | collective-permute-done | bytes 40992 | tf_op jit(solution)/shard_map/ppermute | solution.py:336
  (67 shorter events, 10.8 us)
Async XLA Ops:
  0.0 67.2 %copy-start = (bf16[512,2048]{1,0:T(8,128)(2,1)S(1)}, bf16[512,2048]{1,0:T(8,128)(2,1)}, u32[]{:S(2)}) copy-start(bf16[512,2048]{1,0:T(8,128)(2,1)} %param.11) | copy-start | bytes 6291460
  2.5 20.5 %collective-permute-start.1 = (f16[528,128]{1,0:T(8,128)(2,1)S(1)}, f16[528,128]{1,0:T(8,128)(2,1)S(1)}, u32[]{:S(2)}, u32[]{:S(2)}) collective-permute-start(f16[528,128]{1,0:T(8,128)(2,1)S(1)} %convert_element_type.72), channel_id=1, source_target_pairs={{0,8},{4,12},{8,0},{12,4},{1,9},{5,13},{9,1},{13,5},{2,10},{6,14},... | collective-permute-start | bytes 405512 | tf_op jit(solution)/shard_map/ppermute | solution.py:380
  9.0 14.1 %collective-permute-start = (f16[528,128]{1,0:T(8,128)(2,1)S(1)}, f16[528,128]{1,0:T(8,128)(2,1)S(1)}, u32[]{:S(2)}, u32[]{:S(2)}) collective-permute-start(f16[528,128]{1,0:T(8,128)(2,1)S(1)} %convert_element_type.70), channel_id=1, source_target_pairs={{0,12},{4,8},{8,4},{12,0},{1,13},{5,9},{9,5},{13,1},{2,14},{6,10},... | collective-permute-start | bytes 405512 | tf_op jit(solution)/shard_map/ppermute | solution.py:380
  13.5 9.6 %collective-permute-start.2 = (f16[528,128]{1,0:T(8,128)(2,1)S(1)}, f16[528,128]{1,0:T(8,128)(2,1)S(1)}, u32[]{:S(2)}, u32[]{:S(2)}) collective-permute-start(f16[528,128]{1,0:T(8,128)(2,1)S(1)} %convert_element_type.74), channel_id=1, source_target_pairs={{0,4},{4,0},{8,12},{12,8},{1,5},{5,1},{9,13},{13,9},{2,6},{6,2},{1... | collective-permute-start | bytes 405512 | tf_op jit(solution)/shard_map/ppermute | solution.py:380
  24.0 7.8 %collective-permute-start.3 = (f32[2,32,128]{2,1,0:T(8,128)S(1)}, f32[2,32,128]{2,1,0:T(8,128)S(1)}, u32[]{:S(2)}, u32[]{:S(2)}) collective-permute-start(f32[2,32,128]{2,1,0:T(8,128)S(1)} %get-tuple-element.31), channel_id=1, source_target_pairs={{0,2},{2,0},{16,18},{18,16},{1,3},{3,1},{17,19},{19,17},{4,6},{6,4... | collective-permute-start | bytes 98312 | tf_op jit(solution)/shard_map/ppermute | solution.py:350
  25.6 6.2 %collective-permute-start.4 = (f32[2,32,128]{2,1,0:T(8,128)S(1)}, f32[2,32,128]{2,1,0:T(8,128)S(1)}, u32[]{:S(2)}, u32[]{:S(2)}) collective-permute-start(f32[2,32,128]{2,1,0:T(8,128)S(1)} %get-tuple-element.32), channel_id=1, source_target_pairs={{0,16},{2,18},{16,0},{18,2},{1,17},{3,19},{17,1},{19,3},{4,20},{6,... | collective-permute-start | bytes 98312 | tf_op jit(solution)/shard_map/ppermute | solution.py:350
  27.1 4.8 %collective-permute-start.5 = (f32[2,32,128]{2,1,0:T(8,128)S(1)}, f32[2,32,128]{2,1,0:T(8,128)S(1)}, u32[]{:S(2)}, u32[]{:S(2)}) collective-permute-start(f32[2,32,128]{2,1,0:T(8,128)S(1)} %get-tuple-element.33), channel_id=1, source_target_pairs={{0,18},{2,16},{16,2},{18,0},{1,19},{3,17},{17,3},{19,1},{4,22},{6,... | collective-permute-start | bytes 98312 | tf_op jit(solution)/shard_map/ppermute | solution.py:350
  31.9 4.5 %collective-permute-start.9 = (f32[4,32,128]{2,1,0:T(8,128)S(1)}, f32[4,32,128]{2,1,0:T(8,128)S(1)}, u32[]{:S(2)}, u32[]{:S(2)}) collective-permute-start(f32[4,32,128]{2,1,0:T(8,128)S(1)} %gather.1), channel_id=1, source_target_pairs={{0,1},{1,0},{2,3},{3,2},{4,5},{5,4},{6,7},{7,6},{8,9},{9,8},{10,11... | collective-permute-start | bytes 196616 | tf_op jit(solution)/shard_map/ppermute | solution.py:336
  32.0 7.5 %collective-permute-start.8 = (f16[136,128]{1,0:T(8,128)(2,1)S(1)}, f16[136,128]{1,0:T(8,128)(2,1)S(1)}, u32[]{:S(2)}, u32[]{:S(2)}) collective-permute-start(f16[136,128]{1,0:T(8,128)(2,1)S(1)} %convert_element_type.76), channel_id=1, source_target_pairs={{0,12},{4,8},{8,4},{12,0},{1,13},{5,9},{9,5},{13,1},{2,14},{6,10},... | collective-permute-start | bytes 104456 | tf_op jit(solution)/shard_map/ppermute | solution.py:336
  34.9 6.0 %collective-permute-start.7 = (f16[136,128]{1,0:T(8,128)(2,1)S(1)}, f16[136,128]{1,0:T(8,128)(2,1)S(1)}, u32[]{:S(2)}, u32[]{:S(2)}) collective-permute-start(f16[136,128]{1,0:T(8,128)(2,1)S(1)} %convert_element_type.76), channel_id=1, source_target_pairs={{0,8},{4,12},{8,0},{12,4},{1,9},{5,13},{9,1},{13,5},{2,10},{6,14},... | collective-permute-start | bytes 104456 | tf_op jit(solution)/shard_map/ppermute | solution.py:336
  35.3 5.7 %collective-permute-start.6 = (f16[136,128]{1,0:T(8,128)(2,1)S(1)}, f16[136,128]{1,0:T(8,128)(2,1)S(1)}, u32[]{:S(2)}, u32[]{:S(2)}) collective-permute-start(f16[136,128]{1,0:T(8,128)(2,1)S(1)} %convert_element_type.76), channel_id=1, source_target_pairs={{0,4},{4,0},{8,12},{12,8},{1,5},{5,1},{9,13},{13,9},{2,6},{6,2},{1... | collective-permute-start | bytes 104456 | tf_op jit(solution)/shard_map/ppermute | solution.py:336
  36.5 5.8 %collective-permute-start.12 = (f16[136,128]{1,0:T(8,128)(2,1)S(1)}, f16[136,128]{1,0:T(8,128)(2,1)S(1)}, u32[]{:S(2)}, u32[]{:S(2)}) collective-permute-start(f16[136,128]{1,0:T(8,128)(2,1)S(1)} %convert_element_type.80), channel_id=1, source_target_pairs={{0,12},{4,8},{8,4},{12,0},{1,13},{5,9},{9,5},{13,1},{2,14},{6,10},... | collective-permute-start | bytes 104456 | tf_op jit(solution)/shard_map/ppermute | solution.py:336
  39.4 4.8 %collective-permute-start.11 = (f16[136,128]{1,0:T(8,128)(2,1)S(1)}, f16[136,128]{1,0:T(8,128)(2,1)S(1)}, u32[]{:S(2)}, u32[]{:S(2)}) collective-permute-start(f16[136,128]{1,0:T(8,128)(2,1)S(1)} %convert_element_type.80), channel_id=1, source_target_pairs={{0,8},{4,12},{8,0},{12,4},{1,9},{5,13},{9,1},{13,5},{2,10},{6,14},... | collective-permute-start | bytes 104456 | tf_op jit(solution)/shard_map/ppermute | solution.py:336
  39.5 4.8 %collective-permute-start.10 = (f16[136,128]{1,0:T(8,128)(2,1)S(1)}, f16[136,128]{1,0:T(8,128)(2,1)S(1)}, u32[]{:S(2)}, u32[]{:S(2)}) collective-permute-start(f16[136,128]{1,0:T(8,128)(2,1)S(1)} %convert_element_type.80), channel_id=1, source_target_pairs={{0,4},{4,0},{8,12},{12,8},{1,5},{5,1},{9,13},{13,9},{2,6},{6,2},{1... | collective-permute-start | bytes 104456 | tf_op jit(solution)/shard_map/ppermute | solution.py:336
  50.4 3.2 %collective-permute-start.13 = (f32[2,2,32,1024]{3,2,1,0:T(8,128)S(1)}, f32[2,2,32,1024]{3,2,1,0:T(8,128)S(1)}, u32[]{:S(2)}, u32[]{:S(2)}) collective-permute-start(f32[2,2,32,1024]{3,2,1,0:T(8,128)S(1)} %get-tuple-element.35), channel_id=1, source_target_pairs={{0,1},{1,0},{2,3},{3,2},{4,5},{5,4},{6,7},{7,6},{8,9},{9,8},{10,11... | collective-permute-start | bytes 1572872 | tf_op jit(solution)/shard_map/ppermute | solution.py:336
  53.7 4.7 %collective-permute-start.14 = (bf16[32,1024]{1,0:T(8,128)(2,1)S(1)}, bf16[32,1024]{1,0:T(8,128)(2,1)S(1)}, u32[]{:S(2)}, u32[]{:S(2)}) collective-permute-start(bf16[32,1024]{1,0:T(8,128)(2,1)S(1)} %fusion.7.refs_0_), channel_id=1, source_target_pairs={{0,16},{16,0},{1,17},{17,1},{2,18},{18,2},{3,19},{19,3},{4,20},{20... | collective-permute-start | bytes 196616 | tf_op jit(solution)/shard_map/ppermute | solution.py:336
  58.5 4.3 %collective-permute-start.16 = (bf16[32,1024]{1,0:T(8,128)(2,1)S(1)}, bf16[32,1024]{1,0:T(8,128)(2,1)S(1)}, u32[]{:S(2)}, u32[]{:S(2)}) collective-permute-start(bf16[32,1024]{1,0:T(8,128)(2,1)S(1)} %get-tuple-element.40), channel_id=1, source_target_pairs={{0,16},{16,0},{1,17},{17,1},{2,18},{18,2},{3,19},{19,3},{4,20},{20... | collective-permute-start | bytes 196616 | tf_op jit(solution)/shard_map/ppermute | solution.py:336
  59.8 4.5 %collective-permute-start.15 = (bf16[32,1024]{1,0:T(8,128)(2,1)S(1)}, bf16[32,1024]{1,0:T(8,128)(2,1)S(1)}, u32[]{:S(2)}, u32[]{:S(2)}) collective-permute-start(bf16[32,1024]{1,0:T(8,128)(2,1)S(1)} %get-tuple-element.38), channel_id=1, source_target_pairs={{0,2},{2,0},{1,3},{3,1},{4,6},{6,4},{5,7},{7,5},{8,10},{10,8},{9,1... | collective-permute-start | bytes 196616 | tf_op jit(solution)/shard_map/ppermute | solution.py:336
  62.8 4.3 %collective-permute-start.17 = (bf16[32,1024]{1,0:T(8,128)(2,1)S(1)}, bf16[32,1024]{1,0:T(8,128)(2,1)S(1)}, u32[]{:S(2)}, u32[]{:S(2)}) collective-permute-start(bf16[32,1024]{1,0:T(8,128)(2,1)S(1)} %fusion.6), channel_id=1, source_target_pairs={{0,2},{2,0},{1,3},{3,1},{4,6},{6,4},{5,7},{7,5},{8,10},{10,8},{9,1... | collective-permute-start | bytes 196616 | tf_op jit(solution)/shard_map/ppermute | solution.py:336
  68.0 1.3 %collective-permute-start.18 = (f32[32,512]{1,0:T(8,128)S(1)}, f32[32,512]{1,0:T(8,128)S(1)}, u32[]{:S(2)}, u32[]{:S(2)}) collective-permute-start(f32[32,512]{1,0:T(8,128)S(1)} %slice_add_fusion), channel_id=1, source_target_pairs={{0,1},{1,0},{2,3},{3,2},{4,5},{5,4},{6,7},{7,6},{8,9},{9,8},{10,11... | collective-permute-start | bytes 196616 | tf_op jit(solution)/shard_map/ppermute | solution.py:336
  69.4 6.4 %collective-permute-start.21 = (f16[40,512]{1,0:T(8,128)(2,1)S(1)}, f16[40,512]{1,0:T(8,128)(2,1)S(1)}, u32[]{:S(2)}, u32[]{:S(2)}) collective-permute-start(f16[40,512]{1,0:T(8,128)(2,1)S(1)} %get-tuple-element.43), channel_id=1, source_target_pairs={{0,12},{4,8},{8,4},{12,0},{1,13},{5,9},{9,5},{13,1},{2,14},{6,10},... | collective-permute-start | bytes 122888 | tf_op jit(solution)/shard_map/ppermute | solution.py:336
  71.2 5.6 %collective-permute-start.20 = (f16[40,512]{1,0:T(8,128)(2,1)S(1)}, f16[40,512]{1,0:T(8,128)(2,1)S(1)}, u32[]{:S(2)}, u32[]{:S(2)}) collective-permute-start(f16[40,512]{1,0:T(8,128)(2,1)S(1)} %get-tuple-element.43), channel_id=1, source_target_pairs={{0,8},{4,12},{8,0},{12,4},{1,9},{5,13},{9,1},{13,5},{2,10},{6,14},... | collective-permute-start | bytes 122888 | tf_op jit(solution)/shard_map/ppermute | solution.py:336
  71.6 5.3 %collective-permute-start.19 = (f16[40,512]{1,0:T(8,128)(2,1)S(1)}, f16[40,512]{1,0:T(8,128)(2,1)S(1)}, u32[]{:S(2)}, u32[]{:S(2)}) collective-permute-start(f16[40,512]{1,0:T(8,128)(2,1)S(1)} %get-tuple-element.43), channel_id=1, source_target_pairs={{0,4},{4,0},{8,12},{12,8},{1,5},{5,1},{9,13},{13,9},{2,6},{6,2},{1... | collective-permute-start | bytes 122888 | tf_op jit(solution)/shard_map/ppermute | solution.py:336

commit v2 on v0

--- a/solution.py
+++ b/solution.py
@@ -138,6 +138,12 @@
     out_ref[parts.shape[0] :] = jnp.broadcast_to(k, (PAD, lanes))
 
 
+def gather_kernel(after_ref, *refs):
+    del after_ref
+    for i, ref in enumerate(refs[:-1]):
+        refs[-1][i] = ref[1]
+
+
 def pack_scores_kernel(scores_ref, out_ref):
     scores = scores_ref[...]
     k = exponents(scores)
@@ -195,7 +201,7 @@
     mark_ref[...] = jnp.zeros_like(mark_ref)
 
 
-def gram_split(place, after, inverse_gram, first, count, tile=256, slots=4):
+def gram_split(place, after, inverse_gram, first, count, tile=128, slots=8):
     rows, width = inverse_gram.shape
     half, quarter = width // 2, rows // 4
     tile = min(tile, quarter)
@@ -371,7 +377,7 @@
         for k, part in zip(targets, parts):
             if k:
                 got.append(lax.ppermute(part.astype(jnp.float16), "row", [(i, i ^ k) for i in range(row_count)]))
-    first, mark = gram_split(place, parts[-1], inverse_gram, 0, 3)
+    quarters, mark = gram_split(place, parts[-1], inverse_gram, 0, 2)
     height = own * in_width // 8
     near = call(
         functools.partial(kron_kernel, tokens=tokens),
@@ -383,13 +389,14 @@
         *[x.astype(jnp.float32) for x in got],
         scratch=[pltpu.VMEM((own, in_width, out_width), jnp.float32)],
     )
+    third, mark = gram_split(place, near[0], inverse_gram, 2, 1)
     near = [near[0]] + peers(lambda k: near[k])
-    got = swapped(jnp.stack([x[1] for x in near]), "sub")
+    got = swapped(call(gather_kernel, (4, height, out_width), "gather", mark, *near), "sub")
     packed = call(pack_kernel, (8 * height + PAD, out_width), "pack", *near, got)
     wire = packed.astype(jnp.float16)
     sources = [packed] + [got.astype(jnp.float32) for got in others(lambda d: wire, "row")]
-    last, mark = gram_split(place, packed, inverse_gram, 3, 1)
-    total = gram_product(place, mark, first + last, sources, own, out_width)
+    fourth, mark = gram_split(place, packed, inverse_gram, 3, 1)
+    total = gram_product(place, mark, quarters + third + fourth, sources, own, out_width)
     high = lax.reduce_precision(total, 8, 7)
     terms = jnp.concatenate([high, total - high], 0).astype(jnp.bfloat16)
     scores = lax.dot_general(

time: 75 us -> 73 us (0.973)
  waiting for transfers between devices: 18.4 us -> 11.5 us
  starting transfers between devices: 21 us -> 24.4 us
  Pallas kernels: 33.9 us -> 35.3 us
    ppermute x3, waiting for transfers between devices: 4.33 us -> 0.18 us  [peers(): lax.ppermute(pick(k), ('groups', 'col'), [(i, i ^ k) for i in range(4)])]
    ppermute x13, starting transfers between devices: 11.6 us -> 15 us  [others(): lax.ppermute(pick(index ^ k), axis, [(i, i ^ k) for i in range(size)])]
    ppermute x13, waiting for transfers between devices: 14 us -> 10.8 us  [others(): lax.ppermute(pick(index ^ k), axis, [(i, i ^ k) for i in range(size)])]
    pallas_call x2 -> x3, Pallas kernels: 13.8 us -> 15.2 us  [gram_split(): pl.pallas_call(functools.partial(gram_split_kernel, first=first), in_spec...]
    pallas_call x4 -> x5, Pallas kernels: 1.63 us -> 1.63 us  [call(): pl.pallas_call(kernel, in_specs=specs, out_specs=[WHOLE] * len(shapes), o...]
  transfers between devices with their start and end apart: 19 -> 19, of which waited for: 12 -> 9; matrix products, arithmetic and copies ran while one was open for 0% -> 0% of each run, Pallas kernels for 31% -> 34%
where the time goes in v2:
time: 73 us; the launch traced here: 72.9 us
  Pallas kernels  35.3 us (48%)
  starting transfers between devices  24.4 us (33%)
  waiting for transfers between devices  11.5 us (16%)
  matrix products  0.76 us (1%)
    pallas_call x3, Pallas kernels, gram_split(): pl.pallas_call(functools.partial(gram_split_kernel, first=first), in_spec...  15.2 us
    ppermute x13, starting transfers between devices, others(): lax.ppermute(pick(index ^ k), axis, [(i, i ^ k) for i in range(size)])  15 us
    ppermute x13, waiting for transfers between devices, others(): lax.ppermute(pick(index ^ k), axis, [(i, i ^ k) for i in range(size)])  10.8 us
    pallas_call x2, Pallas kernels, home(): pl.pallas_call(home_kernel, in_specs=[index] + [WHOLE] * (2 + len(after))...  6.23 us
    pallas_call x2, Pallas kernels, project(): pl.pallas_call(functools.partial(project_kernel, targets=targets), in_spe...  6.16 us
    pallas_call x1, Pallas kernels, gram_product(): pl.pallas_call(functools.partial(away_kernel, row_count=row_count, own=ow...  6.09 us
    ppermute x3, starting transfers between devices, body(): lax.ppermute(part.astype(jnp.float16), 'row', [(i, i ^ k) for i in range(...  5.82 us
    ppermute x3, starting transfers between devices, peers(): lax.ppermute(pick(k), ('groups', 'col'), [(i, i ^ k) for i in range(4)])  3.55 us
  transfers between devices with their start and end apart: 19, of which 9 were waited for; matrix products, arithmetic and copies ran while one was open for 0% of the time, Pallas kernels for 34%

profile of v2, /device:TPU:0, one launch (start us, length us, event | category | flops | bytes accessed | tf_op | source)
XLA Modules:
  0.0 72.9 jit_solution(10493762421604317989)
XLA Ops:
  0.1 3.1 %project.3 = (f32[528,128]{1,0:T(8,128)S(1)}, f32[528,128]{1,0:T(8,128)S(1)}) custom-call(s32[4]{0:T(128)S(1)} %pad_add_fusion.place_ref, bf16[8,128,1024]{2,1,0:T(8,128)(2,1)} %refs_0_.3, bf16[8,128,1024]{2,1,0:T(8,128)(2,1)} %refs_1_.3, bf16[1024,128]{1,0:T(8,128)(2,1)} %refs_2_.3, bf16[1024,128]{1,0:T(8,128)(2,1)} %refs_3_.3), custom_call_target="tpu_custom_call" | custom-call | tf_op jit(solution)/shard_map/project/pallas_call | solution.py:90
  3.2 4.1 %collective-permute-start.1 = (f16[528,128]{1,0:T(8,128)(2,1)S(1)}, f16[528,128]{1,0:T(8,128)(2,1)S(1)}, u32[]{:S(2)}, u32[]{:S(2)}) collective-permute-start(f16[528,128]{1,0:T(8,128)(2,1)S(1)} %convert_element_type.60), channel_id=1, source_target_pairs={{0,8},{4,12},{8,0},{12,4},{1,9},{5,13},{9,1},{13,5},{2,10},{6,14},... | collective-permute-start | bytes 405512 | tf_op jit(solution)/shard_map/ppermute | solution.py:379
  7.3 1.4 %collective-permute-start = (f16[528,128]{1,0:T(8,128)(2,1)S(1)}, f16[528,128]{1,0:T(8,128)(2,1)S(1)}, u32[]{:S(2)}, u32[]{:S(2)}) collective-permute-start(f16[528,128]{1,0:T(8,128)(2,1)S(1)} %convert_element_type.58), channel_id=1, source_target_pairs={{0,12},{4,8},{8,4},{12,0},{1,13},{5,9},{9,5},{13,1},{2,14},{6,10},... | collective-permute-start | bytes 405512 | tf_op jit(solution)/shard_map/ppermute | solution.py:379
  8.8 3.1 %project.2 = (f32[528,128]{1,0:T(8,128)S(1)}, f32[528,128]{1,0:T(8,128)S(1)}) custom-call(s32[4]{0:T(128)S(1)} %pad_add_fusion.place_ref, bf16[8,128,1024]{2,1,0:T(8,128)(2,1)} %refs_0_.3, bf16[8,128,1024]{2,1,0:T(8,128)(2,1)} %refs_1_.3, bf16[1024,128]{1,0:T(8,128)(2,1)} %refs_2_.3, bf16[1024,128]{1,0:T(8,128)(2,1)} %refs_3_.3), custom_call_target="tpu_custom_call" | custom-call | tf_op jit(solution)/shard_map/project/pallas_call | solution.py:90
  12.2 6.8 %gram_split.3 = (bf16[2048,2048]{1,0:T(8,128)(2,1)S(1)}, bf16[2048,2048]{1,0:T(8,128)(2,1)S(1)}, f32[8,128]{1,0:T(8,128)S(1)}) custom-call(s32[4]{0:T(128)S(1)} %pad_add_fusion.place_ref, f32[528,128]{1,0:T(8,128)S(1)} %get-tuple-element.26.after_ref.own_ref, f32[4096,4096]{1,0:T(8,128)} %gram_ref.5), custom_call_target="tpu_custom_call" | custom-call | bytes 16777216 | tf_op jit(solution)/shard_map/gram_split/pallas_call | solution.py:208
  20.5 1.6 %collective-permute-start.3 = (f32[2,32,128]{2,1,0:T(8,128)S(1)}, f32[2,32,128]{2,1,0:T(8,128)S(1)}, u32[]{:S(2)}, u32[]{:S(2)}) collective-permute-start(f32[2,32,128]{2,1,0:T(8,128)S(1)} %get-tuple-element.33), channel_id=1, source_target_pairs={{0,2},{2,0},{16,18},{18,16},{1,3},{3,1},{17,19},{19,17},{4,6},{6,4... | collective-permute-start | bytes 98312 | tf_op jit(solution)/shard_map/ppermute | solution.py:349
  22.1 1.5 %collective-permute-start.4 = (f32[2,32,128]{2,1,0:T(8,128)S(1)}, f32[2,32,128]{2,1,0:T(8,128)S(1)}, u32[]{:S(2)}, u32[]{:S(2)}) collective-permute-start(f32[2,32,128]{2,1,0:T(8,128)S(1)} %get-tuple-element.34), channel_id=1, source_target_pairs={{0,16},{2,18},{16,0},{18,2},{1,17},{3,19},{17,1},{19,3},{4,20},{6,... | collective-permute-start | bytes 98312 | tf_op jit(solution)/shard_map/ppermute | solution.py:349
  24.1 4.2 %gram_split.4 = (bf16[2048,2048]{1,0:T(8,128)(2,1)S(1)}, f32[8,128]{1,0:T(8,128)S(1)}) custom-call(s32[4]{0:T(128)S(1)} %pad_add_fusion.place_ref, f32[2,32,128]{2,1,0:T(8,128)S(1)} %get-tuple-element.31.after_ref.refs_0_, f32[4096,4096]{1,0:T(8,128)} %gram_ref.5), custom_call_target="tpu_custom_call" | custom-call | bytes 8388608 | tf_op jit(solution)/shard_map/gram_split/pallas_call | solution.py:208
  28.5 1.2 %collective-permute-done.6.refs_4_ = f32[4,32,128]{2,1,0:T(8,128)S(1)} collective-permute-done((f32[4,32,128]{2,1,0:T(8,128)S(1)}, f32[4,32,128]{2,1,0:T(8,128)S(1)}, u32[]{:S(2)}, u32[]{:S(2)}) %collective-permute-start.6) | collective-permute-done | bytes 65568 | tf_op jit(solution)/shard_map/ppermute | solution.py:335
  29.8 3.6 %collective-permute-start.9 = (f16[264,128]{1,0:T(8,128)(2,1)S(1)}, f16[264,128]{1,0:T(8,128)(2,1)S(1)}, u32[]{:S(2)}, u32[]{:S(2)}) collective-permute-start(f16[264,128]{1,0:T(8,128)(2,1)S(1)} %convert_element_type.64), channel_id=1, source_target_pairs={{0,12},{4,8},{8,4},{12,0},{1,13},{5,9},{9,5},{13,1},{2,14},{6,10},... | collective-permute-start | bytes 202760 | tf_op jit(solution)/shard_map/ppermute | solution.py:335
  34.2 4.2 %gram_split.5 = (bf16[2048,2048]{1,0:T(8,128)(2,1)S(1)}, f32[8,128]{1,0:T(8,128)S(1)}) custom-call(s32[4]{0:T(128)S(1)} %pad_add_fusion.place_ref, f32[264,128]{1,0:T(8,128)S(1)} %pack.1.after_ref.refs_2_, f32[4096,4096]{1,0:T(8,128)} %gram_ref.5), custom_call_target="tpu_custom_call" | custom-call | bytes 8388608 | tf_op jit(solution)/shard_map/gram_split/pallas_call | solution.py:208
  39.4 6.1 %away.1 = (f32[2,2,32,1024]{3,2,1,0:T(8,128)S(1)}, bf16[2048,128]{1,0:T(8,128)(2,1)S(1)}) custom-call(s32[4]{0:T(128)S(1)} %pad_add_fusion.place_ref, f32[8,128]{1,0:T(8,128)S(1)} %get-tuple-element.37.after_ref, bf16[2048,2048]{1,0:T(8,128)(2,1)S(1)} %get-tuple-element.38.refs_0_, bf16[2048,2048]{1,0:T(8,128)(2,1)S(1)} %get-tuple-element.39.refs_1_, ...), custom_call_target="tpu_custom_call" | custom-call | flops 2147483648 | bytes 4194304 | tf_op jit(solution)/shard_map/away/pallas_call | solution.py:290
  45.5 3.1 %home.2 = f32[2,32,1024]{2,1,0:T(8,128)S(1)} custom-call(s32[4]{0:T(128)S(1)} %pad_add_fusion.place_ref, bf16[2048,2048]{1,0:T(8,128)(2,1)S(1)} %get-tuple-element.32.gram_ref, bf16[2048,128]{1,0:T(8,128)(2,1)S(1)} %get-tuple-element.40.terms_ref), custom_call_target="tpu_custom_call" | custom-call | flops 1073741824 | bytes 2097152 | tf_op jit(solution)/shard_map/home/pallas_call | solution.py:305
  48.8 1.6 %collective-permute-start.11 = (bf16[32,1024]{1,0:T(8,128)(2,1)S(1)}, bf16[32,1024]{1,0:T(8,128)(2,1)S(1)}, u32[]{:S(2)}, u32[]{:S(2)}) collective-permute-start(bf16[32,1024]{1,0:T(8,128)(2,1)S(1)} %fusion.7.refs_0_), channel_id=1, source_target_pairs={{0,16},{16,0},{1,17},{17,1},{2,18},{18,2},{3,19},{19,3},{4,20},{20... | collective-permute-start | bytes 196616 | tf_op jit(solution)/shard_map/ppermute | solution.py:335
  50.3 3.1 %home.3.late_ref = f32[2,32,1024]{2,1,0:T(8,128)S(1)} custom-call(s32[4]{0:T(128)S(1)} %pad_add_fusion.place_ref, bf16[2048,2048]{1,0:T(8,128)(2,1)S(1)} %get-tuple-element.42.gram_ref, bf16[2048,128]{1,0:T(8,128)(2,1)S(1)} %get-tuple-element.40.terms_ref, bf16[32,1024]{1,0:T(8,128)(2,1)S(1)} %fusion.7.refs_0_), custom_call_target="tpu_custom_call" | custom-call | flops 1073741824 | bytes 2097152 | tf_op jit(solution)/shard_map/home/pallas_call | solution.py:305
  53.5 1.4 %collective-permute-start.13 = (bf16[32,1024]{1,0:T(8,128)(2,1)S(1)}, bf16[32,1024]{1,0:T(8,128)(2,1)S(1)}, u32[]{:S(2)}, u32[]{:S(2)}) collective-permute-start(bf16[32,1024]{1,0:T(8,128)(2,1)S(1)} %get-tuple-element.46), channel_id=1, source_target_pairs={{0,16},{16,0},{1,17},{17,1},{2,18},{18,2},{3,19},{19,3},{4,20},{20... | collective-permute-start | bytes 196616 | tf_op jit(solution)/shard_map/ppermute | solution.py:335
  54.9 1.5 %collective-permute-start.12 = (bf16[32,1024]{1,0:T(8,128)(2,1)S(1)}, bf16[32,1024]{1,0:T(8,128)(2,1)S(1)}, u32[]{:S(2)}, u32[]{:S(2)}) collective-permute-start(bf16[32,1024]{1,0:T(8,128)(2,1)S(1)} %get-tuple-element.44), channel_id=1, source_target_pairs={{0,2},{2,0},{1,3},{3,1},{4,6},{6,4},{5,7},{7,5},{8,10},{10,8},{9,1... | collective-permute-start | bytes 196616 | tf_op jit(solution)/shard_map/ppermute | solution.py:335
  56.4 1.4 %collective-permute-done.13 = bf16[32,1024]{1,0:T(8,128)(2,1)S(1)} collective-permute-done((bf16[32,1024]{1,0:T(8,128)(2,1)S(1)}, bf16[32,1024]{1,0:T(8,128)(2,1)S(1)}, u32[]{:S(2)}, u32[]{:S(2)}) %collective-permute-start.13) | collective-permute-done | bytes 65568 | tf_op jit(solution)/shard_map/ppermute | solution.py:335
  57.9 1.6 %collective-permute-start.14 = (bf16[32,1024]{1,0:T(8,128)(2,1)S(1)}, bf16[32,1024]{1,0:T(8,128)(2,1)S(1)}, u32[]{:S(2)}, u32[]{:S(2)}) collective-permute-start(bf16[32,1024]{1,0:T(8,128)(2,1)S(1)} %fusion.6), channel_id=1, source_target_pairs={{0,2},{2,0},{1,3},{3,1},{4,6},{6,4},{5,7},{7,5},{8,10},{10,8},{9,1... | collective-permute-start | bytes 196616 | tf_op jit(solution)/shard_map/ppermute | solution.py:335
  59.5 2.8 %collective-permute-done.14 = bf16[32,1024]{1,0:T(8,128)(2,1)S(1)} collective-permute-done((bf16[32,1024]{1,0:T(8,128)(2,1)S(1)}, bf16[32,1024]{1,0:T(8,128)(2,1)S(1)}, u32[]{:S(2)}, u32[]{:S(2)}) %collective-permute-start.14) | collective-permute-done | bytes 65568 | tf_op jit(solution)/shard_map/ppermute | solution.py:335
  64.5 2.8 %collective-permute-start.18 = (f16[40,512]{1,0:T(8,128)(2,1)S(1)}, f16[40,512]{1,0:T(8,128)(2,1)S(1)}, u32[]{:S(2)}, u32[]{:S(2)}) collective-permute-start(f16[40,512]{1,0:T(8,128)(2,1)S(1)} %get-tuple-element.49), channel_id=1, source_target_pairs={{0,12},{4,8},{8,4},{12,0},{1,13},{5,9},{9,5},{13,1},{2,14},{6,10},... | collective-permute-start | bytes 122888 | tf_op jit(solution)/shard_map/ppermute | solution.py:335
  67.3 1.7 %collective-permute-start.16 = (f16[40,512]{1,0:T(8,128)(2,1)S(1)}, f16[40,512]{1,0:T(8,128)(2,1)S(1)}, u32[]{:S(2)}, u32[]{:S(2)}) collective-permute-start(f16[40,512]{1,0:T(8,128)(2,1)S(1)} %get-tuple-element.49), channel_id=1, source_target_pairs={{0,4},{4,0},{8,12},{12,8},{1,5},{5,1},{9,13},{13,9},{2,6},{6,2},{1... | collective-permute-start | bytes 122888 | tf_op jit(solution)/shard_map/ppermute | solution.py:335
  68.9 1.5 %collective-permute-done.18 = f16[40,512]{1,0:T(8,128)(2,1)S(1)} collective-permute-done((f16[40,512]{1,0:T(8,128)(2,1)S(1)}, f16[40,512]{1,0:T(8,128)(2,1)S(1)}, u32[]{:S(2)}, u32[]{:S(2)}) %collective-permute-start.18) | collective-permute-done | bytes 40992 | tf_op jit(solution)/shard_map/ppermute | solution.py:335
  70.5 1.7 %collective-permute-done.17 = f16[40,512]{1,0:T(8,128)(2,1)S(1)} collective-permute-done((f16[40,512]{1,0:T(8,128)(2,1)S(1)}, f16[40,512]{1,0:T(8,128)(2,1)S(1)}, u32[]{:S(2)}, u32[]{:S(2)}) %collective-permute-start.17) | collective-permute-done | bytes 40992 | tf_op jit(solution)/shard_map/ppermute | solution.py:335
  (56 shorter events, 7.6 us)
Async XLA Ops:
  0.0 62.3 %copy-start = (bf16[512,2048]{1,0:T(8,128)(2,1)S(1)}, bf16[512,2048]{1,0:T(8,128)(2,1)}, u32[]{:S(2)}) copy-start(bf16[512,2048]{1,0:T(8,128)(2,1)} %param.11) | copy-start | bytes 6291460
  3.2 15.7 %collective-permute-start.1 = (f16[528,128]{1,0:T(8,128)(2,1)S(1)}, f16[528,128]{1,0:T(8,128)(2,1)S(1)}, u32[]{:S(2)}, u32[]{:S(2)}) collective-permute-start(f16[528,128]{1,0:T(8,128)(2,1)S(1)} %convert_element_type.60), channel_id=1, source_target_pairs={{0,8},{4,12},{8,0},{12,4},{1,9},{5,13},{9,1},{13,5},{2,10},{6,14},... | collective-permute-start | bytes 405512 | tf_op jit(solution)/shard_map/ppermute | solution.py:379
  7.3 11.7 %collective-permute-start = (f16[528,128]{1,0:T(8,128)(2,1)S(1)}, f16[528,128]{1,0:T(8,128)(2,1)S(1)}, u32[]{:S(2)}, u32[]{:S(2)}) collective-permute-start(f16[528,128]{1,0:T(8,128)(2,1)S(1)} %convert_element_type.58), channel_id=1, source_target_pairs={{0,12},{4,8},{8,4},{12,0},{1,13},{5,9},{9,5},{13,1},{2,14},{6,10},... | collective-permute-start | bytes 405512 | tf_op jit(solution)/shard_map/ppermute | solution.py:379
  11.9 7.7 %collective-permute-start.2 = (f16[528,128]{1,0:T(8,128)(2,1)S(1)}, f16[528,128]{1,0:T(8,128)(2,1)S(1)}, u32[]{:S(2)}, u32[]{:S(2)}) collective-permute-start(f16[528,128]{1,0:T(8,128)(2,1)S(1)} %convert_element_type.62), channel_id=1, source_target_pairs={{0,4},{4,0},{8,12},{12,8},{1,5},{5,1},{9,13},{13,9},{2,6},{6,2},{1... | collective-permute-start | bytes 405512 | tf_op jit(solution)/shard_map/ppermute | solution.py:379
  20.5 7.8 %collective-permute-start.3 = (f32[2,32,128]{2,1,0:T(8,128)S(1)}, f32[2,32,128]{2,1,0:T(8,128)S(1)}, u32[]{:S(2)}, u32[]{:S(2)}) collective-permute-start(f32[2,32,128]{2,1,0:T(8,128)S(1)} %get-tuple-element.33), channel_id=1, source_target_pairs={{0,2},{2,0},{16,18},{18,16},{1,3},{3,1},{17,19},{19,17},{4,6},{6,4... | collective-permute-start | bytes 98312 | tf_op jit(solution)/shard_map/ppermute | solution.py:349
  22.1 6.2 %collective-permute-start.4 = (f32[2,32,128]{2,1,0:T(8,128)S(1)}, f32[2,32,128]{2,1,0:T(8,128)S(1)}, u32[]{:S(2)}, u32[]{:S(2)}) collective-permute-start(f32[2,32,128]{2,1,0:T(8,128)S(1)} %get-tuple-element.34), channel_id=1, source_target_pairs={{0,16},{2,18},{16,0},{18,2},{1,17},{3,19},{17,1},{19,3},{4,20},{6,... | collective-permute-start | bytes 98312 | tf_op jit(solution)/shard_map/ppermute | solution.py:349
  23.6 4.8 %collective-permute-start.5 = (f32[2,32,128]{2,1,0:T(8,128)S(1)}, f32[2,32,128]{2,1,0:T(8,128)S(1)}, u32[]{:S(2)}, u32[]{:S(2)}) collective-permute-start(f32[2,32,128]{2,1,0:T(8,128)S(1)} %get-tuple-element.35), channel_id=1, source_target_pairs={{0,18},{2,16},{16,2},{18,0},{1,19},{3,17},{17,3},{19,1},{4,22},{6,... | collective-permute-start | bytes 98312 | tf_op jit(solution)/shard_map/ppermute | solution.py:349
  28.5 1.3 %collective-permute-start.6 = (f32[4,32,128]{2,1,0:T(8,128)S(1)}, f32[4,32,128]{2,1,0:T(8,128)S(1)}, u32[]{:S(2)}, u32[]{:S(2)}) collective-permute-start(f32[4,32,128]{2,1,0:T(8,128)S(1)} %gather.1), channel_id=1, source_target_pairs={{0,1},{1,0},{2,3},{3,2},{4,5},{5,4},{6,7},{7,6},{8,9},{9,8},{10,11... | collective-permute-start | bytes 196616 | tf_op jit(solution)/shard_map/ppermute | solution.py:335
  29.8 8.7 %collective-permute-start.9 = (f16[264,128]{1,0:T(8,128)(2,1)S(1)}, f16[264,128]{1,0:T(8,128)(2,1)S(1)}, u32[]{:S(2)}, u32[]{:S(2)}) collective-permute-start(f16[264,128]{1,0:T(8,128)(2,1)S(1)} %convert_element_type.64), channel_id=1, source_target_pairs={{0,12},{4,8},{8,4},{12,0},{1,13},{5,9},{9,5},{13,1},{2,14},{6,10},... | collective-permute-start | bytes 202760 | tf_op jit(solution)/shard_map/ppermute | solution.py:335
  33.3 6.0 %collective-permute-start.8 = (f16[264,128]{1,0:T(8,128)(2,1)S(1)}, f16[264,128]{1,0:T(8,128)(2,1)S(1)}, u32[]{:S(2)}, u32[]{:S(2)}) collective-permute-start(f16[264,128]{1,0:T(8,128)(2,1)S(1)} %convert_element_type.64), channel_id=1, source_target_pairs={{0,8},{4,12},{8,0},{12,4},{1,9},{5,13},{9,1},{13,5},{2,10},{6,14},... | collective-permute-start | bytes 202760 | tf_op jit(solution)/shard_map/ppermute | solution.py:335
  33.3 6.0 %collective-permute-start.7 = (f16[264,128]{1,0:T(8,128)(2,1)S(1)}, f16[264,128]{1,0:T(8,128)(2,1)S(1)}, u32[]{:S(2)}, u32[]{:S(2)}) collective-permute-start(f16[264,128]{1,0:T(8,128)(2,1)S(1)} %convert_element_type.64), channel_id=1, source_target_pairs={{0,4},{4,0},{8,12},{12,8},{1,5},{5,1},{9,13},{13,9},{2,6},{6,2},{1... | collective-permute-start | bytes 202760 | tf_op jit(solution)/shard_map/ppermute | solution.py:335
  45.5 3.2 %collective-permute-start.10 = (f32[2,2,32,1024]{3,2,1,0:T(8,128)S(1)}, f32[2,2,32,1024]{3,2,1,0:T(8,128)S(1)}, u32[]{:S(2)}, u32[]{:S(2)}) collective-permute-start(f32[2,2,32,1024]{3,2,1,0:T(8,128)S(1)} %get-tuple-element.41), channel_id=1, source_target_pairs={{0,1},{1,0},{2,3},{3,2},{4,5},{5,4},{6,7},{7,6},{8,9},{9,8},{10,11... | collective-permute-start | bytes 1572872 | tf_op jit(solution)/shard_map/ppermute | solution.py:335
  48.8 4.7 %collective-permute-start.11 = (bf16[32,1024]{1,0:T(8,128)(2,1)S(1)}, bf16[32,1024]{1,0:T(8,128)(2,1)S(1)}, u32[]{:S(2)}, u32[]{:S(2)}) collective-permute-start(bf16[32,1024]{1,0:T(8,128)(2,1)S(1)} %fusion.7.refs_0_), channel_id=1, source_target_pairs={{0,16},{16,0},{1,17},{17,1},{2,18},{18,2},{3,19},{19,3},{4,20},{20... | collective-permute-start | bytes 196616 | tf_op jit(solution)/shard_map/ppermute | solution.py:335
  53.5 4.3 %collective-permute-start.13 = (bf16[32,1024]{1,0:T(8,128)(2,1)S(1)}, bf16[32,1024]{1,0:T(8,128)(2,1)S(1)}, u32[]{:S(2)}, u32[]{:S(2)}) collective-permute-start(bf16[32,1024]{1,0:T(8,128)(2,1)S(1)} %get-tuple-element.46), channel_id=1, source_target_pairs={{0,16},{16,0},{1,17},{17,1},{2,18},{18,2},{3,19},{19,3},{4,20},{20... | collective-permute-start | bytes 196616 | tf_op jit(solution)/shard_map/ppermute | solution.py:335
  54.9 4.5 %collective-permute-start.12 = (bf16[32,1024]{1,0:T(8,128)(2,1)S(1)}, bf16[32,1024]{1,0:T(8,128)(2,1)S(1)}, u32[]{:S(2)}, u32[]{:S(2)}) collective-permute-start(bf16[32,1024]{1,0:T(8,128)(2,1)S(1)} %get-tuple-element.44), channel_id=1, source_target_pairs={{0,2},{2,0},{1,3},{3,1},{4,6},{6,4},{5,7},{7,5},{8,10},{10,8},{9,1... | collective-permute-start | bytes 196616 | tf_op jit(solution)/shard_map/ppermute | solution.py:335
  57.9 4.3 %collective-permute-start.14 = (bf16[32,1024]{1,0:T(8,128)(2,1)S(1)}, bf16[32,1024]{1,0:T(8,128)(2,1)S(1)}, u32[]{:S(2)}, u32[]{:S(2)}) collective-permute-start(bf16[32,1024]{1,0:T(8,128)(2,1)S(1)} %fusion.6), channel_id=1, source_target_pairs={{0,2},{2,0},{1,3},{3,1},{4,6},{6,4},{5,7},{7,5},{8,10},{10,8},{9,1... | collective-permute-start | bytes 196616 | tf_op jit(solution)/shard_map/ppermute | solution.py:335
  63.1 1.3 %collective-permute-start.15 = (f32[32,512]{1,0:T(8,128)S(1)}, f32[32,512]{1,0:T(8,128)S(1)}, u32[]{:S(2)}, u32[]{:S(2)}) collective-permute-start(f32[32,512]{1,0:T(8,128)S(1)} %slice_add_fusion), channel_id=1, source_target_pairs={{0,1},{1,0},{2,3},{3,2},{4,5},{5,4},{6,7},{7,6},{8,9},{9,8},{10,11... | collective-permute-start | bytes 196616 | tf_op jit(solution)/shard_map/ppermute | solution.py:335
  64.5 6.0 %collective-permute-start.18 = (f16[40,512]{1,0:T(8,128)(2,1)S(1)}, f16[40,512]{1,0:T(8,128)(2,1)S(1)}, u32[]{:S(2)}, u32[]{:S(2)}) collective-permute-start(f16[40,512]{1,0:T(8,128)(2,1)S(1)} %get-tuple-element.49), channel_id=1, source_target_pairs={{0,12},{4,8},{8,4},{12,0},{1,13},{5,9},{9,5},{13,1},{2,14},{6,10},... | collective-permute-start | bytes 122888 | tf_op jit(solution)/shard_map/ppermute | solution.py:335
  67.3 4.9 %collective-permute-start.17 = (f16[40,512]{1,0:T(8,128)(2,1)S(1)}, f16[40,512]{1,0:T(8,128)(2,1)S(1)}, u32[]{:S(2)}, u32[]{:S(2)}) collective-permute-start(f16[40,512]{1,0:T(8,128)(2,1)S(1)} %get-tuple-element.49), channel_id=1, source_target_pairs={{0,8},{4,12},{8,0},{12,4},{1,9},{5,13},{9,1},{13,5},{2,10},{6,14},... | collective-permute-start | bytes 122888 | tf_op jit(solution)/shard_map/ppermute | solution.py:335
  67.3 4.9 %collective-permute-start.16 = (f16[40,512]{1,0:T(8,128)(2,1)S(1)}, f16[40,512]{1,0:T(8,128)(2,1)S(1)}, u32[]{:S(2)}, u32[]{:S(2)}) collective-permute-start(f16[40,512]{1,0:T(8,128)(2,1)S(1)} %get-tuple-element.49), channel_id=1, source_target_pairs={{0,4},{4,0},{8,12},{12,8},{1,5},{5,1},{9,13},{13,9},{2,6},{6,2},{1... | collective-permute-start | bytes 122888 | tf_op jit(solution)/shard_map/ppermute | solution.py:335

commit v3 on v2

--- a/solution.py
+++ b/solution.py
@@ -157,18 +157,22 @@
     out_ref[...] = tree_sum([restored(ref[:count], ref[count : count + 1]) for ref in refs[:-1]])
 
 
+SMALL = jnp.float8_e5m2
+SMALL_SCALE = 2.0**20
+
+
 def split(block):
     high = block.astype(jnp.bfloat16)
-    return high, (block - high.astype(jnp.float32)).astype(jnp.bfloat16)
+    return high, ((block - high.astype(jnp.float32)) * SMALL_SCALE).astype(SMALL)
 
 
 def gram_split_kernel(place_ref, after_ref, gram_ref, *refs, first):
     del after_ref
     outs, (mark_ref, buffer, sems) = refs[:-3], refs[-3:]
     slots, tile, width = buffer.shape
-    quarter = outs[0].shape[0] // 2
+    quarter = outs[0].shape[0]
     steps = quarter // tile
-    total = steps * len(outs)
+    total = steps * (len(outs) // 2)
     column = pl.multiple_of(place_ref[0] * width, width)
     sub = place_ref[3]
 
@@ -182,7 +186,7 @@
     for i in range(min(slots - 1, total)):
         copy(i).start()
 
-    for part, out_ref in enumerate(outs):
+    for part in range(len(outs) // 2):
 
         @pl.loop(0, steps)
         def _(j):
@@ -195,8 +199,8 @@
             copy(i).wait()
             high, low = split(buffer[lax.rem(i, slots)])
             start = pl.multiple_of(j * tile, tile)
-            out_ref[pl.ds(start, tile)] = high
-            out_ref[pl.ds(start + quarter, tile)] = low
+            outs[2 * part][pl.ds(start, tile)] = high
+            outs[2 * part + 1][pl.ds(start, tile)] = low
 
     mark_ref[...] = jnp.zeros_like(mark_ref)
 
@@ -208,8 +212,8 @@
     *quarters, mark = pl.pallas_call(
         functools.partial(gram_split_kernel, first=first),
         in_specs=[pl.BlockSpec(memory_space=pltpu.SMEM), WHOLE, pl.BlockSpec(memory_space=pltpu.HBM)],
-        out_specs=[WHOLE] * (count + 1),
-        out_shape=[pltpu.VMEM((2 * quarter, half), jnp.bfloat16)] * count
+        out_specs=[WHOLE] * (2 * count + 1),
+        out_shape=[pltpu.VMEM((quarter, half), kind) for kind in (jnp.bfloat16, SMALL)] * count
         + [jax.ShapeDtypeStruct((8, 128), jnp.float32)],
         scratch_shapes=[pltpu.VMEM((slots, tile, half), jnp.float32), pltpu.SemaphoreType.DMA((slots,))],
         compiler_params=pltpu.CompilerParams(vmem_limit_bytes=12 * MIB),
@@ -219,19 +223,19 @@
     return [pltpu.with_memory_space_constraint(x, pltpu.VMEM) for x in quarters], mark
 
 
-def gram_rows(group, gram_ref, terms, write):
-    quarter = gram_ref.shape[0] // 2
-    queries = terms.shape[1] // 2
-    part = jnp.dot(gram_ref[...], terms[...], preferred_element_type=jnp.float32)
-    part = part[:quarter] + part[quarter:]
-    done = (part[:, :queries] + part[:, queries:]).T
+def gram_rows(group, high_ref, low_ref, terms, small_terms, unit, write):
+    queries = small_terms.shape[1]
+    part = jnp.dot(high_ref[...], terms[...], preferred_element_type=jnp.float32)
+    low = jnp.dot(low_ref[...], small_terms[...], preferred_element_type=jnp.float32)
+    done = (part[:, :queries] + part[:, queries:] + low * unit[:1]).T
     for g in range(2):
         write(g ^ group, done[g * (queries // 2) : (g + 1) * (queries // 2)])
 
 
 def away_kernel(place_ref, after_ref, *refs, row_count, own):
     del after_ref
-    grams, sources, (out_ref, terms, natural) = refs[:2], refs[2 : 2 + row_count], refs[2 + row_count :]
+    grams, sources = refs[:4], refs[4 : 4 + row_count]
+    out_ref, terms, small_terms, unit, natural = refs[4 + row_count :]
     group, row, col, sub = (place_ref[i] for i in range(4))
     height, queries, lanes = natural.shape
     for z in range(row_count):
@@ -243,26 +247,32 @@
             for j in range(own):
                 start = (place * own + j) * height
                 natural[:, pl.ds(first + j, 1), :] = piece[start : start + height].reshape(height, 1, lanes)
+    top = jnp.max(jnp.max(jnp.abs(natural[...]), axis=0), axis=1, keepdims=True)
+    k = jnp.ceil(jnp.log(jnp.clip(top, 1e-30, 1e30)) * LOG2E)
+    k = jnp.broadcast_to(k, (queries, lanes)).T[: unit.shape[0]]
+    unit[...] = jnp.exp2(k - 7.0) * (1.0 / SMALL_SCALE)
+    factor = jnp.exp2(7.0 - k[:1])
     for a in range(height):
         block = natural[a]
         high = block.astype(jnp.bfloat16).astype(jnp.float32)
         both = jnp.concatenate([high, block - high], 0).T
         terms[a * lanes : (a + 1) * lanes] = both.astype(jnp.bfloat16)
+        small_terms[a * lanes : (a + 1) * lanes] = (both[:, :queries] * factor).astype(SMALL)
     for i in range(2):
 
         def write(g, value):
             out_ref[i, g] = value
 
-        gram_rows(group, grams[i], terms, write)
-
-
-def home_kernel(place_ref, gram_ref, terms_ref, *refs):
+        gram_rows(group, *grams[2 * i : 2 * i + 2], terms, small_terms, unit, write)
+
+
+def home_kernel(place_ref, high_ref, low_ref, terms_ref, small_ref, unit_ref, *refs):
     out_ref = refs[-1]
 
     def write(g, value):
         out_ref[g] = value
 
-    gram_rows(place_ref[0], gram_ref, terms_ref, write)
+    gram_rows(place_ref[0], high_ref, low_ref, terms_ref, small_ref, unit_ref, write)
 
 
 def join_kernel(early_ref, early_got_ref, late_ref, late_got_ref, early_out, early_wire, late_out, late_wire):
@@ -274,7 +284,7 @@
 
 
 def gram_product(place, after, quarters, sources, own, lanes):
-    quarter, half = quarters[0].shape[0] // 2, quarters[0].shape[1]
+    quarter, half = quarters[0].shape
     row_count = len(sources)
     queries = 8 * row_count * own
     index = pl.BlockSpec(memory_space=pltpu.SMEM)
@@ -287,29 +297,31 @@
             ),
         )
 
-    away, terms = pl.pallas_call(
+    away, *terms = pl.pallas_call(
         functools.partial(away_kernel, row_count=row_count, own=own),
-        in_specs=[index] + [WHOLE] * (3 + row_count),
-        out_specs=[WHOLE, WHOLE],
+        in_specs=[index] + [WHOLE] * (5 + row_count),
+        out_specs=[WHOLE] * 4,
         out_shape=[
             jax.ShapeDtypeStruct((2, 2, queries // 2, quarter), jnp.float32),
             jax.ShapeDtypeStruct((half, 2 * queries), jnp.bfloat16),
+            jax.ShapeDtypeStruct((half, queries), SMALL),
+            jax.ShapeDtypeStruct((PAD, queries), jnp.float32),
         ],
         scratch_shapes=[pltpu.VMEM((half // lanes, queries, lanes), jnp.float32)],
         name="away",
         **common(2),
-    )(place, after, *quarters[:2], *sources)
+    )(place, after, *quarters[:4], *sources)
     got = swapped(away, "sub")
 
     def home(i, *after):
         return pl.pallas_call(
             home_kernel,
-            in_specs=[index] + [WHOLE] * (2 + len(after)),
+            in_specs=[index] + [WHOLE] * (5 + len(after)),
             out_specs=WHOLE,
             out_shape=jax.ShapeDtypeStruct((2, queries // 2, quarter), jnp.float32),
             name="home",
             **common(1),
-        )(place, quarters[2 + i], terms, *after)
+        )(place, *quarters[4 + 2 * i : 6 + 2 * i], *terms, *after)
 
     early = home(0) + got[0]
     wire = early[1].astype(jnp.bfloat16)

time: 73 us -> 71.2 us (0.975)
  Pallas kernels: 35.3 us -> 33.2 us
    pallas_call x1, Pallas kernels: 6.09 us -> 4.9 us  [gram_product(): pl.pallas_call(functools.partial(away_kernel, row_count=row_count, own=ow...]
    pallas_call x2, Pallas kernels: 6.23 us -> 5.24 us  [home(): pl.pallas_call(home_kernel, in_specs=[index] + [WHOLE] * (5 + len(after))...]
  transfers between devices with their start and end apart: 19 -> 19, of which waited for: 9 -> 11; matrix products, arithmetic and copies ran while one was open for 0% -> 0% of each run, Pallas kernels for 34% -> 33%
where the time goes in v3:
time: 71.2 us; the launch traced here: 71 us
  Pallas kernels  33.2 us (47%)
  starting transfers between devices  24.6 us (35%)
  waiting for transfers between devices  11.6 us (16%)
  matrix products  0.76 us (1%)
    pallas_call x3, Pallas kernels, gram_split(): pl.pallas_call(functools.partial(gram_split_kernel, first=first), in_spec...  15.2 us
    ppermute x13, starting transfers between devices, others(): lax.ppermute(pick(index ^ k), axis, [(i, i ^ k) for i in range(size)])  15.2 us
    ppermute x13, waiting for transfers between devices, others(): lax.ppermute(pick(index ^ k), axis, [(i, i ^ k) for i in range(size)])  10.9 us
    pallas_call x2, Pallas kernels, project(): pl.pallas_call(functools.partial(project_kernel, targets=targets), in_spe...  6.16 us
    ppermute x3, starting transfers between devices, body(): lax.ppermute(part.astype(jnp.float16), 'row', [(i, i ^ k) for i in range(...  5.82 us
    pallas_call x2, Pallas kernels, home(): pl.pallas_call(home_kernel, in_specs=[index] + [WHOLE] * (5 + len(after))...  5.24 us
    pallas_call x1, Pallas kernels, gram_product(): pl.pallas_call(functools.partial(away_kernel, row_count=row_count, own=ow...  4.9 us
    ppermute x3, starting transfers between devices, peers(): lax.ppermute(pick(k), ('groups', 'col'), [(i, i ^ k) for i in range(4)])  3.55 us
  transfers between devices with their start and end apart: 19, of which 11 were waited for; matrix products, arithmetic and copies ran while one was open for 0% of the time, Pallas kernels for 33%

profile of v3, /device:TPU:0, one launch (start us, length us, event | category | flops | bytes accessed | tf_op | source)
XLA Modules:
  0.0 71.0 jit_solution(12496822721507351297)
XLA Ops:
  0.1 3.1 %project.3 = (f32[528,128]{1,0:T(8,128)S(1)}, f32[528,128]{1,0:T(8,128)S(1)}) custom-call(s32[4]{0:T(128)S(1)} %pad_add_fusion.place_ref, bf16[8,128,1024]{2,1,0:T(8,128)(2,1)} %refs_0_.3, bf16[8,128,1024]{2,1,0:T(8,128)(2,1)} %refs_1_.3, bf16[1024,128]{1,0:T(8,128)(2,1)} %refs_2_.3, bf16[1024,128]{1,0:T(8,128)(2,1)} %refs_3_.3), custom_call_target="tpu_custom_call" | custom-call | tf_op jit(solution)/shard_map/project/pallas_call | solution.py:90
  3.2 4.1 %collective-permute-start.1 = (f16[528,128]{1,0:T(8,128)(2,1)S(1)}, f16[528,128]{1,0:T(8,128)(2,1)S(1)}, u32[]{:S(2)}, u32[]{:S(2)}) collective-permute-start(f16[528,128]{1,0:T(8,128)(2,1)S(1)} %convert_element_type.60), channel_id=1, source_target_pairs={{0,8},{4,12},{8,0},{12,4},{1,9},{5,13},{9,1},{13,5},{2,10},{6,14},... | collective-permute-start | bytes 405512 | tf_op jit(solution)/shard_map/ppermute | solution.py:391
  7.3 1.4 %collective-permute-start = (f16[528,128]{1,0:T(8,128)(2,1)S(1)}, f16[528,128]{1,0:T(8,128)(2,1)S(1)}, u32[]{:S(2)}, u32[]{:S(2)}) collective-permute-start(f16[528,128]{1,0:T(8,128)(2,1)S(1)} %convert_element_type.58), channel_id=1, source_target_pairs={{0,12},{4,8},{8,4},{12,0},{1,13},{5,9},{9,5},{13,1},{2,14},{6,10},... | collective-permute-start | bytes 405512 | tf_op jit(solution)/shard_map/ppermute | solution.py:391
  8.8 3.1 %project.2 = (f32[528,128]{1,0:T(8,128)S(1)}, f32[528,128]{1,0:T(8,128)S(1)}) custom-call(s32[4]{0:T(128)S(1)} %pad_add_fusion.place_ref, bf16[8,128,1024]{2,1,0:T(8,128)(2,1)} %refs_0_.3, bf16[8,128,1024]{2,1,0:T(8,128)(2,1)} %refs_1_.3, bf16[1024,128]{1,0:T(8,128)(2,1)} %refs_2_.3, bf16[1024,128]{1,0:T(8,128)(2,1)} %refs_3_.3), custom_call_target="tpu_custom_call" | custom-call | tf_op jit(solution)/shard_map/project/pallas_call | solution.py:90
  12.2 6.8 %gram_split.3 = (bf16[1024,2048]{1,0:T(8,128)(2,1)S(1)}, f8e5m2[1024,2048]{1,0:T(32,128)(4,1)S(1)}, bf16[1024,2048]{1,0:T(8,128)(2,1)S(1)}, f8e5m2[1024,2048]{1,0:T(32,128)(4,1)S(1)}, f32[8,128]{1,0:T(8,128)S(1)}) custom-call(s32[4]{0:T(128)S(1)} %pad_add_fusion.place_ref, f32[528,128]{1,0:T(8,128)S(1)} %get-tuple-element.32.after_ref.own_ref, ...), custom_call_target="tpu_custom_call" | custom-call | bytes 16777216 | tf_op jit(solution)/shard_map/gram_split/pallas_call | solution.py:212
  20.5 1.6 %collective-permute-start.3 = (f32[2,32,128]{2,1,0:T(8,128)S(1)}, f32[2,32,128]{2,1,0:T(8,128)S(1)}, u32[]{:S(2)}, u32[]{:S(2)}) collective-permute-start(f32[2,32,128]{2,1,0:T(8,128)S(1)} %get-tuple-element.40), channel_id=1, source_target_pairs={{0,2},{2,0},{16,18},{18,16},{1,3},{3,1},{17,19},{19,17},{4,6},{6,4... | collective-permute-start | bytes 98312 | tf_op jit(solution)/shard_map/ppermute | solution.py:361
  22.1 1.5 %collective-permute-start.4 = (f32[2,32,128]{2,1,0:T(8,128)S(1)}, f32[2,32,128]{2,1,0:T(8,128)S(1)}, u32[]{:S(2)}, u32[]{:S(2)}) collective-permute-start(f32[2,32,128]{2,1,0:T(8,128)S(1)} %get-tuple-element.41), channel_id=1, source_target_pairs={{0,16},{2,18},{16,0},{18,2},{1,17},{3,19},{17,1},{19,3},{4,20},{6,... | collective-permute-start | bytes 98312 | tf_op jit(solution)/shard_map/ppermute | solution.py:361
  24.1 4.2 %gram_split.4 = (bf16[1024,2048]{1,0:T(8,128)(2,1)S(1)}, f8e5m2[1024,2048]{1,0:T(32,128)(4,1)S(1)}, f32[8,128]{1,0:T(8,128)S(1)}) custom-call(s32[4]{0:T(128)S(1)} %pad_add_fusion.place_ref, f32[2,32,128]{2,1,0:T(8,128)S(1)} %get-tuple-element.37.after_ref.refs_0_, f32[4096,4096]{1,0:T(8,128)} %gram_ref.5), custom_call_target="tpu_custom_call" | custom-call | bytes 8388608 | tf_op jit(solution)/shard_map/gram_split/pallas_call | solution.py:212
  28.5 1.2 %collective-permute-done.6.refs_4_ = f32[4,32,128]{2,1,0:T(8,128)S(1)} collective-permute-done((f32[4,32,128]{2,1,0:T(8,128)S(1)}, f32[4,32,128]{2,1,0:T(8,128)S(1)}, u32[]{:S(2)}, u32[]{:S(2)}) %collective-permute-start.6) | collective-permute-done | bytes 65568 | tf_op jit(solution)/shard_map/ppermute | solution.py:347
  29.8 3.6 %collective-permute-start.9 = (f16[264,128]{1,0:T(8,128)(2,1)S(1)}, f16[264,128]{1,0:T(8,128)(2,1)S(1)}, u32[]{:S(2)}, u32[]{:S(2)}) collective-permute-start(f16[264,128]{1,0:T(8,128)(2,1)S(1)} %convert_element_type.64), channel_id=1, source_target_pairs={{0,12},{4,8},{8,4},{12,0},{1,13},{5,9},{9,5},{13,1},{2,14},{6,10},... | collective-permute-start | bytes 202760 | tf_op jit(solution)/shard_map/ppermute | solution.py:347
  34.2 4.2 %gram_split.5 = (bf16[1024,2048]{1,0:T(8,128)(2,1)S(1)}, f8e5m2[1024,2048]{1,0:T(32,128)(4,1)S(1)}, f32[8,128]{1,0:T(8,128)S(1)}) custom-call(s32[4]{0:T(128)S(1)} %pad_add_fusion.place_ref, f32[264,128]{1,0:T(8,128)S(1)} %pack.1.after_ref.refs_4_, f32[4096,4096]{1,0:T(8,128)} %gram_ref.5), custom_call_target="tpu_custom_call" | custom-call | bytes 8388608 | tf_op jit(solution)/shard_map/gram_split/pallas_call | solution.py:212
  39.4 4.9 %away.1 = (f32[2,2,32,1024]{3,2,1,0:T(8,128)S(1)}, bf16[2048,128]{1,0:T(8,128)(2,1)S(1)}, f8e5m2[2048,64]{1,0:T(32,128)(4,1)S(1)}, f32[8,64]{1,0:T(8,128)S(1)}) custom-call(s32[4]{0:T(128)S(1)} %pad_add_fusion.place_ref, f32[8,128]{1,0:T(8,128)S(1)} %get-tuple-element.44.after_ref, bf16[1024,2048]{1,0:T(8,128)(2,1)S(1)} %get-tuple-element.45.refs_0_, ...), custom_call_target="tpu_custom_call" | custom-call | flops 2147483648 | bytes 4194304 | tf_op jit(solution)/shard_map/away/pallas_call | solution.py:300
  44.4 2.6 %home.2 = f32[2,32,1024]{2,1,0:T(8,128)S(1)} custom-call(s32[4]{0:T(128)S(1)} %pad_add_fusion.place_ref, bf16[1024,2048]{1,0:T(8,128)(2,1)S(1)} %get-tuple-element.38.high_ref, f8e5m2[1024,2048]{1,0:T(32,128)(4,1)S(1)} %get-tuple-element.39.low_ref, bf16[2048,128]{1,0:T(8,128)(2,1)S(1)} %get-tuple-element.49.terms_ref, ...), custom_call_target="tpu_custom_call" | custom-call | flops 1073741824 | bytes 2097152 | tf_op jit(solution)/shard_map/home/pallas_call | solution.py:317
  47.1 1.6 %collective-permute-start.11 = (bf16[32,1024]{1,0:T(8,128)(2,1)S(1)}, bf16[32,1024]{1,0:T(8,128)(2,1)S(1)}, u32[]{:S(2)}, u32[]{:S(2)}) collective-permute-start(bf16[32,1024]{1,0:T(8,128)(2,1)S(1)} %fusion.7.refs_0_), channel_id=1, source_target_pairs={{0,16},{16,0},{1,17},{17,1},{2,18},{18,2},{3,19},{19,3},{4,20},{20... | collective-permute-start | bytes 196616 | tf_op jit(solution)/shard_map/ppermute | solution.py:347
  48.7 2.6 %home.3.late_ref = f32[2,32,1024]{2,1,0:T(8,128)S(1)} custom-call(s32[4]{0:T(128)S(1)} %pad_add_fusion.place_ref, bf16[1024,2048]{1,0:T(8,128)(2,1)S(1)} %get-tuple-element.53.high_ref, f8e5m2[1024,2048]{1,0:T(32,128)(4,1)S(1)} %get-tuple-element.54.low_ref, bf16[2048,128]{1,0:T(8,128)(2,1)S(1)} %get-tuple-element.49.terms_ref, ...), custom_call_target="tpu_custom_call" | custom-call | flops 1073741824 | bytes 2097152 | tf_op jit(solution)/shard_map/home/pallas_call | solution.py:317
  51.7 1.6 %collective-permute-start.13 = (bf16[32,1024]{1,0:T(8,128)(2,1)S(1)}, bf16[32,1024]{1,0:T(8,128)(2,1)S(1)}, u32[]{:S(2)}, u32[]{:S(2)}) collective-permute-start(bf16[32,1024]{1,0:T(8,128)(2,1)S(1)} %get-tuple-element.58), channel_id=1, source_target_pairs={{0,16},{16,0},{1,17},{17,1},{2,18},{18,2},{3,19},{19,3},{4,20},{20... | collective-permute-start | bytes 196616 | tf_op jit(solution)/shard_map/ppermute | solution.py:347
  53.2 1.5 %collective-permute-start.12 = (bf16[32,1024]{1,0:T(8,128)(2,1)S(1)}, bf16[32,1024]{1,0:T(8,128)(2,1)S(1)}, u32[]{:S(2)}, u32[]{:S(2)}) collective-permute-start(bf16[32,1024]{1,0:T(8,128)(2,1)S(1)} %get-tuple-element.56), channel_id=1, source_target_pairs={{0,2},{2,0},{1,3},{3,1},{4,6},{6,4},{5,7},{7,5},{8,10},{10,8},{9,1... | collective-permute-start | bytes 196616 | tf_op jit(solution)/shard_map/ppermute | solution.py:347
  54.7 1.3 %collective-permute-done.13 = bf16[32,1024]{1,0:T(8,128)(2,1)S(1)} collective-permute-done((bf16[32,1024]{1,0:T(8,128)(2,1)S(1)}, bf16[32,1024]{1,0:T(8,128)(2,1)S(1)}, u32[]{:S(2)}, u32[]{:S(2)}) %collective-permute-start.13) | collective-permute-done | bytes 65568 | tf_op jit(solution)/shard_map/ppermute | solution.py:347
  56.0 1.5 %collective-permute-start.14 = (bf16[32,1024]{1,0:T(8,128)(2,1)S(1)}, bf16[32,1024]{1,0:T(8,128)(2,1)S(1)}, u32[]{:S(2)}, u32[]{:S(2)}) collective-permute-start(bf16[32,1024]{1,0:T(8,128)(2,1)S(1)} %fusion.6), channel_id=1, source_target_pairs={{0,2},{2,0},{1,3},{3,1},{4,6},{6,4},{5,7},{7,5},{8,10},{10,8},{9,1... | collective-permute-start | bytes 196616 | tf_op jit(solution)/shard_map/ppermute | solution.py:347
  57.7 2.7 %collective-permute-done.14 = bf16[32,1024]{1,0:T(8,128)(2,1)S(1)} collective-permute-done((bf16[32,1024]{1,0:T(8,128)(2,1)S(1)}, bf16[32,1024]{1,0:T(8,128)(2,1)S(1)}, u32[]{:S(2)}, u32[]{:S(2)}) %collective-permute-start.14) | collective-permute-done | bytes 65568 | tf_op jit(solution)/shard_map/ppermute | solution.py:347
  62.7 2.8 %collective-permute-start.18 = (f16[40,512]{1,0:T(8,128)(2,1)S(1)}, f16[40,512]{1,0:T(8,128)(2,1)S(1)}, u32[]{:S(2)}, u32[]{:S(2)}) collective-permute-start(f16[40,512]{1,0:T(8,128)(2,1)S(1)} %get-tuple-element.61), channel_id=1, source_target_pairs={{0,12},{4,8},{8,4},{12,0},{1,13},{5,9},{9,5},{13,1},{2,14},{6,10},... | collective-permute-start | bytes 122888 | tf_op jit(solution)/shard_map/ppermute | solution.py:347
  65.5 1.7 %collective-permute-start.16 = (f16[40,512]{1,0:T(8,128)(2,1)S(1)}, f16[40,512]{1,0:T(8,128)(2,1)S(1)}, u32[]{:S(2)}, u32[]{:S(2)}) collective-permute-start(f16[40,512]{1,0:T(8,128)(2,1)S(1)} %get-tuple-element.61), channel_id=1, source_target_pairs={{0,4},{4,0},{8,12},{12,8},{1,5},{5,1},{9,13},{13,9},{2,6},{6,2},{1... | collective-permute-start | bytes 122888 | tf_op jit(solution)/shard_map/ppermute | solution.py:347
  67.1 1.5 %collective-permute-done.18 = f16[40,512]{1,0:T(8,128)(2,1)S(1)} collective-permute-done((f16[40,512]{1,0:T(8,128)(2,1)S(1)}, f16[40,512]{1,0:T(8,128)(2,1)S(1)}, u32[]{:S(2)}, u32[]{:S(2)}) %collective-permute-start.18) | collective-permute-done | bytes 40992 | tf_op jit(solution)/shard_map/ppermute | solution.py:347
  68.7 1.7 %collective-permute-done.17 = f16[40,512]{1,0:T(8,128)(2,1)S(1)} collective-permute-done((f16[40,512]{1,0:T(8,128)(2,1)S(1)}, f16[40,512]{1,0:T(8,128)(2,1)S(1)}, u32[]{:S(2)}, u32[]{:S(2)}) %collective-permute-start.17) | collective-permute-done | bytes 40992 | tf_op jit(solution)/shard_map/ppermute | solution.py:347
  (56 shorter events, 7.9 us)
Async XLA Ops:
  0.0 60.4 %copy-start = (bf16[512,2048]{1,0:T(8,128)(2,1)S(1)}, bf16[512,2048]{1,0:T(8,128)(2,1)}, u32[]{:S(2)}) copy-start(bf16[512,2048]{1,0:T(8,128)(2,1)} %param.11) | copy-start | bytes 6291460
  3.2 15.8 %collective-permute-start.1 = (f16[528,128]{1,0:T(8,128)(2,1)S(1)}, f16[528,128]{1,0:T(8,128)(2,1)S(1)}, u32[]{:S(2)}, u32[]{:S(2)}) collective-permute-start(f16[528,128]{1,0:T(8,128)(2,1)S(1)} %convert_element_type.60), channel_id=1, source_target_pairs={{0,8},{4,12},{8,0},{12,4},{1,9},{5,13},{9,1},{13,5},{2,10},{6,14},... | collective-permute-start | bytes 405512 | tf_op jit(solution)/shard_map/ppermute | solution.py:391
  7.3 11.7 %collective-permute-start = (f16[528,128]{1,0:T(8,128)(2,1)S(1)}, f16[528,128]{1,0:T(8,128)(2,1)S(1)}, u32[]{:S(2)}, u32[]{:S(2)}) collective-permute-start(f16[528,128]{1,0:T(8,128)(2,1)S(1)} %convert_element_type.58), channel_id=1, source_target_pairs={{0,12},{4,8},{8,4},{12,0},{1,13},{5,9},{9,5},{13,1},{2,14},{6,10},... | collective-permute-start | bytes 405512 | tf_op jit(solution)/shard_map/ppermute | solution.py:391
  11.9 7.7 %collective-permute-start.2 = (f16[528,128]{1,0:T(8,128)(2,1)S(1)}, f16[528,128]{1,0:T(8,128)(2,1)S(1)}, u32[]{:S(2)}, u32[]{:S(2)}) collective-permute-start(f16[528,128]{1,0:T(8,128)(2,1)S(1)} %convert_element_type.62), channel_id=1, source_target_pairs={{0,4},{4,0},{8,12},{12,8},{1,5},{5,1},{9,13},{13,9},{2,6},{6,2},{1... | collective-permute-start | bytes 405512 | tf_op jit(solution)/shard_map/ppermute | solution.py:391
  20.5 7.8 %collective-permute-start.3 = (f32[2,32,128]{2,1,0:T(8,128)S(1)}, f32[2,32,128]{2,1,0:T(8,128)S(1)}, u32[]{:S(2)}, u32[]{:S(2)}) collective-permute-start(f32[2,32,128]{2,1,0:T(8,128)S(1)} %get-tuple-element.40), channel_id=1, source_target_pairs={{0,2},{2,0},{16,18},{18,16},{1,3},{3,1},{17,19},{19,17},{4,6},{6,4... | collective-permute-start | bytes 98312 | tf_op jit(solution)/shard_map/ppermute | solution.py:361
  22.1 6.2 %collective-permute-start.4 = (f32[2,32,128]{2,1,0:T(8,128)S(1)}, f32[2,32,128]{2,1,0:T(8,128)S(1)}, u32[]{:S(2)}, u32[]{:S(2)}) collective-permute-start(f32[2,32,128]{2,1,0:T(8,128)S(1)} %get-tuple-element.41), channel_id=1, source_target_pairs={{0,16},{2,18},{16,0},{18,2},{1,17},{3,19},{17,1},{19,3},{4,20},{6,... | collective-permute-start | bytes 98312 | tf_op jit(solution)/shard_map/ppermute | solution.py:361
  23.6 4.8 %collective-permute-start.5 = (f32[2,32,128]{2,1,0:T(8,128)S(1)}, f32[2,32,128]{2,1,0:T(8,128)S(1)}, u32[]{:S(2)}, u32[]{:S(2)}) collective-permute-start(f32[2,32,128]{2,1,0:T(8,128)S(1)} %get-tuple-element.42), channel_id=1, source_target_pairs={{0,18},{2,16},{16,2},{18,0},{1,19},{3,17},{17,3},{19,1},{4,22},{6,... | collective-permute-start | bytes 98312 | tf_op jit(solution)/shard_map/ppermute | solution.py:361
  28.5 1.3 %collective-permute-start.6 = (f32[4,32,128]{2,1,0:T(8,128)S(1)}, f32[4,32,128]{2,1,0:T(8,128)S(1)}, u32[]{:S(2)}, u32[]{:S(2)}) collective-permute-start(f32[4,32,128]{2,1,0:T(8,128)S(1)} %gather.1), channel_id=1, source_target_pairs={{0,1},{1,0},{2,3},{3,2},{4,5},{5,4},{6,7},{7,6},{8,9},{9,8},{10,11... | collective-permute-start | bytes 196616 | tf_op jit(solution)/shard_map/ppermute | solution.py:347
  29.8 8.7 %collective-permute-start.9 = (f16[264,128]{1,0:T(8,128)(2,1)S(1)}, f16[264,128]{1,0:T(8,128)(2,1)S(1)}, u32[]{:S(2)}, u32[]{:S(2)}) collective-permute-start(f16[264,128]{1,0:T(8,128)(2,1)S(1)} %convert_element_type.64), channel_id=1, source_target_pairs={{0,12},{4,8},{8,4},{12,0},{1,13},{5,9},{9,5},{13,1},{2,14},{6,10},... | collective-permute-start | bytes 202760 | tf_op jit(solution)/shard_map/ppermute | solution.py:347
  33.3 6.0 %collective-permute-start.8 = (f16[264,128]{1,0:T(8,128)(2,1)S(1)}, f16[264,128]{1,0:T(8,128)(2,1)S(1)}, u32[]{:S(2)}, u32[]{:S(2)}) collective-permute-start(f16[264,128]{1,0:T(8,128)(2,1)S(1)} %convert_element_type.64), channel_id=1, source_target_pairs={{0,8},{4,12},{8,0},{12,4},{1,9},{5,13},{9,1},{13,5},{2,10},{6,14},... | collective-permute-start | bytes 202760 | tf_op jit(solution)/shard_map/ppermute | solution.py:347
  33.3 6.0 %collective-permute-start.7 = (f16[264,128]{1,0:T(8,128)(2,1)S(1)}, f16[264,128]{1,0:T(8,128)(2,1)S(1)}, u32[]{:S(2)}, u32[]{:S(2)}) collective-permute-start(f16[264,128]{1,0:T(8,128)(2,1)S(1)} %convert_element_type.64), channel_id=1, source_target_pairs={{0,4},{4,0},{8,12},{12,8},{1,5},{5,1},{9,13},{13,9},{2,6},{6,2},{1... | collective-permute-start | bytes 202760 | tf_op jit(solution)/shard_map/ppermute | solution.py:347
  44.3 2.7 %collective-permute-start.10 = (f32[2,2,32,1024]{3,2,1,0:T(8,128)S(1)}, f32[2,2,32,1024]{3,2,1,0:T(8,128)S(1)}, u32[]{:S(2)}, u32[]{:S(2)}) collective-permute-start(f32[2,2,32,1024]{3,2,1,0:T(8,128)S(1)} %get-tuple-element.52), channel_id=1, source_target_pairs={{0,1},{1,0},{2,3},{3,2},{4,5},{5,4},{6,7},{7,6},{8,9},{9,8},{10,11... | collective-permute-start | bytes 1572872 | tf_op jit(solution)/shard_map/ppermute | solution.py:347
  47.1 4.6 %collective-permute-start.11 = (bf16[32,1024]{1,0:T(8,128)(2,1)S(1)}, bf16[32,1024]{1,0:T(8,128)(2,1)S(1)}, u32[]{:S(2)}, u32[]{:S(2)}) collective-permute-start(bf16[32,1024]{1,0:T(8,128)(2,1)S(1)} %fusion.7.refs_0_), channel_id=1, source_target_pairs={{0,16},{16,0},{1,17},{17,1},{2,18},{18,2},{3,19},{19,3},{4,20},{20... | collective-permute-start | bytes 196616 | tf_op jit(solution)/shard_map/ppermute | solution.py:347
  51.7 4.3 %collective-permute-start.13 = (bf16[32,1024]{1,0:T(8,128)(2,1)S(1)}, bf16[32,1024]{1,0:T(8,128)(2,1)S(1)}, u32[]{:S(2)}, u32[]{:S(2)}) collective-permute-start(bf16[32,1024]{1,0:T(8,128)(2,1)S(1)} %get-tuple-element.58), channel_id=1, source_target_pairs={{0,16},{16,0},{1,17},{17,1},{2,18},{18,2},{3,19},{19,3},{4,20},{20... | collective-permute-start | bytes 196616 | tf_op jit(solution)/shard_map/ppermute | solution.py:347
  53.2 4.4 %collective-permute-start.12 = (bf16[32,1024]{1,0:T(8,128)(2,1)S(1)}, bf16[32,1024]{1,0:T(8,128)(2,1)S(1)}, u32[]{:S(2)}, u32[]{:S(2)}) collective-permute-start(bf16[32,1024]{1,0:T(8,128)(2,1)S(1)} %get-tuple-element.56), channel_id=1, source_target_pairs={{0,2},{2,0},{1,3},{3,1},{4,6},{6,4},{5,7},{7,5},{8,10},{10,8},{9,1... | collective-permute-start | bytes 196616 | tf_op jit(solution)/shard_map/ppermute | solution.py:347
  56.0 4.3 %collective-permute-start.14 = (bf16[32,1024]{1,0:T(8,128)(2,1)S(1)}, bf16[32,1024]{1,0:T(8,128)(2,1)S(1)}, u32[]{:S(2)}, u32[]{:S(2)}) collective-permute-start(bf16[32,1024]{1,0:T(8,128)(2,1)S(1)} %fusion.6), channel_id=1, source_target_pairs={{0,2},{2,0},{1,3},{3,1},{4,6},{6,4},{5,7},{7,5},{8,10},{10,8},{9,1... | collective-permute-start | bytes 196616 | tf_op jit(solution)/shard_map/ppermute | solution.py:347
  61.2 1.3 %collective-permute-start.15 = (f32[32,512]{1,0:T(8,128)S(1)}, f32[32,512]{1,0:T(8,128)S(1)}, u32[]{:S(2)}, u32[]{:S(2)}) collective-permute-start(f32[32,512]{1,0:T(8,128)S(1)} %slice_add_fusion), channel_id=1, source_target_pairs={{0,1},{1,0},{2,3},{3,2},{4,5},{5,4},{6,7},{7,6},{8,9},{9,8},{10,11... | collective-permute-start | bytes 196616 | tf_op jit(solution)/shard_map/ppermute | solution.py:347
  62.7 6.0 %collective-permute-start.18 = (f16[40,512]{1,0:T(8,128)(2,1)S(1)}, f16[40,512]{1,0:T(8,128)(2,1)S(1)}, u32[]{:S(2)}, u32[]{:S(2)}) collective-permute-start(f16[40,512]{1,0:T(8,128)(2,1)S(1)} %get-tuple-element.61), channel_id=1, source_target_pairs={{0,12},{4,8},{8,4},{12,0},{1,13},{5,9},{9,5},{13,1},{2,14},{6,10},... | collective-permute-start | bytes 122888 | tf_op jit(solution)/shard_map/ppermute | solution.py:347
  65.5 4.9 %collective-permute-start.17 = (f16[40,512]{1,0:T(8,128)(2,1)S(1)}, f16[40,512]{1,0:T(8,128)(2,1)S(1)}, u32[]{:S(2)}, u32[]{:S(2)}) collective-permute-start(f16[40,512]{1,0:T(8,128)(2,1)S(1)} %get-tuple-element.61), channel_id=1, source_target_pairs={{0,8},{4,12},{8,0},{12,4},{1,9},{5,13},{9,1},{13,5},{2,10},{6,14},... | collective-permute-start | bytes 122888 | tf_op jit(solution)/shard_map/ppermute | solution.py:347
  65.5 4.9 %collective-permute-start.16 = (f16[40,512]{1,0:T(8,128)(2,1)S(1)}, f16[40,512]{1,0:T(8,128)(2,1)S(1)}, u32[]{:S(2)}, u32[]{:S(2)}) collective-permute-start(f16[40,512]{1,0:T(8,128)(2,1)S(1)} %get-tuple-element.61), channel_id=1, source_target_pairs={{0,4},{4,0},{8,12},{12,8},{1,5},{5,1},{9,13},{13,9},{2,6},{6,2},{1... | collective-permute-start | bytes 122888 | tf_op jit(solution)/shard_map/ppermute | solution.py:347

commit v4 on v3

--- a/solution.py
+++ b/solution.py
@@ -223,13 +223,16 @@
     return [pltpu.with_memory_space_constraint(x, pltpu.VMEM) for x in quarters], mark
 
 
-def gram_rows(group, high_ref, low_ref, terms, small_terms, unit, write):
+def gram_rows(group, grams, terms, small_terms, unit, out_ref):
     queries = small_terms.shape[1]
-    part = jnp.dot(high_ref[...], terms[...], preferred_element_type=jnp.float32)
-    low = jnp.dot(low_ref[...], small_terms[...], preferred_element_type=jnp.float32)
-    done = (part[:, :queries] + part[:, queries:] + low * unit[:1]).T
-    for g in range(2):
-        write(g ^ group, done[g * (queries // 2) : (g + 1) * (queries // 2)])
+    quarter = grams[0].shape[0]
+    for i in range(len(grams) // 2):
+        part = jnp.dot(grams[2 * i][...], terms[...], preferred_element_type=jnp.float32)
+        low = jnp.dot(grams[2 * i + 1][...], small_terms[...], preferred_element_type=jnp.float32)
+        done = (part[:, :queries] + part[:, queries:] + low * unit[:1]).T
+        for g in range(2):
+            rows = slice(i * quarter, (i + 1) * quarter)
+            out_ref[g ^ group, :, rows] = done[g * (queries // 2) : (g + 1) * (queries // 2)]
 
 
 def away_kernel(place_ref, after_ref, *refs, row_count, own):
@@ -258,29 +261,11 @@
         both = jnp.concatenate([high, block - high], 0).T
         terms[a * lanes : (a + 1) * lanes] = both.astype(jnp.bfloat16)
         small_terms[a * lanes : (a + 1) * lanes] = (both[:, :queries] * factor).astype(SMALL)
-    for i in range(2):
-
-        def write(g, value):
-            out_ref[i, g] = value
-
-        gram_rows(group, *grams[2 * i : 2 * i + 2], terms, small_terms, unit, write)
-
-
-def home_kernel(place_ref, high_ref, low_ref, terms_ref, small_ref, unit_ref, *refs):
-    out_ref = refs[-1]
-
-    def write(g, value):
-        out_ref[g] = value
-
-    gram_rows(place_ref[0], high_ref, low_ref, terms_ref, small_ref, unit_ref, write)
-
-
-def join_kernel(early_ref, early_got_ref, late_ref, late_got_ref, early_out, early_wire, late_out, late_wire):
-    early = early_ref[...] + early_got_ref[...].astype(jnp.float32)
-    early_out[...] = early
-    early_wire[...] = early.astype(jnp.bfloat16)
-    late_out[...] = late_ref[0] + late_got_ref[0]
-    late_wire[...] = (late_ref[1] + late_got_ref[1]).astype(jnp.bfloat16)
+    gram_rows(group, grams, terms, small_terms, unit, out_ref)
+
+
+def home_kernel(place_ref, *refs):
+    gram_rows(place_ref[0], refs[:4], *refs[4:])
 
 
 def gram_product(place, after, quarters, sources, own, lanes):
@@ -289,56 +274,34 @@
     queries = 8 * row_count * own
     index = pl.BlockSpec(memory_space=pltpu.SMEM)
 
-    def common(count):
-        return dict(
-            compiler_params=pltpu.CompilerParams(vmem_limit_bytes=8 * MIB),
-            cost_estimate=pl.CostEstimate(
-                flops=8 * count * queries * quarter * half, bytes_accessed=count * quarter * half, transcendentals=0
-            ),
-        )
-
+    out = jax.ShapeDtypeStruct((2, queries // 2, 2 * quarter), jnp.float32)
+    common = dict(
+        compiler_params=pltpu.CompilerParams(vmem_limit_bytes=8 * MIB),
+        cost_estimate=pl.CostEstimate(
+            flops=16 * queries * quarter * half, bytes_accessed=6 * quarter * half, transcendentals=0
+        ),
+    )
     away, *terms = pl.pallas_call(
         functools.partial(away_kernel, row_count=row_count, own=own),
         in_specs=[index] + [WHOLE] * (5 + row_count),
         out_specs=[WHOLE] * 4,
         out_shape=[
-            jax.ShapeDtypeStruct((2, 2, queries // 2, quarter), jnp.float32),
+            out,
             jax.ShapeDtypeStruct((half, 2 * queries), jnp.bfloat16),
             jax.ShapeDtypeStruct((half, queries), SMALL),
             jax.ShapeDtypeStruct((PAD, queries), jnp.float32),
         ],
         scratch_shapes=[pltpu.VMEM((half // lanes, queries, lanes), jnp.float32)],
         name="away",
-        **common(2),
+        **common,
     )(place, after, *quarters[:4], *sources)
     got = swapped(away, "sub")
-
-    def home(i, *after):
-        return pl.pallas_call(
-            home_kernel,
-            in_specs=[index] + [WHOLE] * (5 + len(after)),
-            out_specs=WHOLE,
-            out_shape=jax.ShapeDtypeStruct((2, queries // 2, quarter), jnp.float32),
-            name="home",
-            **common(1),
-        )(place, *quarters[4 + 2 * i : 6 + 2 * i], *terms, *after)
-
-    early = home(0) + got[0]
-    wire = early[1].astype(jnp.bfloat16)
-    late = home(1, wire)
-    shape = (queries // 2, quarter)
-    early, early_wire, late, late_wire = pl.pallas_call(
-        join_kernel,
-        in_specs=[WHOLE] * 4,
-        out_specs=[WHOLE] * 4,
-        out_shape=[jax.ShapeDtypeStruct(shape, kind) for kind in (jnp.float32, jnp.bfloat16) * 2],
-        compiler_params=pltpu.CompilerParams(vmem_limit_bytes=4 * MIB),
-        name="join",
-    )(early[0], swapped(wire, "groups"), late, got[1])
-    late = late + swapped(late_wire, "groups").astype(jnp.float32)
-    early = early + swapped(early_wire, "col").astype(jnp.float32)
-    late = late + swapped(late.astype(jnp.bfloat16), "col").astype(jnp.float32)
-    return jnp.concatenate([early, late], 1)
+    home = pl.pallas_call(
+        home_kernel, in_specs=[index] + [WHOLE] * 7, out_specs=WHOLE, out_shape=out, name="home", **common
+    )(place, *quarters[4:], *terms)
+    total = home + got
+    total = total[0] + swapped(total[1].astype(jnp.bfloat16), "groups").astype(jnp.float32)
+    return total + swapped(total.astype(jnp.bfloat16), "col").astype(jnp.float32)
 
 
 def others(pick, axis):

time: 71.2 us -> 72 us (1.011)
  waiting for transfers between devices: 11.6 us -> 16.6 us
  starting transfers between devices: 24.6 us -> 21.5 us
  Pallas kernels: 33.2 us -> 32.1 us
    ppermute x13 -> x11, waiting for transfers between devices: 10.9 us -> 15.7 us  [others(): lax.ppermute(pick(index ^ k), axis, [(i, i ^ k) for i in range(size)])]
    ppermute x13 -> x11, starting transfers between devices: 15.2 us -> 12.2 us  [others(): lax.ppermute(pick(index ^ k), axis, [(i, i ^ k) for i in range(size)])]
    pallas_call x3 -> x1, Pallas kernels: 5.29 us -> 4.22 us  [gram_product(): pl.pallas_call(home_kernel, in_specs=[index] + [WHOLE] * 7, out_specs=WHO...]
  transfers between devices with their start and end apart: 19 -> 17, of which waited for: 11 -> 9; matrix products, arithmetic and copies ran while one was open for 0% -> 0% of each run, Pallas kernels for 33% -> 31%
where the time goes in v4:
time: 72 us; the launch traced here: 71.8 us
  Pallas kernels  32.1 us (45%)
  starting transfers between devices  21.5 us (30%)
  waiting for transfers between devices  16.6 us (23%)
  matrix products  0.76 us (1%)
    ppermute x11, waiting for transfers between devices, others(): lax.ppermute(pick(index ^ k), axis, [(i, i ^ k) for i in range(size)])  15.7 us
    pallas_call x3, Pallas kernels, gram_split(): pl.pallas_call(functools.partial(gram_split_kernel, first=first), in_spec...  15.2 us
    ppermute x11, starting transfers between devices, others(): lax.ppermute(pick(index ^ k), axis, [(i, i ^ k) for i in range(size)])  12.2 us
    pallas_call x2, Pallas kernels, project(): pl.pallas_call(functools.partial(project_kernel, targets=targets), in_spe...  6.16 us
    ppermute x3, starting transfers between devices, body(): lax.ppermute(part.astype(jnp.float16), 'row', [(i, i ^ k) for i in range(...  5.81 us
    pallas_call x1, Pallas kernels, gram_product(): pl.pallas_call(functools.partial(away_kernel, row_count=row_count, own=ow...  4.9 us
    pallas_call x1, Pallas kernels, gram_product(): pl.pallas_call(home_kernel, in_specs=[index] + [WHOLE] * 7, out_specs=WHO...  4.22 us
    ppermute x3, starting transfers between devices, peers(): lax.ppermute(pick(k), ('groups', 'col'), [(i, i ^ k) for i in range(4)])  3.55 us
  transfers between devices with their start and end apart: 17, of which 9 were waited for; matrix products, arithmetic and copies ran while one was open for 0% of the time, Pallas kernels for 31%

profile of v4, /device:TPU:0, one launch (start us, length us, event | category | flops | bytes accessed | tf_op | source)
XLA Modules:
  0.0 71.8 jit_solution(149044166176292519)
XLA Ops:
  0.1 3.1 %project.3 = (f32[528,128]{1,0:T(8,128)S(1)}, f32[528,128]{1,0:T(8,128)S(1)}) custom-call(s32[4]{0:T(128)S(1)} %pad_add_fusion.place_ref, bf16[8,128,1024]{2,1,0:T(8,128)(2,1)} %refs_0_.3, bf16[8,128,1024]{2,1,0:T(8,128)(2,1)} %refs_1_.3, bf16[1024,128]{1,0:T(8,128)(2,1)} %refs_2_.3, bf16[1024,128]{1,0:T(8,128)(2,1)} %refs_3_.3), custom_call_target="tpu_custom_call" | custom-call | tf_op jit(solution)/shard_map/project/pallas_call | solution.py:90
  3.2 5.1 %collective-permute-start = (f16[528,128]{1,0:T(8,128)(2,1)S(1)}, f16[528,128]{1,0:T(8,128)(2,1)S(1)}, u32[]{:S(2)}, u32[]{:S(2)}) collective-permute-start(f16[528,128]{1,0:T(8,128)(2,1)S(1)} %convert_element_type.56), channel_id=1, source_target_pairs={{0,12},{4,8},{8,4},{12,0},{1,13},{5,9},{9,5},{13,1},{2,14},{6,10},... | collective-permute-start | bytes 405512 | tf_op jit(solution)/shard_map/ppermute | solution.py:354
  8.4 3.1 %project.2 = (f32[528,128]{1,0:T(8,128)S(1)}, f32[528,128]{1,0:T(8,128)S(1)}) custom-call(s32[4]{0:T(128)S(1)} %pad_add_fusion.place_ref, bf16[8,128,1024]{2,1,0:T(8,128)(2,1)} %refs_0_.3, bf16[8,128,1024]{2,1,0:T(8,128)(2,1)} %refs_1_.3, bf16[1024,128]{1,0:T(8,128)(2,1)} %refs_2_.3, bf16[1024,128]{1,0:T(8,128)(2,1)} %refs_3_.3), custom_call_target="tpu_custom_call" | custom-call | tf_op jit(solution)/shard_map/project/pallas_call | solution.py:90
  12.2 6.8 %gram_split.3 = (bf16[1024,2048]{1,0:T(8,128)(2,1)S(1)}, f8e5m2[1024,2048]{1,0:T(32,128)(4,1)S(1)}, bf16[1024,2048]{1,0:T(8,128)(2,1)S(1)}, f8e5m2[1024,2048]{1,0:T(32,128)(4,1)S(1)}, f32[8,128]{1,0:T(8,128)S(1)}) custom-call(s32[4]{0:T(128)S(1)} %pad_add_fusion.place_ref, f32[528,128]{1,0:T(8,128)S(1)} %get-tuple-element.28.after_ref.own_ref, ...), custom_call_target="tpu_custom_call" | custom-call | bytes 16777216 | tf_op jit(solution)/shard_map/gram_split/pallas_call | solution.py:212
  19.8 0.9 %kron.1 = (f32[2,32,128]{2,1,0:T(8,128)S(1)}, f32[2,32,128]{2,1,0:T(8,128)S(1)}, f32[2,32,128]{2,1,0:T(8,128)S(1)}, f32[2,32,128]{2,1,0:T(8,128)S(1)}) custom-call(s32[4]{0:T(128)S(1)} %pad_add_fusion.place_ref, f32[8,128]{1,0:T(8,128)S(1)} %get-tuple-element.29.after_ref, f32[528,128]{1,0:T(8,128)S(1)} %get-tuple-element.28.after_ref.own_ref, ...), custom_call_target="tpu_custom_call" | custom-call | tf_op jit(solution)/shard_map/kron/pallas_call | solution.py:331
  20.7 1.6 %collective-permute-start.3 = (f32[2,32,128]{2,1,0:T(8,128)S(1)}, f32[2,32,128]{2,1,0:T(8,128)S(1)}, u32[]{:S(2)}, u32[]{:S(2)}) collective-permute-start(f32[2,32,128]{2,1,0:T(8,128)S(1)} %get-tuple-element.36), channel_id=1, source_target_pairs={{0,2},{2,0},{16,18},{18,16},{1,3},{3,1},{17,19},{19,17},{4,6},{6,4... | collective-permute-start | bytes 98312 | tf_op jit(solution)/shard_map/ppermute | solution.py:324
  22.3 1.5 %collective-permute-start.4 = (f32[2,32,128]{2,1,0:T(8,128)S(1)}, f32[2,32,128]{2,1,0:T(8,128)S(1)}, u32[]{:S(2)}, u32[]{:S(2)}) collective-permute-start(f32[2,32,128]{2,1,0:T(8,128)S(1)} %get-tuple-element.37), channel_id=1, source_target_pairs={{0,16},{2,18},{16,0},{18,2},{1,17},{3,19},{17,1},{19,3},{4,20},{6,... | collective-permute-start | bytes 98312 | tf_op jit(solution)/shard_map/ppermute | solution.py:324
  24.3 4.2 %gram_split.4 = (bf16[1024,2048]{1,0:T(8,128)(2,1)S(1)}, f8e5m2[1024,2048]{1,0:T(32,128)(4,1)S(1)}, f32[8,128]{1,0:T(8,128)S(1)}) custom-call(s32[4]{0:T(128)S(1)} %pad_add_fusion.place_ref, f32[2,32,128]{2,1,0:T(8,128)S(1)} %get-tuple-element.33.after_ref.refs_0_, f32[4096,4096]{1,0:T(8,128)} %gram_ref.5), custom_call_target="tpu_custom_call" | custom-call | bytes 8388608 | tf_op jit(solution)/shard_map/gram_split/pallas_call | solution.py:212
  28.6 1.2 %collective-permute-done.6.refs_4_ = f32[4,32,128]{2,1,0:T(8,128)S(1)} collective-permute-done((f32[4,32,128]{2,1,0:T(8,128)S(1)}, f32[4,32,128]{2,1,0:T(8,128)S(1)}, u32[]{:S(2)}, u32[]{:S(2)}) %collective-permute-start.6) | collective-permute-done | bytes 65568 | tf_op jit(solution)/shard_map/ppermute | solution.py:310
  30.7 2.9 %collective-permute-start.8 = (f16[264,128]{1,0:T(8,128)(2,1)S(1)}, f16[264,128]{1,0:T(8,128)(2,1)S(1)}, u32[]{:S(2)}, u32[]{:S(2)}) collective-permute-start(f16[264,128]{1,0:T(8,128)(2,1)S(1)} %convert_element_type.62), channel_id=1, source_target_pairs={{0,8},{4,12},{8,0},{12,4},{1,9},{5,13},{9,1},{13,5},{2,10},{6,14},... | collective-permute-start | bytes 202760 | tf_op jit(solution)/shard_map/ppermute | solution.py:310
  34.4 4.2 %gram_split.5 = (bf16[1024,2048]{1,0:T(8,128)(2,1)S(1)}, f8e5m2[1024,2048]{1,0:T(32,128)(4,1)S(1)}, f32[8,128]{1,0:T(8,128)S(1)}) custom-call(s32[4]{0:T(128)S(1)} %pad_add_fusion.place_ref, f32[264,128]{1,0:T(8,128)S(1)} %pack.1.after_ref.refs_4_, f32[4096,4096]{1,0:T(8,128)} %gram_ref.5), custom_call_target="tpu_custom_call" | custom-call | bytes 8388608 | tf_op jit(solution)/shard_map/gram_split/pallas_call | solution.py:212
  38.7 1.2 %collective-permute-done.9 = f16[264,128]{1,0:T(8,128)(2,1)S(1)} collective-permute-done((f16[264,128]{1,0:T(8,128)(2,1)S(1)}, f16[264,128]{1,0:T(8,128)(2,1)S(1)}, u32[]{:S(2)}, u32[]{:S(2)}) %collective-permute-start.9) | collective-permute-done | bytes 67616 | tf_op jit(solution)/shard_map/ppermute | solution.py:310
  39.9 4.9 %away.1 = (f32[2,32,2048]{2,1,0:T(8,128)S(1)}, bf16[2048,128]{1,0:T(8,128)(2,1)S(1)}, f8e5m2[2048,64]{1,0:T(32,128)(4,1)S(1)}, f32[8,64]{1,0:T(8,128)S(1)}) custom-call(s32[4]{0:T(128)S(1)} %pad_add_fusion.place_ref, f32[8,128]{1,0:T(8,128)S(1)} %get-tuple-element.42.after_ref, bf16[1024,2048]{1,0:T(8,128)(2,1)S(1)} %get-tuple-element.43.refs_0_, ...), custom_call_target="tpu_custom_call" | custom-call | flops 2147483648 | bytes 12582912 | tf_op jit(solution)/shard_map/away/pallas_call | solution.py:284
  44.8 4.2 %home.1 = f32[2,32,2048]{2,1,0:T(8,128)S(1)} custom-call(s32[4]{0:T(128)S(1)} %pad_add_fusion.place_ref, bf16[1024,2048]{1,0:T(8,128)(2,1)S(1)} %get-tuple-element.34.refs_0_, f8e5m2[1024,2048]{1,0:T(32,128)(4,1)S(1)} %get-tuple-element.35.refs_1_, bf16[1024,2048]{1,0:T(8,128)(2,1)S(1)} %get-tuple-element.40.refs_2_, ...), custom_call_target="tpu_custom_call" | custom-call | flops 2147483648 | bytes 12582912 | tf_op jit(solution)/shard_map/home/pallas_call | solution.py:299
  49.2 1.6 %collective-permute-start.11 = (bf16[32,2048]{1,0:T(8,128)(2,1)S(1)}, bf16[32,2048]{1,0:T(8,128)(2,1)S(1)}, u32[]{:S(2)}, u32[]{:S(2)}) collective-permute-start(bf16[32,2048]{1,0:T(8,128)(2,1)S(1)} %fusion.6), channel_id=1, source_target_pairs={{0,16},{16,0},{1,17},{17,1},{2,18},{18,2},{3,19},{19,3},{4,20},{20... | collective-permute-start | bytes 393224 | tf_op jit(solution)/shard_map/ppermute | solution.py:310
  50.8 4.4 %collective-permute-done.11 = bf16[32,2048]{1,0:T(8,128)(2,1)S(1)} collective-permute-done((bf16[32,2048]{1,0:T(8,128)(2,1)S(1)}, bf16[32,2048]{1,0:T(8,128)(2,1)S(1)}, u32[]{:S(2)}, u32[]{:S(2)}) %collective-permute-start.11) | collective-permute-done | bytes 131104 | tf_op jit(solution)/shard_map/ppermute | solution.py:310
  55.2 1.5 %collective-permute-start.12 = (bf16[32,2048]{1,0:T(8,128)(2,1)S(1)}, bf16[32,2048]{1,0:T(8,128)(2,1)S(1)}, u32[]{:S(2)}, u32[]{:S(2)}) collective-permute-start(bf16[32,2048]{1,0:T(8,128)(2,1)S(1)} %fusion.7), channel_id=1, source_target_pairs={{0,2},{2,0},{1,3},{3,1},{4,6},{6,4},{5,7},{7,5},{8,10},{10,8},{9,1... | collective-permute-start | bytes 393224 | tf_op jit(solution)/shard_map/ppermute | solution.py:310
  56.7 3.6 %collective-permute-done.12 = bf16[32,2048]{1,0:T(8,128)(2,1)S(1)} collective-permute-done((bf16[32,2048]{1,0:T(8,128)(2,1)S(1)}, bf16[32,2048]{1,0:T(8,128)(2,1)S(1)}, u32[]{:S(2)}, u32[]{:S(2)}) %collective-permute-start.12) | collective-permute-done | bytes 131104 | tf_op jit(solution)/shard_map/ppermute | solution.py:310
  61.3 1.2 %collective-permute-done.13 = f32[32,512]{1,0:T(8,128)S(1)} collective-permute-done((f32[32,512]{1,0:T(8,128)S(1)}, f32[32,512]{1,0:T(8,128)S(1)}, u32[]{:S(2)}, u32[]{:S(2)}) %collective-permute-start.13) | collective-permute-done | bytes 65568 | tf_op jit(solution)/shard_map/ppermute | solution.py:310
  62.6 1.0 %collective-permute-start.14 = (f16[40,512]{1,0:T(8,128)(2,1)S(1)}, f16[40,512]{1,0:T(8,128)(2,1)S(1)}, u32[]{:S(2)}, u32[]{:S(2)}) collective-permute-start(f16[40,512]{1,0:T(8,128)(2,1)S(1)} %get-tuple-element.53), channel_id=1, source_target_pairs={{0,4},{4,0},{8,12},{12,8},{1,5},{5,1},{9,13},{13,9},{2,6},{6,2},{1... | collective-permute-start | bytes 122888 | tf_op jit(solution)/shard_map/ppermute | solution.py:310
  63.6 1.7 %collective-permute-start.15 = (f16[40,512]{1,0:T(8,128)(2,1)S(1)}, f16[40,512]{1,0:T(8,128)(2,1)S(1)}, u32[]{:S(2)}, u32[]{:S(2)}) collective-permute-start(f16[40,512]{1,0:T(8,128)(2,1)S(1)} %get-tuple-element.53), channel_id=1, source_target_pairs={{0,8},{4,12},{8,0},{12,4},{1,9},{5,13},{9,1},{13,5},{2,10},{6,14},... | collective-permute-start | bytes 122888 | tf_op jit(solution)/shard_map/ppermute | solution.py:310
  65.3 1.7 %collective-permute-start.16 = (f16[40,512]{1,0:T(8,128)(2,1)S(1)}, f16[40,512]{1,0:T(8,128)(2,1)S(1)}, u32[]{:S(2)}, u32[]{:S(2)}) collective-permute-start(f16[40,512]{1,0:T(8,128)(2,1)S(1)} %get-tuple-element.53), channel_id=1, source_target_pairs={{0,12},{4,8},{8,4},{12,0},{1,13},{5,9},{9,5},{13,1},{2,14},{6,10},... | collective-permute-start | bytes 122888 | tf_op jit(solution)/shard_map/ppermute | solution.py:310
  67.1 2.8 %collective-permute-done.15 = f16[40,512]{1,0:T(8,128)(2,1)S(1)} collective-permute-done((f16[40,512]{1,0:T(8,128)(2,1)S(1)}, f16[40,512]{1,0:T(8,128)(2,1)S(1)}, u32[]{:S(2)}, u32[]{:S(2)}) %collective-permute-start.15) | collective-permute-done | bytes 40992 | tf_op jit(solution)/shard_map/ppermute | solution.py:310
  69.9 1.2 %collective-permute-done.16 = f16[40,512]{1,0:T(8,128)(2,1)S(1)} collective-permute-done((f16[40,512]{1,0:T(8,128)(2,1)S(1)}, f16[40,512]{1,0:T(8,128)(2,1)S(1)}, u32[]{:S(2)}, u32[]{:S(2)}) %collective-permute-start.16) | collective-permute-done | bytes 40992 | tf_op jit(solution)/shard_map/ppermute | solution.py:310
  (46 shorter events, 5.7 us)
Async XLA Ops:
  0.0 60.4 %copy-start = (bf16[512,2048]{1,0:T(8,128)(2,1)S(1)}, bf16[512,2048]{1,0:T(8,128)(2,1)}, u32[]{:S(2)}) copy-start(bf16[512,2048]{1,0:T(8,128)(2,1)} %param.11) | copy-start | bytes 6291460
  3.2 15.8 %collective-permute-start = (f16[528,128]{1,0:T(8,128)(2,1)S(1)}, f16[528,128]{1,0:T(8,128)(2,1)S(1)}, u32[]{:S(2)}, u32[]{:S(2)}) collective-permute-start(f16[528,128]{1,0:T(8,128)(2,1)S(1)} %convert_element_type.56), channel_id=1, source_target_pairs={{0,12},{4,8},{8,4},{12,0},{1,13},{5,9},{9,5},{13,1},{2,14},{6,10},... | collective-permute-start | bytes 405512 | tf_op jit(solution)/shard_map/ppermute | solution.py:354
  8.3 11.4 %collective-permute-start.1 = (f16[528,128]{1,0:T(8,128)(2,1)S(1)}, f16[528,128]{1,0:T(8,128)(2,1)S(1)}, u32[]{:S(2)}, u32[]{:S(2)}) collective-permute-start(f16[528,128]{1,0:T(8,128)(2,1)S(1)} %convert_element_type.58), channel_id=1, source_target_pairs={{0,8},{4,12},{8,0},{12,4},{1,9},{5,13},{9,1},{13,5},{2,10},{6,14},... | collective-permute-start | bytes 405512 | tf_op jit(solution)/shard_map/ppermute | solution.py:354
  11.5 8.2 %collective-permute-start.2 = (f16[528,128]{1,0:T(8,128)(2,1)S(1)}, f16[528,128]{1,0:T(8,128)(2,1)S(1)}, u32[]{:S(2)}, u32[]{:S(2)}) collective-permute-start(f16[528,128]{1,0:T(8,128)(2,1)S(1)} %convert_element_type.60), channel_id=1, source_target_pairs={{0,4},{4,0},{8,12},{12,8},{1,5},{5,1},{9,13},{13,9},{2,6},{6,2},{1... | collective-permute-start | bytes 405512 | tf_op jit(solution)/shard_map/ppermute | solution.py:354
  20.7 7.8 %collective-permute-start.3 = (f32[2,32,128]{2,1,0:T(8,128)S(1)}, f32[2,32,128]{2,1,0:T(8,128)S(1)}, u32[]{:S(2)}, u32[]{:S(2)}) collective-permute-start(f32[2,32,128]{2,1,0:T(8,128)S(1)} %get-tuple-element.36), channel_id=1, source_target_pairs={{0,2},{2,0},{16,18},{18,16},{1,3},{3,1},{17,19},{19,17},{4,6},{6,4... | collective-permute-start | bytes 98312 | tf_op jit(solution)/shard_map/ppermute | solution.py:324
  22.3 6.2 %collective-permute-start.4 = (f32[2,32,128]{2,1,0:T(8,128)S(1)}, f32[2,32,128]{2,1,0:T(8,128)S(1)}, u32[]{:S(2)}, u32[]{:S(2)}) collective-permute-start(f32[2,32,128]{2,1,0:T(8,128)S(1)} %get-tuple-element.37), channel_id=1, source_target_pairs={{0,16},{2,18},{16,0},{18,2},{1,17},{3,19},{17,1},{19,3},{4,20},{6,... | collective-permute-start | bytes 98312 | tf_op jit(solution)/shard_map/ppermute | solution.py:324
  23.8 4.8 %collective-permute-start.5 = (f32[2,32,128]{2,1,0:T(8,128)S(1)}, f32[2,32,128]{2,1,0:T(8,128)S(1)}, u32[]{:S(2)}, u32[]{:S(2)}) collective-permute-start(f32[2,32,128]{2,1,0:T(8,128)S(1)} %get-tuple-element.38), channel_id=1, source_target_pairs={{0,18},{2,16},{16,2},{18,0},{1,19},{3,17},{17,3},{19,1},{4,22},{6,... | collective-permute-start | bytes 98312 | tf_op jit(solution)/shard_map/ppermute | solution.py:324
  28.6 1.3 %collective-permute-start.6 = (f32[4,32,128]{2,1,0:T(8,128)S(1)}, f32[4,32,128]{2,1,0:T(8,128)S(1)}, u32[]{:S(2)}, u32[]{:S(2)}) collective-permute-start(f32[4,32,128]{2,1,0:T(8,128)S(1)} %gather.1), channel_id=1, source_target_pairs={{0,1},{1,0},{2,3},{3,2},{4,5},{5,4},{6,7},{7,6},{8,9},{9,8},{10,11... | collective-permute-start | bytes 196616 | tf_op jit(solution)/shard_map/ppermute | solution.py:310
  29.9 8.7 %collective-permute-start.7 = (f16[264,128]{1,0:T(8,128)(2,1)S(1)}, f16[264,128]{1,0:T(8,128)(2,1)S(1)}, u32[]{:S(2)}, u32[]{:S(2)}) collective-permute-start(f16[264,128]{1,0:T(8,128)(2,1)S(1)} %convert_element_type.62), channel_id=1, source_target_pairs={{0,4},{4,0},{8,12},{12,8},{1,5},{5,1},{9,13},{13,9},{2,6},{6,2},{1... | collective-permute-start | bytes 202760 | tf_op jit(solution)/shard_map/ppermute | solution.py:310
  30.7 7.9 %collective-permute-start.8 = (f16[264,128]{1,0:T(8,128)(2,1)S(1)}, f16[264,128]{1,0:T(8,128)(2,1)S(1)}, u32[]{:S(2)}, u32[]{:S(2)}) collective-permute-start(f16[264,128]{1,0:T(8,128)(2,1)S(1)} %convert_element_type.62), channel_id=1, source_target_pairs={{0,8},{4,12},{8,0},{12,4},{1,9},{5,13},{9,1},{13,5},{2,10},{6,14},... | collective-permute-start | bytes 202760 | tf_op jit(solution)/shard_map/ppermute | solution.py:310
  33.7 6.2 %collective-permute-start.9 = (f16[264,128]{1,0:T(8,128)(2,1)S(1)}, f16[264,128]{1,0:T(8,128)(2,1)S(1)}, u32[]{:S(2)}, u32[]{:S(2)}) collective-permute-start(f16[264,128]{1,0:T(8,128)(2,1)S(1)} %convert_element_type.62), channel_id=1, source_target_pairs={{0,12},{4,8},{8,4},{12,0},{1,13},{5,9},{9,5},{13,1},{2,14},{6,10},... | collective-permute-start | bytes 202760 | tf_op jit(solution)/shard_map/ppermute | solution.py:310
  44.8 4.3 %collective-permute-start.10 = (f32[2,32,2048]{2,1,0:T(8,128)S(1)}, f32[2,32,2048]{2,1,0:T(8,128)S(1)}, u32[]{:S(2)}, u32[]{:S(2)}) collective-permute-start(f32[2,32,2048]{2,1,0:T(8,128)S(1)} %get-tuple-element.50), channel_id=1, source_target_pairs={{0,1},{1,0},{2,3},{3,2},{4,5},{5,4},{6,7},{7,6},{8,9},{9,8},{10,11... | collective-permute-start | bytes 1572872 | tf_op jit(solution)/shard_map/ppermute | solution.py:310
  49.2 6.0 %collective-permute-start.11 = (bf16[32,2048]{1,0:T(8,128)(2,1)S(1)}, bf16[32,2048]{1,0:T(8,128)(2,1)S(1)}, u32[]{:S(2)}, u32[]{:S(2)}) collective-permute-start(bf16[32,2048]{1,0:T(8,128)(2,1)S(1)} %fusion.6), channel_id=1, source_target_pairs={{0,16},{16,0},{1,17},{17,1},{2,18},{18,2},{3,19},{19,3},{4,20},{20... | collective-permute-start | bytes 393224 | tf_op jit(solution)/shard_map/ppermute | solution.py:310
  55.2 5.2 %collective-permute-start.12 = (bf16[32,2048]{1,0:T(8,128)(2,1)S(1)}, bf16[32,2048]{1,0:T(8,128)(2,1)S(1)}, u32[]{:S(2)}, u32[]{:S(2)}) collective-permute-start(bf16[32,2048]{1,0:T(8,128)(2,1)S(1)} %fusion.7), channel_id=1, source_target_pairs={{0,2},{2,0},{1,3},{3,1},{4,6},{6,4},{5,7},{7,5},{8,10},{10,8},{9,1... | collective-permute-start | bytes 393224 | tf_op jit(solution)/shard_map/ppermute | solution.py:310
  61.2 1.3 %collective-permute-start.13 = (f32[32,512]{1,0:T(8,128)S(1)}, f32[32,512]{1,0:T(8,128)S(1)}, u32[]{:S(2)}, u32[]{:S(2)}) collective-permute-start(f32[32,512]{1,0:T(8,128)S(1)} %slice_add_fusion), channel_id=1, source_target_pairs={{0,1},{1,0},{2,3},{3,2},{4,5},{5,4},{6,7},{7,6},{8,9},{9,8},{10,11... | collective-permute-start | bytes 196616 | tf_op jit(solution)/shard_map/ppermute | solution.py:310
  62.6 4.5 %collective-permute-start.14 = (f16[40,512]{1,0:T(8,128)(2,1)S(1)}, f16[40,512]{1,0:T(8,128)(2,1)S(1)}, u32[]{:S(2)}, u32[]{:S(2)}) collective-permute-start(f16[40,512]{1,0:T(8,128)(2,1)S(1)} %get-tuple-element.53), channel_id=1, source_target_pairs={{0,4},{4,0},{8,12},{12,8},{1,5},{5,1},{9,13},{13,9},{2,6},{6,2},{1... | collective-permute-start | bytes 122888 | tf_op jit(solution)/shard_map/ppermute | solution.py:310
  63.6 6.3 %collective-permute-start.15 = (f16[40,512]{1,0:T(8,128)(2,1)S(1)}, f16[40,512]{1,0:T(8,128)(2,1)S(1)}, u32[]{:S(2)}, u32[]{:S(2)}) collective-permute-start(f16[40,512]{1,0:T(8,128)(2,1)S(1)} %get-tuple-element.53), channel_id=1, source_target_pairs={{0,8},{4,12},{8,0},{12,4},{1,9},{5,13},{9,1},{13,5},{2,10},{6,14},... | collective-permute-start | bytes 122888 | tf_op jit(solution)/shard_map/ppermute | solution.py:310
  65.3 5.8 %collective-permute-start.16 = (f16[40,512]{1,0:T(8,128)(2,1)S(1)}, f16[40,512]{1,0:T(8,128)(2,1)S(1)}, u32[]{:S(2)}, u32[]{:S(2)}) collective-permute-start(f16[40,512]{1,0:T(8,128)(2,1)S(1)} %get-tuple-element.53), channel_id=1, source_target_pairs={{0,12},{4,8},{8,4},{12,0},{1,13},{5,9},{9,5},{13,1},{2,14},{6,10},... | collective-permute-start | bytes 122888 | tf_op jit(solution)/shard_map/ppermute | solution.py:310

commit v5 on v3

--- a/solution.py
+++ b/solution.py
@@ -151,10 +151,9 @@
     out_ref[scores.shape[0] :] = jnp.broadcast_to(k, (PAD, scores.shape[1]))
 
 
-def sum_scores_kernel(*refs):
-    out_ref = refs[-1]
+def sum_scores_kernel(parts_ref, out_ref):
     count = out_ref.shape[0]
-    out_ref[...] = tree_sum([restored(ref[:count], ref[count : count + 1]) for ref in refs[:-1]])
+    out_ref[...] = tree_sum([restored(parts_ref[i, :count], parts_ref[i, count : count + 1]) for i in range(parts_ref.shape[0])])
 
 
 SMALL = jnp.float8_e5m2
@@ -415,12 +414,9 @@
         terms, store_slab, (((1,), (1,)), ((), ())), preferred_element_type=jnp.float32
     )
     scores = scores[: total.shape[0]] + scores[total.shape[0] :]
-    scores = scores + swapped(scores, "sub")
     packed = call(pack_scores_kernel, (scores.shape[0] + PAD, scores.shape[1]), "pack_scores", scores)
-    packed = lax.reduce_precision(packed, 5, 10)
-    wire = packed.astype(jnp.float16)
-    sources = [packed] + [got.astype(jnp.float32) for got in others(lambda d: wire, "row")]
-    return call(sum_scores_kernel, scores.shape, "sum_scores", *sources)
+    whole = lax.all_gather(packed.astype(jnp.float16), ("row", "sub")).astype(jnp.float32)
+    return call(sum_scores_kernel, scores.shape, "sum_scores", whole)
 
 
 def solution(mesh):

time: 71.2 us -> 76.5 us (1.074)
  blocking collectives: 0 us -> 14.3 us
  starting transfers between devices: 24.6 us -> 20.1 us
  waiting for transfers between devices: 11.6 us -> 7.16 us
    all_gather x0 -> x1, blocking collectives: none -> 14.3 us  [body(): lax.all_gather(packed.astype(jnp.float16), ('row', 'sub'))]
    ppermute x13 -> x9, starting transfers between devices: 15.2 us -> 10.7 us  [others(): lax.ppermute(pick(index ^ k), axis, [(i, i ^ k) for i in range(size)])]
    ppermute x13 -> x9, waiting for transfers between devices: 10.9 us -> 6.46 us  [others(): lax.ppermute(pick(index ^ k), axis, [(i, i ^ k) for i in range(size)])]
  transfers between devices with their start and end apart: 19 -> 15, of which waited for: 11 -> 8; matrix products, arithmetic and copies ran while one was open for 0% -> 0% of each run, Pallas kernels for 33% -> 31%
where the time goes in v5:
time: 76.5 us; the launch traced here: 76.4 us
  Pallas kernels  33.2 us (43%)
  starting transfers between devices  20.1 us (26%)
  blocking collectives  14.3 us (19%)
  waiting for transfers between devices  7.16 us (9%)
    pallas_call x3, Pallas kernels, gram_split(): pl.pallas_call(functools.partial(gram_split_kernel, first=first), in_spec...  15.2 us
    all_gather x1, blocking collectives, body(): lax.all_gather(packed.astype(jnp.float16), ('row', 'sub'))  14.3 us
    ppermute x9, starting transfers between devices, others(): lax.ppermute(pick(index ^ k), axis, [(i, i ^ k) for i in range(size)])  10.7 us
    ppermute x9, waiting for transfers between devices, others(): lax.ppermute(pick(index ^ k), axis, [(i, i ^ k) for i in range(size)])  6.46 us
    pallas_call x2, Pallas kernels, project(): pl.pallas_call(functools.partial(project_kernel, targets=targets), in_spe...  6.16 us
    ppermute x3, starting transfers between devices, body(): lax.ppermute(part.astype(jnp.float16), 'row', [(i, i ^ k) for i in range(...  5.82 us
    pallas_call x2, Pallas kernels, home(): pl.pallas_call(home_kernel, in_specs=[index] + [WHOLE] * (5 + len(after))...  5.24 us
    pallas_call x1, Pallas kernels, gram_product(): pl.pallas_call(functools.partial(away_kernel, row_count=row_count, own=ow...  4.9 us
  transfers between devices with their start and end apart: 15, of which 8 were waited for; matrix products, arithmetic and copies ran while one was open for 0% of the time, Pallas kernels for 31%

profile of v5, /device:TPU:0, one launch (start us, length us, event | category | flops | bytes accessed | tf_op | source)
XLA Modules:
  0.0 76.4 jit_solution(17827208582892876145)
XLA Ops:
  0.1 3.1 %project.3 = (f32[528,128]{1,0:T(8,128)S(1)}, f32[528,128]{1,0:T(8,128)S(1)}) custom-call(s32[4]{0:T(128)S(1)} %pad_add_fusion.place_ref, bf16[8,128,1024]{2,1,0:T(8,128)(2,1)} %refs_0_.3, bf16[8,128,1024]{2,1,0:T(8,128)(2,1)} %refs_1_.3, bf16[1024,128]{1,0:T(8,128)(2,1)} %refs_2_.3, bf16[1024,128]{1,0:T(8,128)(2,1)} %refs_3_.3), custom_call_target="tpu_custom_call" | custom-call | tf_op jit(solution)/shard_map/project/pallas_call | solution.py:90
  3.2 4.1 %collective-permute-start.1 = (f16[528,128]{1,0:T(8,128)(2,1)S(1)}, f16[528,128]{1,0:T(8,128)(2,1)S(1)}, u32[]{:S(2)}, u32[]{:S(2)}) collective-permute-start(f16[528,128]{1,0:T(8,128)(2,1)S(1)} %convert_element_type.54), channel_id=1, source_target_pairs={{0,8},{4,12},{8,0},{12,4},{1,9},{5,13},{9,1},{13,5},{2,10},{6,14},... | collective-permute-start | bytes 405512 | tf_op jit(solution)/shard_map/ppermute | solution.py:390
  7.3 1.4 %collective-permute-start = (f16[528,128]{1,0:T(8,128)(2,1)S(1)}, f16[528,128]{1,0:T(8,128)(2,1)S(1)}, u32[]{:S(2)}, u32[]{:S(2)}) collective-permute-start(f16[528,128]{1,0:T(8,128)(2,1)S(1)} %convert_element_type.52), channel_id=1, source_target_pairs={{0,12},{4,8},{8,4},{12,0},{1,13},{5,9},{9,5},{13,1},{2,14},{6,10},... | collective-permute-start | bytes 405512 | tf_op jit(solution)/shard_map/ppermute | solution.py:390
  8.8 3.1 %project.2 = (f32[528,128]{1,0:T(8,128)S(1)}, f32[528,128]{1,0:T(8,128)S(1)}) custom-call(s32[4]{0:T(128)S(1)} %pad_add_fusion.place_ref, bf16[8,128,1024]{2,1,0:T(8,128)(2,1)} %refs_0_.3, bf16[8,128,1024]{2,1,0:T(8,128)(2,1)} %refs_1_.3, bf16[1024,128]{1,0:T(8,128)(2,1)} %refs_2_.3, bf16[1024,128]{1,0:T(8,128)(2,1)} %refs_3_.3), custom_call_target="tpu_custom_call" | custom-call | tf_op jit(solution)/shard_map/project/pallas_call | solution.py:90
  12.2 6.8 %gram_split.3 = (bf16[1024,2048]{1,0:T(8,128)(2,1)S(1)}, f8e5m2[1024,2048]{1,0:T(32,128)(4,1)S(1)}, bf16[1024,2048]{1,0:T(8,128)(2,1)S(1)}, f8e5m2[1024,2048]{1,0:T(32,128)(4,1)S(1)}, f32[8,128]{1,0:T(8,128)S(1)}) custom-call(s32[4]{0:T(128)S(1)} %pad_add_fusion.place_ref, f32[528,128]{1,0:T(8,128)S(1)} %get-tuple-element.32.after_ref.own_ref, ...), custom_call_target="tpu_custom_call" | custom-call | bytes 16777216 | tf_op jit(solution)/shard_map/gram_split/pallas_call | solution.py:211
  19.6 0.9 %kron.1 = (f32[2,32,128]{2,1,0:T(8,128)S(1)}, f32[2,32,128]{2,1,0:T(8,128)S(1)}, f32[2,32,128]{2,1,0:T(8,128)S(1)}, f32[2,32,128]{2,1,0:T(8,128)S(1)}) custom-call(s32[4]{0:T(128)S(1)} %pad_add_fusion.place_ref, f32[8,128]{1,0:T(8,128)S(1)} %get-tuple-element.33.after_ref, f32[528,128]{1,0:T(8,128)S(1)} %get-tuple-element.32.after_ref.own_ref, ...), custom_call_target="tpu_custom_call" | custom-call | tf_op jit(solution)/shard_map/kron/pallas_call | solution.py:367
  20.5 1.6 %collective-permute-start.3 = (f32[2,32,128]{2,1,0:T(8,128)S(1)}, f32[2,32,128]{2,1,0:T(8,128)S(1)}, u32[]{:S(2)}, u32[]{:S(2)}) collective-permute-start(f32[2,32,128]{2,1,0:T(8,128)S(1)} %get-tuple-element.40), channel_id=1, source_target_pairs={{0,2},{2,0},{16,18},{18,16},{1,3},{3,1},{17,19},{19,17},{4,6},{6,4... | collective-permute-start | bytes 98312 | tf_op jit(solution)/shard_map/ppermute | solution.py:360
  22.1 1.5 %collective-permute-start.4 = (f32[2,32,128]{2,1,0:T(8,128)S(1)}, f32[2,32,128]{2,1,0:T(8,128)S(1)}, u32[]{:S(2)}, u32[]{:S(2)}) collective-permute-start(f32[2,32,128]{2,1,0:T(8,128)S(1)} %get-tuple-element.41), channel_id=1, source_target_pairs={{0,16},{2,18},{16,0},{18,2},{1,17},{3,19},{17,1},{19,3},{4,20},{6,... | collective-permute-start | bytes 98312 | tf_op jit(solution)/shard_map/ppermute | solution.py:360
  24.1 4.2 %gram_split.4 = (bf16[1024,2048]{1,0:T(8,128)(2,1)S(1)}, f8e5m2[1024,2048]{1,0:T(32,128)(4,1)S(1)}, f32[8,128]{1,0:T(8,128)S(1)}) custom-call(s32[4]{0:T(128)S(1)} %pad_add_fusion.place_ref, f32[2,32,128]{2,1,0:T(8,128)S(1)} %get-tuple-element.37.after_ref.refs_0_, f32[4096,4096]{1,0:T(8,128)} %gram_ref.5), custom_call_target="tpu_custom_call" | custom-call | bytes 8388608 | tf_op jit(solution)/shard_map/gram_split/pallas_call | solution.py:211
  28.5 1.2 %collective-permute-done.6.refs_4_ = f32[4,32,128]{2,1,0:T(8,128)S(1)} collective-permute-done((f32[4,32,128]{2,1,0:T(8,128)S(1)}, f32[4,32,128]{2,1,0:T(8,128)S(1)}, u32[]{:S(2)}, u32[]{:S(2)}) %collective-permute-start.6) | collective-permute-done | bytes 65568 | tf_op jit(solution)/shard_map/ppermute | solution.py:346
  29.8 3.6 %collective-permute-start.9 = (f16[264,128]{1,0:T(8,128)(2,1)S(1)}, f16[264,128]{1,0:T(8,128)(2,1)S(1)}, u32[]{:S(2)}, u32[]{:S(2)}) collective-permute-start(f16[264,128]{1,0:T(8,128)(2,1)S(1)} %convert_element_type.58), channel_id=1, source_target_pairs={{0,12},{4,8},{8,4},{12,0},{1,13},{5,9},{9,5},{13,1},{2,14},{6,10},... | collective-permute-start | bytes 202760 | tf_op jit(solution)/shard_map/ppermute | solution.py:346
  33.3 0.9 %collective-permute-start.7 = (f16[264,128]{1,0:T(8,128)(2,1)S(1)}, f16[264,128]{1,0:T(8,128)(2,1)S(1)}, u32[]{:S(2)}, u32[]{:S(2)}) collective-permute-start(f16[264,128]{1,0:T(8,128)(2,1)S(1)} %convert_element_type.58), channel_id=1, source_target_pairs={{0,4},{4,0},{8,12},{12,8},{1,5},{5,1},{9,13},{13,9},{2,6},{6,2},{1... | collective-permute-start | bytes 202760 | tf_op jit(solution)/shard_map/ppermute | solution.py:346
  34.2 4.2 %gram_split.5 = (bf16[1024,2048]{1,0:T(8,128)(2,1)S(1)}, f8e5m2[1024,2048]{1,0:T(32,128)(4,1)S(1)}, f32[8,128]{1,0:T(8,128)S(1)}) custom-call(s32[4]{0:T(128)S(1)} %pad_add_fusion.place_ref, f32[264,128]{1,0:T(8,128)S(1)} %pack.1.after_ref.refs_4_, f32[4096,4096]{1,0:T(8,128)} %gram_ref.5), custom_call_target="tpu_custom_call" | custom-call | bytes 8388608 | tf_op jit(solution)/shard_map/gram_split/pallas_call | solution.py:211
  38.5 0.8 %collective-permute-done.8 = f16[264,128]{1,0:T(8,128)(2,1)S(1)} collective-permute-done((f16[264,128]{1,0:T(8,128)(2,1)S(1)}, f16[264,128]{1,0:T(8,128)(2,1)S(1)}, u32[]{:S(2)}, u32[]{:S(2)}) %collective-permute-start.8) | collective-permute-done | bytes 67616 | tf_op jit(solution)/shard_map/ppermute | solution.py:346
  39.4 4.9 %away.1 = (f32[2,2,32,1024]{3,2,1,0:T(8,128)S(1)}, bf16[2048,128]{1,0:T(8,128)(2,1)S(1)}, f8e5m2[2048,64]{1,0:T(32,128)(4,1)S(1)}, f32[8,64]{1,0:T(8,128)S(1)}) custom-call(s32[4]{0:T(128)S(1)} %pad_add_fusion.place_ref, f32[8,128]{1,0:T(8,128)S(1)} %get-tuple-element.44.after_ref, bf16[1024,2048]{1,0:T(8,128)(2,1)S(1)} %get-tuple-element.45.refs_0_, ...), custom_call_target="tpu_custom_call" | custom-call | flops 2147483648 | bytes 4194304 | tf_op jit(solution)/shard_map/away/pallas_call | solution.py:299
  44.4 2.6 %home.2 = f32[2,32,1024]{2,1,0:T(8,128)S(1)} custom-call(s32[4]{0:T(128)S(1)} %pad_add_fusion.place_ref, bf16[1024,2048]{1,0:T(8,128)(2,1)S(1)} %get-tuple-element.38.high_ref, f8e5m2[1024,2048]{1,0:T(32,128)(4,1)S(1)} %get-tuple-element.39.low_ref, bf16[2048,128]{1,0:T(8,128)(2,1)S(1)} %get-tuple-element.49.terms_ref, ...), custom_call_target="tpu_custom_call" | custom-call | flops 1073741824 | bytes 2097152 | tf_op jit(solution)/shard_map/home/pallas_call | solution.py:316
  47.1 1.6 %collective-permute-start.11 = (bf16[32,1024]{1,0:T(8,128)(2,1)S(1)}, bf16[32,1024]{1,0:T(8,128)(2,1)S(1)}, u32[]{:S(2)}, u32[]{:S(2)}) collective-permute-start(bf16[32,1024]{1,0:T(8,128)(2,1)S(1)} %fusion.7.refs_0_), channel_id=1, source_target_pairs={{0,16},{16,0},{1,17},{17,1},{2,18},{18,2},{3,19},{19,3},{4,20},{20... | collective-permute-start | bytes 196616 | tf_op jit(solution)/shard_map/ppermute | solution.py:346
  48.7 2.6 %home.3.late_ref = f32[2,32,1024]{2,1,0:T(8,128)S(1)} custom-call(s32[4]{0:T(128)S(1)} %pad_add_fusion.place_ref, bf16[1024,2048]{1,0:T(8,128)(2,1)S(1)} %get-tuple-element.53.high_ref, f8e5m2[1024,2048]{1,0:T(32,128)(4,1)S(1)} %get-tuple-element.54.low_ref, bf16[2048,128]{1,0:T(8,128)(2,1)S(1)} %get-tuple-element.49.terms_ref, ...), custom_call_target="tpu_custom_call" | custom-call | flops 1073741824 | bytes 2097152 | tf_op jit(solution)/shard_map/home/pallas_call | solution.py:316
  51.7 1.6 %collective-permute-start.13 = (bf16[32,1024]{1,0:T(8,128)(2,1)S(1)}, bf16[32,1024]{1,0:T(8,128)(2,1)S(1)}, u32[]{:S(2)}, u32[]{:S(2)}) collective-permute-start(bf16[32,1024]{1,0:T(8,128)(2,1)S(1)} %get-tuple-element.58), channel_id=1, source_target_pairs={{0,16},{16,0},{1,17},{17,1},{2,18},{18,2},{3,19},{19,3},{4,20},{20... | collective-permute-start | bytes 196616 | tf_op jit(solution)/shard_map/ppermute | solution.py:346
  53.2 1.5 %collective-permute-start.12 = (bf16[32,1024]{1,0:T(8,128)(2,1)S(1)}, bf16[32,1024]{1,0:T(8,128)(2,1)S(1)}, u32[]{:S(2)}, u32[]{:S(2)}) collective-permute-start(bf16[32,1024]{1,0:T(8,128)(2,1)S(1)} %get-tuple-element.56), channel_id=1, source_target_pairs={{0,2},{2,0},{1,3},{3,1},{4,6},{6,4},{5,7},{7,5},{8,10},{10,8},{9,1... | collective-permute-start | bytes 196616 | tf_op jit(solution)/shard_map/ppermute | solution.py:346
  54.7 1.3 %collective-permute-done.13 = bf16[32,1024]{1,0:T(8,128)(2,1)S(1)} collective-permute-done((bf16[32,1024]{1,0:T(8,128)(2,1)S(1)}, bf16[32,1024]{1,0:T(8,128)(2,1)S(1)}, u32[]{:S(2)}, u32[]{:S(2)}) %collective-permute-start.13) | collective-permute-done | bytes 65568 | tf_op jit(solution)/shard_map/ppermute | solution.py:346
  56.0 1.5 %collective-permute-start.14 = (bf16[32,1024]{1,0:T(8,128)(2,1)S(1)}, bf16[32,1024]{1,0:T(8,128)(2,1)S(1)}, u32[]{:S(2)}, u32[]{:S(2)}) collective-permute-start(bf16[32,1024]{1,0:T(8,128)(2,1)S(1)} %fusion.6), channel_id=1, source_target_pairs={{0,2},{2,0},{1,3},{3,1},{4,6},{6,4},{5,7},{7,5},{8,10},{10,8},{9,1... | collective-permute-start | bytes 196616 | tf_op jit(solution)/shard_map/ppermute | solution.py:346
  57.7 2.7 %collective-permute-done.14 = bf16[32,1024]{1,0:T(8,128)(2,1)S(1)} collective-permute-done((bf16[32,1024]{1,0:T(8,128)(2,1)S(1)}, bf16[32,1024]{1,0:T(8,128)(2,1)S(1)}, u32[]{:S(2)}, u32[]{:S(2)}) %collective-permute-start.14) | collective-permute-done | bytes 65568 | tf_op jit(solution)/shard_map/ppermute | solution.py:346
  61.3 14.3 %all-gather = f16[320,512]{1,0:T(8,128)(2,1)S(1)} all-gather(f16[40,512]{1,0:T(8,128)(2,1)S(1)} %convert_element_type.67), channel_id=2, replica_groups=mesh['groups'=2,'row'=4,'col'=2,'sub'=2] {'row','sub'}, dimensions={0}, use_global_device_ids=true | all-gather | bytes 368640 | tf_op jit(solution)/shard_map/all_gather | solution.py:418
  (46 shorter events, 4.0 us)
Async XLA Ops:
  0.0 60.4 %copy-start = (bf16[512,2048]{1,0:T(8,128)(2,1)S(1)}, bf16[512,2048]{1,0:T(8,128)(2,1)}, u32[]{:S(2)}) copy-start(bf16[512,2048]{1,0:T(8,128)(2,1)} %param.11) | copy-start | bytes 6291460
  3.2 15.8 %collective-permute-start.1 = (f16[528,128]{1,0:T(8,128)(2,1)S(1)}, f16[528,128]{1,0:T(8,128)(2,1)S(1)}, u32[]{:S(2)}, u32[]{:S(2)}) collective-permute-start(f16[528,128]{1,0:T(8,128)(2,1)S(1)} %convert_element_type.54), channel_id=1, source_target_pairs={{0,8},{4,12},{8,0},{12,4},{1,9},{5,13},{9,1},{13,5},{2,10},{6,14},... | collective-permute-start | bytes 405512 | tf_op jit(solution)/shard_map/ppermute | solution.py:390
  7.3 11.7 %collective-permute-start = (f16[528,128]{1,0:T(8,128)(2,1)S(1)}, f16[528,128]{1,0:T(8,128)(2,1)S(1)}, u32[]{:S(2)}, u32[]{:S(2)}) collective-permute-start(f16[528,128]{1,0:T(8,128)(2,1)S(1)} %convert_element_type.52), channel_id=1, source_target_pairs={{0,12},{4,8},{8,4},{12,0},{1,13},{5,9},{9,5},{13,1},{2,14},{6,10},... | collective-permute-start | bytes 405512 | tf_op jit(solution)/shard_map/ppermute | solution.py:390
  11.9 7.7 %collective-permute-start.2 = (f16[528,128]{1,0:T(8,128)(2,1)S(1)}, f16[528,128]{1,0:T(8,128)(2,1)S(1)}, u32[]{:S(2)}, u32[]{:S(2)}) collective-permute-start(f16[528,128]{1,0:T(8,128)(2,1)S(1)} %convert_element_type.56), channel_id=1, source_target_pairs={{0,4},{4,0},{8,12},{12,8},{1,5},{5,1},{9,13},{13,9},{2,6},{6,2},{1... | collective-permute-start | bytes 405512 | tf_op jit(solution)/shard_map/ppermute | solution.py:390
  20.5 7.8 %collective-permute-start.3 = (f32[2,32,128]{2,1,0:T(8,128)S(1)}, f32[2,32,128]{2,1,0:T(8,128)S(1)}, u32[]{:S(2)}, u32[]{:S(2)}) collective-permute-start(f32[2,32,128]{2,1,0:T(8,128)S(1)} %get-tuple-element.40), channel_id=1, source_target_pairs={{0,2},{2,0},{16,18},{18,16},{1,3},{3,1},{17,19},{19,17},{4,6},{6,4... | collective-permute-start | bytes 98312 | tf_op jit(solution)/shard_map/ppermute | solution.py:360
  22.1 6.2 %collective-permute-start.4 = (f32[2,32,128]{2,1,0:T(8,128)S(1)}, f32[2,32,128]{2,1,0:T(8,128)S(1)}, u32[]{:S(2)}, u32[]{:S(2)}) collective-permute-start(f32[2,32,128]{2,1,0:T(8,128)S(1)} %get-tuple-element.41), channel_id=1, source_target_pairs={{0,16},{2,18},{16,0},{18,2},{1,17},{3,19},{17,1},{19,3},{4,20},{6,... | collective-permute-start | bytes 98312 | tf_op jit(solution)/shard_map/ppermute | solution.py:360
  23.6 4.8 %collective-permute-start.5 = (f32[2,32,128]{2,1,0:T(8,128)S(1)}, f32[2,32,128]{2,1,0:T(8,128)S(1)}, u32[]{:S(2)}, u32[]{:S(2)}) collective-permute-start(f32[2,32,128]{2,1,0:T(8,128)S(1)} %get-tuple-element.42), channel_id=1, source_target_pairs={{0,18},{2,16},{16,2},{18,0},{1,19},{3,17},{17,3},{19,1},{4,22},{6,... | collective-permute-start | bytes 98312 | tf_op jit(solution)/shard_map/ppermute | solution.py:360
  28.5 1.3 %collective-permute-start.6 = (f32[4,32,128]{2,1,0:T(8,128)S(1)}, f32[4,32,128]{2,1,0:T(8,128)S(1)}, u32[]{:S(2)}, u32[]{:S(2)}) collective-permute-start(f32[4,32,128]{2,1,0:T(8,128)S(1)} %gather.1), channel_id=1, source_target_pairs={{0,1},{1,0},{2,3},{3,2},{4,5},{5,4},{6,7},{7,6},{8,9},{9,8},{10,11... | collective-permute-start | bytes 196616 | tf_op jit(solution)/shard_map/ppermute | solution.py:346
  29.8 8.7 %collective-permute-start.9 = (f16[264,128]{1,0:T(8,128)(2,1)S(1)}, f16[264,128]{1,0:T(8,128)(2,1)S(1)}, u32[]{:S(2)}, u32[]{:S(2)}) collective-permute-start(f16[264,128]{1,0:T(8,128)(2,1)S(1)} %convert_element_type.58), channel_id=1, source_target_pairs={{0,12},{4,8},{8,4},{12,0},{1,13},{5,9},{9,5},{13,1},{2,14},{6,10},... | collective-permute-start | bytes 202760 | tf_op jit(solution)/shard_map/ppermute | solution.py:346
  33.3 6.0 %collective-permute-start.8 = (f16[264,128]{1,0:T(8,128)(2,1)S(1)}, f16[264,128]{1,0:T(8,128)(2,1)S(1)}, u32[]{:S(2)}, u32[]{:S(2)}) collective-permute-start(f16[264,128]{1,0:T(8,128)(2,1)S(1)} %convert_element_type.58), channel_id=1, source_target_pairs={{0,8},{4,12},{8,0},{12,4},{1,9},{5,13},{9,1},{13,5},{2,10},{6,14},... | collective-permute-start | bytes 202760 | tf_op jit(solution)/shard_map/ppermute | solution.py:346
  33.3 6.0 %collective-permute-start.7 = (f16[264,128]{1,0:T(8,128)(2,1)S(1)}, f16[264,128]{1,0:T(8,128)(2,1)S(1)}, u32[]{:S(2)}, u32[]{:S(2)}) collective-permute-start(f16[264,128]{1,0:T(8,128)(2,1)S(1)} %convert_element_type.58), channel_id=1, source_target_pairs={{0,4},{4,0},{8,12},{12,8},{1,5},{5,1},{9,13},{13,9},{2,6},{6,2},{1... | collective-permute-start | bytes 202760 | tf_op jit(solution)/shard_map/ppermute | solution.py:346
  44.3 2.7 %collective-permute-start.10 = (f32[2,2,32,1024]{3,2,1,0:T(8,128)S(1)}, f32[2,2,32,1024]{3,2,1,0:T(8,128)S(1)}, u32[]{:S(2)}, u32[]{:S(2)}) collective-permute-start(f32[2,2,32,1024]{3,2,1,0:T(8,128)S(1)} %get-tuple-element.52), channel_id=1, source_target_pairs={{0,1},{1,0},{2,3},{3,2},{4,5},{5,4},{6,7},{7,6},{8,9},{9,8},{10,11... | collective-permute-start | bytes 1572872 | tf_op jit(solution)/shard_map/ppermute | solution.py:346
  47.1 4.6 %collective-permute-start.11 = (bf16[32,1024]{1,0:T(8,128)(2,1)S(1)}, bf16[32,1024]{1,0:T(8,128)(2,1)S(1)}, u32[]{:S(2)}, u32[]{:S(2)}) collective-permute-start(bf16[32,1024]{1,0:T(8,128)(2,1)S(1)} %fusion.7.refs_0_), channel_id=1, source_target_pairs={{0,16},{16,0},{1,17},{17,1},{2,18},{18,2},{3,19},{19,3},{4,20},{20... | collective-permute-start | bytes 196616 | tf_op jit(solution)/shard_map/ppermute | solution.py:346
  51.7 4.3 %collective-permute-start.13 = (bf16[32,1024]{1,0:T(8,128)(2,1)S(1)}, bf16[32,1024]{1,0:T(8,128)(2,1)S(1)}, u32[]{:S(2)}, u32[]{:S(2)}) collective-permute-start(bf16[32,1024]{1,0:T(8,128)(2,1)S(1)} %get-tuple-element.58), channel_id=1, source_target_pairs={{0,16},{16,0},{1,17},{17,1},{2,18},{18,2},{3,19},{19,3},{4,20},{20... | collective-permute-start | bytes 196616 | tf_op jit(solution)/shard_map/ppermute | solution.py:346
  53.2 4.4 %collective-permute-start.12 = (bf16[32,1024]{1,0:T(8,128)(2,1)S(1)}, bf16[32,1024]{1,0:T(8,128)(2,1)S(1)}, u32[]{:S(2)}, u32[]{:S(2)}) collective-permute-start(bf16[32,1024]{1,0:T(8,128)(2,1)S(1)} %get-tuple-element.56), channel_id=1, source_target_pairs={{0,2},{2,0},{1,3},{3,1},{4,6},{6,4},{5,7},{7,5},{8,10},{10,8},{9,1... | collective-permute-start | bytes 196616 | tf_op jit(solution)/shard_map/ppermute | solution.py:346
  56.0 4.3 %collective-permute-start.14 = (bf16[32,1024]{1,0:T(8,128)(2,1)S(1)}, bf16[32,1024]{1,0:T(8,128)(2,1)S(1)}, u32[]{:S(2)}, u32[]{:S(2)}) collective-permute-start(bf16[32,1024]{1,0:T(8,128)(2,1)S(1)} %fusion.6), channel_id=1, source_target_pairs={{0,2},{2,0},{1,3},{3,1},{4,6},{6,4},{5,7},{7,5},{8,10},{10,8},{9,1... | collective-permute-start | bytes 196616 | tf_op jit(solution)/shard_map/ppermute | solution.py:346

commit v6 on v3

--- a/solution.py
+++ b/solution.py
@@ -384,7 +384,8 @@
     own = queries // row_count
     in_width, out_width = proj_in.shape[1], proj_out.shape[1]
     got = []
-    for targets in (range(row_count)[: row_count // 2 - 1 : -1], range(row_count)[: row_count // 2][::-1]):
+    order = range(row_count)[::-1]
+    for targets in (order[:1], order[1:]) if row_count > 1 else (order,):
         parts = project(targets, row_count, place, query_acts, query_grads, proj_in, proj_out)
         for k, part in zip(targets, parts):
             if k:

time: 71.2 us -> 71.5 us (level)
    ppermute x13, waiting for transfers between devices: 10.9 us -> 10 us  [others(): lax.ppermute(pick(index ^ k), axis, [(i, i ^ k) for i in range(size)])]
    ppermute x3, waiting for transfers between devices: 0.54 us -> 1.43 us  [body(): lax.ppermute(part.astype(jnp.float16), 'row', [(i, i ^ k) for i in range(...]
  transfers between devices with their start and end apart: 19 -> 19, of which waited for: 11 -> 11; matrix products, arithmetic and copies ran while one was open for 0% -> 0% of each run, Pallas kernels for 33% -> 34%
where the time goes in v6:
time: 71.5 us; the launch traced here: 71.3 us
  Pallas kernels  33.5 us (47%)
  starting transfers between devices  24.6 us (34%)
  waiting for transfers between devices  11.6 us (16%)
  matrix products  0.76 us (1%)
    ppermute x13, starting transfers between devices, others(): lax.ppermute(pick(index ^ k), axis, [(i, i ^ k) for i in range(size)])  15.2 us
    pallas_call x3, Pallas kernels, gram_split(): pl.pallas_call(functools.partial(gram_split_kernel, first=first), in_spec...  15.2 us
    ppermute x13, waiting for transfers between devices, others(): lax.ppermute(pick(index ^ k), axis, [(i, i ^ k) for i in range(size)])  10 us
    pallas_call x2, Pallas kernels, project(): pl.pallas_call(functools.partial(project_kernel, targets=targets), in_spe...  6.5 us
    ppermute x3, starting transfers between devices, body(): lax.ppermute(part.astype(jnp.float16), 'row', [(i, i ^ k) for i in range(...  5.81 us
    pallas_call x2, Pallas kernels, home(): pl.pallas_call(home_kernel, in_specs=[index] + [WHOLE] * (5 + len(after))...  5.23 us
    pallas_call x1, Pallas kernels, gram_product(): pl.pallas_call(functools.partial(away_kernel, row_count=row_count, own=ow...  4.9 us
    ppermute x3, starting transfers between devices, peers(): lax.ppermute(pick(k), ('groups', 'col'), [(i, i ^ k) for i in range(4)])  3.55 us
  transfers between devices with their start and end apart: 19, of which 11 were waited for; matrix products, arithmetic and copies ran while one was open for 0% of the time, Pallas kernels for 34%

profile of v6, /device:TPU:0, one launch (start us, length us, event | category | flops | bytes accessed | tf_op | source)
XLA Modules:
  0.0 71.3 jit_solution(17973457470794260652)
XLA Ops:
  0.1 2.4 %project.3 = f32[528,128]{1,0:T(8,128)S(1)} custom-call(s32[4]{0:T(128)S(1)} %pad_add_fusion.place_ref, bf16[8,128,1024]{2,1,0:T(8,128)(2,1)} %refs_0_.3, bf16[8,128,1024]{2,1,0:T(8,128)(2,1)} %refs_1_.3, bf16[1024,128]{1,0:T(8,128)(2,1)} %refs_2_.3, bf16[1024,128]{1,0:T(8,128)(2,1)} %refs_3_.3), custom_call_target="tpu_custom_call" | custom-call | tf_op jit(solution)/shard_map/project/pallas_call | solution.py:90
  2.5 5.1 %collective-permute-start = (f16[528,128]{1,0:T(8,128)(2,1)S(1)}, f16[528,128]{1,0:T(8,128)(2,1)S(1)}, u32[]{:S(2)}, u32[]{:S(2)}) collective-permute-start(f16[528,128]{1,0:T(8,128)(2,1)S(1)} %convert_element_type.58), channel_id=1, source_target_pairs={{0,12},{4,8},{8,4},{12,0},{1,13},{5,9},{9,5},{13,1},{2,14},{6,10},... | collective-permute-start | bytes 405512 | tf_op jit(solution)/shard_map/ppermute | solution.py:392
  7.6 4.1 %project.2 = (f32[528,128]{1,0:T(8,128)S(1)}, f32[528,128]{1,0:T(8,128)S(1)}, f32[528,128]{1,0:T(8,128)S(1)}) custom-call(s32[4]{0:T(128)S(1)} %pad_add_fusion.place_ref, bf16[8,128,1024]{2,1,0:T(8,128)(2,1)} %refs_0_.3, bf16[8,128,1024]{2,1,0:T(8,128)(2,1)} %refs_1_.3, bf16[1024,128]{1,0:T(8,128)(2,1)} %refs_2_.3, bf16[1024,128]{1,0:T(8,128)(2,1)} %refs_3_.3), custom_call_target="tpu_custom_call" | custom-call | tf_op jit(solution)/shard_map/project/pallas_call | solution.py:90
  12.5 6.8 %gram_split.3 = (bf16[1024,2048]{1,0:T(8,128)(2,1)S(1)}, f8e5m2[1024,2048]{1,0:T(32,128)(4,1)S(1)}, bf16[1024,2048]{1,0:T(8,128)(2,1)S(1)}, f8e5m2[1024,2048]{1,0:T(32,128)(4,1)S(1)}, f32[8,128]{1,0:T(8,128)S(1)}) custom-call(s32[4]{0:T(128)S(1)} %pad_add_fusion.place_ref, f32[528,128]{1,0:T(8,128)S(1)} %get-tuple-element.31.after_ref.own_ref, ...), custom_call_target="tpu_custom_call" | custom-call | bytes 16777216 | tf_op jit(solution)/shard_map/gram_split/pallas_call | solution.py:212
  19.4 1.4 %collective-permute-done.1 = f16[528,128]{1,0:T(8,128)(2,1)S(1)} collective-permute-done((f16[528,128]{1,0:T(8,128)(2,1)S(1)}, f16[528,128]{1,0:T(8,128)(2,1)S(1)}, u32[]{:S(2)}, u32[]{:S(2)}) %collective-permute-start.1) | collective-permute-done | bytes 135200 | tf_op jit(solution)/shard_map/ppermute | solution.py:392
  21.7 1.6 %collective-permute-start.3 = (f32[2,32,128]{2,1,0:T(8,128)S(1)}, f32[2,32,128]{2,1,0:T(8,128)S(1)}, u32[]{:S(2)}, u32[]{:S(2)}) collective-permute-start(f32[2,32,128]{2,1,0:T(8,128)S(1)} %get-tuple-element.38), channel_id=1, source_target_pairs={{0,2},{2,0},{16,18},{18,16},{1,3},{3,1},{17,19},{19,17},{4,6},{6,4... | collective-permute-start | bytes 98312 | tf_op jit(solution)/shard_map/ppermute | solution.py:361
  23.3 1.5 %collective-permute-start.4 = (f32[2,32,128]{2,1,0:T(8,128)S(1)}, f32[2,32,128]{2,1,0:T(8,128)S(1)}, u32[]{:S(2)}, u32[]{:S(2)}) collective-permute-start(f32[2,32,128]{2,1,0:T(8,128)S(1)} %get-tuple-element.39), channel_id=1, source_target_pairs={{0,16},{2,18},{16,0},{18,2},{1,17},{3,19},{17,1},{19,3},{4,20},{6,... | collective-permute-start | bytes 98312 | tf_op jit(solution)/shard_map/ppermute | solution.py:361
  25.3 4.2 %gram_split.4 = (bf16[1024,2048]{1,0:T(8,128)(2,1)S(1)}, f8e5m2[1024,2048]{1,0:T(32,128)(4,1)S(1)}, f32[8,128]{1,0:T(8,128)S(1)}) custom-call(s32[4]{0:T(128)S(1)} %pad_add_fusion.place_ref, f32[2,32,128]{2,1,0:T(8,128)S(1)} %get-tuple-element.35.after_ref.refs_0_, f32[4096,4096]{1,0:T(8,128)} %gram_ref.5), custom_call_target="tpu_custom_call" | custom-call | bytes 8388608 | tf_op jit(solution)/shard_map/gram_split/pallas_call | solution.py:212
  31.0 2.5 %collective-permute-start.9 = (f16[264,128]{1,0:T(8,128)(2,1)S(1)}, f16[264,128]{1,0:T(8,128)(2,1)S(1)}, u32[]{:S(2)}, u32[]{:S(2)}) collective-permute-start(f16[264,128]{1,0:T(8,128)(2,1)S(1)} %convert_element_type.64), channel_id=1, source_target_pairs={{0,12},{4,8},{8,4},{12,0},{1,13},{5,9},{9,5},{13,1},{2,14},{6,10},... | collective-permute-start | bytes 202760 | tf_op jit(solution)/shard_map/ppermute | solution.py:347
  33.4 2.0 %collective-permute-start.7 = (f16[264,128]{1,0:T(8,128)(2,1)S(1)}, f16[264,128]{1,0:T(8,128)(2,1)S(1)}, u32[]{:S(2)}, u32[]{:S(2)}) collective-permute-start(f16[264,128]{1,0:T(8,128)(2,1)S(1)} %convert_element_type.64), channel_id=1, source_target_pairs={{0,4},{4,0},{8,12},{12,8},{1,5},{5,1},{9,13},{13,9},{2,6},{6,2},{1... | collective-permute-start | bytes 202760 | tf_op jit(solution)/shard_map/ppermute | solution.py:347
  35.4 4.2 %gram_split.5 = (bf16[1024,2048]{1,0:T(8,128)(2,1)S(1)}, f8e5m2[1024,2048]{1,0:T(32,128)(4,1)S(1)}, f32[8,128]{1,0:T(8,128)S(1)}) custom-call(s32[4]{0:T(128)S(1)} %pad_add_fusion.place_ref, f32[264,128]{1,0:T(8,128)S(1)} %pack.1.after_ref.refs_4_, f32[4096,4096]{1,0:T(8,128)} %gram_ref.5), custom_call_target="tpu_custom_call" | custom-call | bytes 8388608 | tf_op jit(solution)/shard_map/gram_split/pallas_call | solution.py:212
  40.0 4.9 %away.1 = (f32[2,2,32,1024]{3,2,1,0:T(8,128)S(1)}, bf16[2048,128]{1,0:T(8,128)(2,1)S(1)}, f8e5m2[2048,64]{1,0:T(32,128)(4,1)S(1)}, f32[8,64]{1,0:T(8,128)S(1)}) custom-call(s32[4]{0:T(128)S(1)} %pad_add_fusion.place_ref, f32[8,128]{1,0:T(8,128)S(1)} %get-tuple-element.42.after_ref, bf16[1024,2048]{1,0:T(8,128)(2,1)S(1)} %get-tuple-element.43.refs_0_, ...), custom_call_target="tpu_custom_call" | custom-call | flops 2147483648 | bytes 4194304 | tf_op jit(solution)/shard_map/away/pallas_call | solution.py:300
  45.0 2.6 %home.2 = f32[2,32,1024]{2,1,0:T(8,128)S(1)} custom-call(s32[4]{0:T(128)S(1)} %pad_add_fusion.place_ref, bf16[1024,2048]{1,0:T(8,128)(2,1)S(1)} %get-tuple-element.36.high_ref, f8e5m2[1024,2048]{1,0:T(32,128)(4,1)S(1)} %get-tuple-element.37.low_ref, bf16[2048,128]{1,0:T(8,128)(2,1)S(1)} %get-tuple-element.47.terms_ref, ...), custom_call_target="tpu_custom_call" | custom-call | flops 1073741824 | bytes 2097152 | tf_op jit(solution)/shard_map/home/pallas_call | solution.py:317
  47.7 1.6 %collective-permute-start.11 = (bf16[32,1024]{1,0:T(8,128)(2,1)S(1)}, bf16[32,1024]{1,0:T(8,128)(2,1)S(1)}, u32[]{:S(2)}, u32[]{:S(2)}) collective-permute-start(bf16[32,1024]{1,0:T(8,128)(2,1)S(1)} %fusion.7.refs_0_), channel_id=1, source_target_pairs={{0,16},{16,0},{1,17},{17,1},{2,18},{18,2},{3,19},{19,3},{4,20},{20... | collective-permute-start | bytes 196616 | tf_op jit(solution)/shard_map/ppermute | solution.py:347
  49.3 2.6 %home.3.late_ref = f32[2,32,1024]{2,1,0:T(8,128)S(1)} custom-call(s32[4]{0:T(128)S(1)} %pad_add_fusion.place_ref, bf16[1024,2048]{1,0:T(8,128)(2,1)S(1)} %get-tuple-element.51.high_ref, f8e5m2[1024,2048]{1,0:T(32,128)(4,1)S(1)} %get-tuple-element.52.low_ref, bf16[2048,128]{1,0:T(8,128)(2,1)S(1)} %get-tuple-element.47.terms_ref, ...), custom_call_target="tpu_custom_call" | custom-call | flops 1073741824 | bytes 2097152 | tf_op jit(solution)/shard_map/home/pallas_call | solution.py:317
  52.3 1.6 %collective-permute-start.13 = (bf16[32,1024]{1,0:T(8,128)(2,1)S(1)}, bf16[32,1024]{1,0:T(8,128)(2,1)S(1)}, u32[]{:S(2)}, u32[]{:S(2)}) collective-permute-start(bf16[32,1024]{1,0:T(8,128)(2,1)S(1)} %get-tuple-element.56), channel_id=1, source_target_pairs={{0,16},{16,0},{1,17},{17,1},{2,18},{18,2},{3,19},{19,3},{4,20},{20... | collective-permute-start | bytes 196616 | tf_op jit(solution)/shard_map/ppermute | solution.py:347
  53.9 1.5 %collective-permute-start.12 = (bf16[32,1024]{1,0:T(8,128)(2,1)S(1)}, bf16[32,1024]{1,0:T(8,128)(2,1)S(1)}, u32[]{:S(2)}, u32[]{:S(2)}) collective-permute-start(bf16[32,1024]{1,0:T(8,128)(2,1)S(1)} %get-tuple-element.54), channel_id=1, source_target_pairs={{0,2},{2,0},{1,3},{3,1},{4,6},{6,4},{5,7},{7,5},{8,10},{10,8},{9,1... | collective-permute-start | bytes 196616 | tf_op jit(solution)/shard_map/ppermute | solution.py:347
  55.3 1.3 %collective-permute-done.13 = bf16[32,1024]{1,0:T(8,128)(2,1)S(1)} collective-permute-done((bf16[32,1024]{1,0:T(8,128)(2,1)S(1)}, bf16[32,1024]{1,0:T(8,128)(2,1)S(1)}, u32[]{:S(2)}, u32[]{:S(2)}) %collective-permute-start.13) | collective-permute-done | bytes 65568 | tf_op jit(solution)/shard_map/ppermute | solution.py:347
  56.6 1.5 %collective-permute-start.14 = (bf16[32,1024]{1,0:T(8,128)(2,1)S(1)}, bf16[32,1024]{1,0:T(8,128)(2,1)S(1)}, u32[]{:S(2)}, u32[]{:S(2)}) collective-permute-start(bf16[32,1024]{1,0:T(8,128)(2,1)S(1)} %fusion.6), channel_id=1, source_target_pairs={{0,2},{2,0},{1,3},{3,1},{4,6},{6,4},{5,7},{7,5},{8,10},{10,8},{9,1... | collective-permute-start | bytes 196616 | tf_op jit(solution)/shard_map/ppermute | solution.py:347
  58.3 2.7 %collective-permute-done.14 = bf16[32,1024]{1,0:T(8,128)(2,1)S(1)} collective-permute-done((bf16[32,1024]{1,0:T(8,128)(2,1)S(1)}, bf16[32,1024]{1,0:T(8,128)(2,1)S(1)}, u32[]{:S(2)}, u32[]{:S(2)}) %collective-permute-start.14) | collective-permute-done | bytes 65568 | tf_op jit(solution)/shard_map/ppermute | solution.py:347
  63.3 2.5 %collective-permute-start.18 = (f16[40,512]{1,0:T(8,128)(2,1)S(1)}, f16[40,512]{1,0:T(8,128)(2,1)S(1)}, u32[]{:S(2)}, u32[]{:S(2)}) collective-permute-start(f16[40,512]{1,0:T(8,128)(2,1)S(1)} %get-tuple-element.59), channel_id=1, source_target_pairs={{0,12},{4,8},{8,4},{12,0},{1,13},{5,9},{9,5},{13,1},{2,14},{6,10},... | collective-permute-start | bytes 122888 | tf_op jit(solution)/shard_map/ppermute | solution.py:347
  65.7 2.0 %collective-permute-start.16 = (f16[40,512]{1,0:T(8,128)(2,1)S(1)}, f16[40,512]{1,0:T(8,128)(2,1)S(1)}, u32[]{:S(2)}, u32[]{:S(2)}) collective-permute-start(f16[40,512]{1,0:T(8,128)(2,1)S(1)} %get-tuple-element.59), channel_id=1, source_target_pairs={{0,4},{4,0},{8,12},{12,8},{1,5},{5,1},{9,13},{13,9},{2,6},{6,2},{1... | collective-permute-start | bytes 122888 | tf_op jit(solution)/shard_map/ppermute | solution.py:347
  67.7 1.5 %collective-permute-done.18 = f16[40,512]{1,0:T(8,128)(2,1)S(1)} collective-permute-done((f16[40,512]{1,0:T(8,128)(2,1)S(1)}, f16[40,512]{1,0:T(8,128)(2,1)S(1)}, u32[]{:S(2)}, u32[]{:S(2)}) %collective-permute-start.18) | collective-permute-done | bytes 40992 | tf_op jit(solution)/shard_map/ppermute | solution.py:347
  69.2 1.4 %collective-permute-done.17 = f16[40,512]{1,0:T(8,128)(2,1)S(1)} collective-permute-done((f16[40,512]{1,0:T(8,128)(2,1)S(1)}, f16[40,512]{1,0:T(8,128)(2,1)S(1)}, u32[]{:S(2)}, u32[]{:S(2)}) %collective-permute-start.17) | collective-permute-done | bytes 40992 | tf_op jit(solution)/shard_map/ppermute | solution.py:347
  (56 shorter events, 7.6 us)
Async XLA Ops:
  0.0 61.0 %copy-start = (bf16[512,2048]{1,0:T(8,128)(2,1)S(1)}, bf16[512,2048]{1,0:T(8,128)(2,1)}, u32[]{:S(2)}) copy-start(bf16[512,2048]{1,0:T(8,128)(2,1)} %param.11) | copy-start | bytes 6291460
  2.5 16.8 %collective-permute-start = (f16[528,128]{1,0:T(8,128)(2,1)S(1)}, f16[528,128]{1,0:T(8,128)(2,1)S(1)}, u32[]{:S(2)}, u32[]{:S(2)}) collective-permute-start(f16[528,128]{1,0:T(8,128)(2,1)S(1)} %convert_element_type.58), channel_id=1, source_target_pairs={{0,12},{4,8},{8,4},{12,0},{1,13},{5,9},{9,5},{13,1},{2,14},{6,10},... | collective-permute-start | bytes 405512 | tf_op jit(solution)/shard_map/ppermute | solution.py:392
  11.8 7.6 %collective-permute-start.2 = (f16[528,128]{1,0:T(8,128)(2,1)S(1)}, f16[528,128]{1,0:T(8,128)(2,1)S(1)}, u32[]{:S(2)}, u32[]{:S(2)}) collective-permute-start(f16[528,128]{1,0:T(8,128)(2,1)S(1)} %convert_element_type.62), channel_id=1, source_target_pairs={{0,4},{4,0},{8,12},{12,8},{1,5},{5,1},{9,13},{13,9},{2,6},{6,2},{1... | collective-permute-start | bytes 405512 | tf_op jit(solution)/shard_map/ppermute | solution.py:392
  11.9 9.0 %collective-permute-start.1 = (f16[528,128]{1,0:T(8,128)(2,1)S(1)}, f16[528,128]{1,0:T(8,128)(2,1)S(1)}, u32[]{:S(2)}, u32[]{:S(2)}) collective-permute-start(f16[528,128]{1,0:T(8,128)(2,1)S(1)} %convert_element_type.60), channel_id=1, source_target_pairs={{0,8},{4,12},{8,0},{12,4},{1,9},{5,13},{9,1},{13,5},{2,10},{6,14},... | collective-permute-start | bytes 405512 | tf_op jit(solution)/shard_map/ppermute | solution.py:392
  21.7 7.8 %collective-permute-start.3 = (f32[2,32,128]{2,1,0:T(8,128)S(1)}, f32[2,32,128]{2,1,0:T(8,128)S(1)}, u32[]{:S(2)}, u32[]{:S(2)}) collective-permute-start(f32[2,32,128]{2,1,0:T(8,128)S(1)} %get-tuple-element.38), channel_id=1, source_target_pairs={{0,2},{2,0},{16,18},{18,16},{1,3},{3,1},{17,19},{19,17},{4,6},{6,4... | collective-permute-start | bytes 98312 | tf_op jit(solution)/shard_map/ppermute | solution.py:361
  23.3 6.2 %collective-permute-start.4 = (f32[2,32,128]{2,1,0:T(8,128)S(1)}, f32[2,32,128]{2,1,0:T(8,128)S(1)}, u32[]{:S(2)}, u32[]{:S(2)}) collective-permute-start(f32[2,32,128]{2,1,0:T(8,128)S(1)} %get-tuple-element.39), channel_id=1, source_target_pairs={{0,16},{2,18},{16,0},{18,2},{1,17},{3,19},{17,1},{19,3},{4,20},{6,... | collective-permute-start | bytes 98312 | tf_op jit(solution)/shard_map/ppermute | solution.py:361
  24.8 4.8 %collective-permute-start.5 = (f32[2,32,128]{2,1,0:T(8,128)S(1)}, f32[2,32,128]{2,1,0:T(8,128)S(1)}, u32[]{:S(2)}, u32[]{:S(2)}) collective-permute-start(f32[2,32,128]{2,1,0:T(8,128)S(1)} %get-tuple-element.40), channel_id=1, source_target_pairs={{0,18},{2,16},{16,2},{18,0},{1,19},{3,17},{17,3},{19,1},{4,22},{6,... | collective-permute-start | bytes 98312 | tf_op jit(solution)/shard_map/ppermute | solution.py:361
  29.6 1.3 %collective-permute-start.6 = (f32[4,32,128]{2,1,0:T(8,128)S(1)}, f32[4,32,128]{2,1,0:T(8,128)S(1)}, u32[]{:S(2)}, u32[]{:S(2)}) collective-permute-start(f32[4,32,128]{2,1,0:T(8,128)S(1)} %gather.1), channel_id=1, source_target_pairs={{0,1},{1,0},{2,3},{3,2},{4,5},{5,4},{6,7},{7,6},{8,9},{9,8},{10,11... | collective-permute-start | bytes 196616 | tf_op jit(solution)/shard_map/ppermute | solution.py:347
  31.0 8.7 %collective-permute-start.9 = (f16[264,128]{1,0:T(8,128)(2,1)S(1)}, f16[264,128]{1,0:T(8,128)(2,1)S(1)}, u32[]{:S(2)}, u32[]{:S(2)}) collective-permute-start(f16[264,128]{1,0:T(8,128)(2,1)S(1)} %convert_element_type.64), channel_id=1, source_target_pairs={{0,12},{4,8},{8,4},{12,0},{1,13},{5,9},{9,5},{13,1},{2,14},{6,10},... | collective-permute-start | bytes 202760 | tf_op jit(solution)/shard_map/ppermute | solution.py:347
  33.4 6.5 %collective-permute-start.8 = (f16[264,128]{1,0:T(8,128)(2,1)S(1)}, f16[264,128]{1,0:T(8,128)(2,1)S(1)}, u32[]{:S(2)}, u32[]{:S(2)}) collective-permute-start(f16[264,128]{1,0:T(8,128)(2,1)S(1)} %convert_element_type.64), channel_id=1, source_target_pairs={{0,8},{4,12},{8,0},{12,4},{1,9},{5,13},{9,1},{13,5},{2,10},{6,14},... | collective-permute-start | bytes 202760 | tf_op jit(solution)/shard_map/ppermute | solution.py:347
  33.4 6.5 %collective-permute-start.7 = (f16[264,128]{1,0:T(8,128)(2,1)S(1)}, f16[264,128]{1,0:T(8,128)(2,1)S(1)}, u32[]{:S(2)}, u32[]{:S(2)}) collective-permute-start(f16[264,128]{1,0:T(8,128)(2,1)S(1)} %convert_element_type.64), channel_id=1, source_target_pairs={{0,4},{4,0},{8,12},{12,8},{1,5},{5,1},{9,13},{13,9},{2,6},{6,2},{1... | collective-permute-start | bytes 202760 | tf_op jit(solution)/shard_map/ppermute | solution.py:347
  44.9 2.7 %collective-permute-start.10 = (f32[2,2,32,1024]{3,2,1,0:T(8,128)S(1)}, f32[2,2,32,1024]{3,2,1,0:T(8,128)S(1)}, u32[]{:S(2)}, u32[]{:S(2)}) collective-permute-start(f32[2,2,32,1024]{3,2,1,0:T(8,128)S(1)} %get-tuple-element.50), channel_id=1, source_target_pairs={{0,1},{1,0},{2,3},{3,2},{4,5},{5,4},{6,7},{7,6},{8,9},{9,8},{10,11... | collective-permute-start | bytes 1572872 | tf_op jit(solution)/shard_map/ppermute | solution.py:347
  47.7 4.6 %collective-permute-start.11 = (bf16[32,1024]{1,0:T(8,128)(2,1)S(1)}, bf16[32,1024]{1,0:T(8,128)(2,1)S(1)}, u32[]{:S(2)}, u32[]{:S(2)}) collective-permute-start(bf16[32,1024]{1,0:T(8,128)(2,1)S(1)} %fusion.7.refs_0_), channel_id=1, source_target_pairs={{0,16},{16,0},{1,17},{17,1},{2,18},{18,2},{3,19},{19,3},{4,20},{20... | collective-permute-start | bytes 196616 | tf_op jit(solution)/shard_map/ppermute | solution.py:347
  52.3 4.3 %collective-permute-start.13 = (bf16[32,1024]{1,0:T(8,128)(2,1)S(1)}, bf16[32,1024]{1,0:T(8,128)(2,1)S(1)}, u32[]{:S(2)}, u32[]{:S(2)}) collective-permute-start(bf16[32,1024]{1,0:T(8,128)(2,1)S(1)} %get-tuple-element.56), channel_id=1, source_target_pairs={{0,16},{16,0},{1,17},{17,1},{2,18},{18,2},{3,19},{19,3},{4,20},{20... | collective-permute-start | bytes 196616 | tf_op jit(solution)/shard_map/ppermute | solution.py:347
  53.9 4.4 %collective-permute-start.12 = (bf16[32,1024]{1,0:T(8,128)(2,1)S(1)}, bf16[32,1024]{1,0:T(8,128)(2,1)S(1)}, u32[]{:S(2)}, u32[]{:S(2)}) collective-permute-start(bf16[32,1024]{1,0:T(8,128)(2,1)S(1)} %get-tuple-element.54), channel_id=1, source_target_pairs={{0,2},{2,0},{1,3},{3,1},{4,6},{6,4},{5,7},{7,5},{8,10},{10,8},{9,1... | collective-permute-start | bytes 196616 | tf_op jit(solution)/shard_map/ppermute | solution.py:347
  56.6 4.3 %collective-permute-start.14 = (bf16[32,1024]{1,0:T(8,128)(2,1)S(1)}, bf16[32,1024]{1,0:T(8,128)(2,1)S(1)}, u32[]{:S(2)}, u32[]{:S(2)}) collective-permute-start(bf16[32,1024]{1,0:T(8,128)(2,1)S(1)} %fusion.6), channel_id=1, source_target_pairs={{0,2},{2,0},{1,3},{3,1},{4,6},{6,4},{5,7},{7,5},{8,10},{10,8},{9,1... | collective-permute-start | bytes 196616 | tf_op jit(solution)/shard_map/ppermute | solution.py:347
  61.8 1.3 %collective-permute-start.15 = (f32[32,512]{1,0:T(8,128)S(1)}, f32[32,512]{1,0:T(8,128)S(1)}, u32[]{:S(2)}, u32[]{:S(2)}) collective-permute-start(f32[32,512]{1,0:T(8,128)S(1)} %slice_add_fusion), channel_id=1, source_target_pairs={{0,1},{1,0},{2,3},{3,2},{4,5},{5,4},{6,7},{7,6},{8,9},{9,8},{10,11... | collective-permute-start | bytes 196616 | tf_op jit(solution)/shard_map/ppermute | solution.py:347
  63.3 5.9 %collective-permute-start.18 = (f16[40,512]{1,0:T(8,128)(2,1)S(1)}, f16[40,512]{1,0:T(8,128)(2,1)S(1)}, u32[]{:S(2)}, u32[]{:S(2)}) collective-permute-start(f16[40,512]{1,0:T(8,128)(2,1)S(1)} %get-tuple-element.59), channel_id=1, source_target_pairs={{0,12},{4,8},{8,4},{12,0},{1,13},{5,9},{9,5},{13,1},{2,14},{6,10},... | collective-permute-start | bytes 122888 | tf_op jit(solution)/shard_map/ppermute | solution.py:347
  65.7 4.9 %collective-permute-start.17 = (f16[40,512]{1,0:T(8,128)(2,1)S(1)}, f16[40,512]{1,0:T(8,128)(2,1)S(1)}, u32[]{:S(2)}, u32[]{:S(2)}) collective-permute-start(f16[40,512]{1,0:T(8,128)(2,1)S(1)} %get-tuple-element.59), channel_id=1, source_target_pairs={{0,8},{4,12},{8,0},{12,4},{1,9},{5,13},{9,1},{13,5},{2,10},{6,14},... | collective-permute-start | bytes 122888 | tf_op jit(solution)/shard_map/ppermute | solution.py:347
  65.7 4.9 %collective-permute-start.16 = (f16[40,512]{1,0:T(8,128)(2,1)S(1)}, f16[40,512]{1,0:T(8,128)(2,1)S(1)}, u32[]{:S(2)}, u32[]{:S(2)}) collective-permute-start(f16[40,512]{1,0:T(8,128)(2,1)S(1)} %get-tuple-element.59), channel_id=1, source_target_pairs={{0,4},{4,0},{8,12},{12,8},{1,5},{5,1},{9,13},{13,9},{2,6},{6,2},{1... | collective-permute-start | bytes 122888 | tf_op jit(solution)/shard_map/ppermute | solution.py:347

commit v7 on v3

--- a/solution.py
+++ b/solution.py
@@ -103,6 +103,11 @@
     )(place, *[pltpu.with_memory_space_constraint(x, pltpu.HBM) for x in (query_acts, query_grads, proj_in, proj_out)])
 
 
+def two_terms(block):
+    high = block.astype(jnp.bfloat16)
+    return high, (block - high.astype(jnp.float32)).astype(jnp.bfloat16)
+
+
 def kron_kernel(place_ref, after_ref, own_ref, *refs, tokens):
     del after_ref
     refs, outs, scratch = refs[:-5], refs[-5:-1], refs[-1]
@@ -120,9 +125,10 @@
     group, col, sub = place_ref[0], place_ref[2], place_ref[3]
     for j in range(count // tokens):
         rows = slice(j * tokens, (j + 1) * tokens)
-        scratch[j] = lax.dot_general(
-            acts[rows], grads[rows], (((0,), (0,)), ((), ())), precision=HIGHEST, preferred_element_type=jnp.float32
-        )
+        act_high, act_low = two_terms(acts[rows].T)
+        grad_high, grad_low = two_terms(grads[rows])
+        dot = functools.partial(jnp.dot, preferred_element_type=jnp.float32)
+        scratch[j] = dot(act_high, grad_high) + (dot(act_high, grad_low) + dot(act_low, grad_high))
         for k in range(4):
             for s in range(2):
                 start = (((col ^ (k % 2)) * 2 + (sub ^ s)) * 2 + (group ^ (k // 2))) * height

time: 71.2 us -> 71.2 us (level)
  no operation moved by 1% of the time
where the time goes in v7:
time: 71.2 us; the launch traced here: 71 us
  Pallas kernels  33.1 us (46%)
  starting transfers between devices  24.6 us (35%)
  waiting for transfers between devices  11.6 us (16%)
  matrix products  0.76 us (1%)
    pallas_call x3, Pallas kernels, gram_split(): pl.pallas_call(functools.partial(gram_split_kernel, first=first), in_spec...  15.2 us
    ppermute x13, starting transfers between devices, others(): lax.ppermute(pick(index ^ k), axis, [(i, i ^ k) for i in range(size)])  15.2 us
    ppermute x13, waiting for transfers between devices, others(): lax.ppermute(pick(index ^ k), axis, [(i, i ^ k) for i in range(size)])  10.9 us
    pallas_call x2, Pallas kernels, project(): pl.pallas_call(functools.partial(project_kernel, targets=targets), in_spe...  6.16 us
    ppermute x3, starting transfers between devices, body(): lax.ppermute(part.astype(jnp.float16), 'row', [(i, i ^ k) for i in range(...  5.82 us
    pallas_call x2, Pallas kernels, home(): pl.pallas_call(home_kernel, in_specs=[index] + [WHOLE] * (5 + len(after))...  5.23 us
    pallas_call x1, Pallas kernels, gram_product(): pl.pallas_call(functools.partial(away_kernel, row_count=row_count, own=ow...  4.9 us
    ppermute x3, starting transfers between devices, peers(): lax.ppermute(pick(k), ('groups', 'col'), [(i, i ^ k) for i in range(4)])  3.55 us
  transfers between devices with their start and end apart: 19, of which 11 were waited for; matrix products, arithmetic and copies ran while one was open for 0% of the time, Pallas kernels for 33%

profile of v7, /device:TPU:0, one launch (start us, length us, event | category | flops | bytes accessed | tf_op | source)
XLA Modules:
  0.0 71.0 jit_solution(3754887906744828497)
XLA Ops:
  0.1 3.1 %project.3 = (f32[528,128]{1,0:T(8,128)S(1)}, f32[528,128]{1,0:T(8,128)S(1)}) custom-call(s32[4]{0:T(128)S(1)} %pad_add_fusion.place_ref, bf16[8,128,1024]{2,1,0:T(8,128)(2,1)} %refs_0_.3, bf16[8,128,1024]{2,1,0:T(8,128)(2,1)} %refs_1_.3, bf16[1024,128]{1,0:T(8,128)(2,1)} %refs_2_.3, bf16[1024,128]{1,0:T(8,128)(2,1)} %refs_3_.3), custom_call_target="tpu_custom_call" | custom-call | tf_op jit(solution)/shard_map/project/pallas_call | solution.py:90
  3.2 4.1 %collective-permute-start.1 = (f16[528,128]{1,0:T(8,128)(2,1)S(1)}, f16[528,128]{1,0:T(8,128)(2,1)S(1)}, u32[]{:S(2)}, u32[]{:S(2)}) collective-permute-start(f16[528,128]{1,0:T(8,128)(2,1)S(1)} %convert_element_type.60), channel_id=1, source_target_pairs={{0,8},{4,12},{8,0},{12,4},{1,9},{5,13},{9,1},{13,5},{2,10},{6,14},... | collective-permute-start | bytes 405512 | tf_op jit(solution)/shard_map/ppermute | solution.py:397
  7.3 1.4 %collective-permute-start = (f16[528,128]{1,0:T(8,128)(2,1)S(1)}, f16[528,128]{1,0:T(8,128)(2,1)S(1)}, u32[]{:S(2)}, u32[]{:S(2)}) collective-permute-start(f16[528,128]{1,0:T(8,128)(2,1)S(1)} %convert_element_type.58), channel_id=1, source_target_pairs={{0,12},{4,8},{8,4},{12,0},{1,13},{5,9},{9,5},{13,1},{2,14},{6,10},... | collective-permute-start | bytes 405512 | tf_op jit(solution)/shard_map/ppermute | solution.py:397
  8.8 3.1 %project.2 = (f32[528,128]{1,0:T(8,128)S(1)}, f32[528,128]{1,0:T(8,128)S(1)}) custom-call(s32[4]{0:T(128)S(1)} %pad_add_fusion.place_ref, bf16[8,128,1024]{2,1,0:T(8,128)(2,1)} %refs_0_.3, bf16[8,128,1024]{2,1,0:T(8,128)(2,1)} %refs_1_.3, bf16[1024,128]{1,0:T(8,128)(2,1)} %refs_2_.3, bf16[1024,128]{1,0:T(8,128)(2,1)} %refs_3_.3), custom_call_target="tpu_custom_call" | custom-call | tf_op jit(solution)/shard_map/project/pallas_call | solution.py:90
  12.2 6.8 %gram_split.3 = (bf16[1024,2048]{1,0:T(8,128)(2,1)S(1)}, f8e5m2[1024,2048]{1,0:T(32,128)(4,1)S(1)}, bf16[1024,2048]{1,0:T(8,128)(2,1)S(1)}, f8e5m2[1024,2048]{1,0:T(32,128)(4,1)S(1)}, f32[8,128]{1,0:T(8,128)S(1)}) custom-call(s32[4]{0:T(128)S(1)} %pad_add_fusion.place_ref, f32[528,128]{1,0:T(8,128)S(1)} %get-tuple-element.32.after_ref.own_ref, ...), custom_call_target="tpu_custom_call" | custom-call | bytes 16777216 | tf_op jit(solution)/shard_map/gram_split/pallas_call | solution.py:218
  20.5 1.6 %collective-permute-start.3 = (f32[2,32,128]{2,1,0:T(8,128)S(1)}, f32[2,32,128]{2,1,0:T(8,128)S(1)}, u32[]{:S(2)}, u32[]{:S(2)}) collective-permute-start(f32[2,32,128]{2,1,0:T(8,128)S(1)} %get-tuple-element.40), channel_id=1, source_target_pairs={{0,2},{2,0},{16,18},{18,16},{1,3},{3,1},{17,19},{19,17},{4,6},{6,4... | collective-permute-start | bytes 98312 | tf_op jit(solution)/shard_map/ppermute | solution.py:367
  22.1 1.5 %collective-permute-start.4 = (f32[2,32,128]{2,1,0:T(8,128)S(1)}, f32[2,32,128]{2,1,0:T(8,128)S(1)}, u32[]{:S(2)}, u32[]{:S(2)}) collective-permute-start(f32[2,32,128]{2,1,0:T(8,128)S(1)} %get-tuple-element.41), channel_id=1, source_target_pairs={{0,16},{2,18},{16,0},{18,2},{1,17},{3,19},{17,1},{19,3},{4,20},{6,... | collective-permute-start | bytes 98312 | tf_op jit(solution)/shard_map/ppermute | solution.py:367
  24.0 4.2 %gram_split.4 = (bf16[1024,2048]{1,0:T(8,128)(2,1)S(1)}, f8e5m2[1024,2048]{1,0:T(32,128)(4,1)S(1)}, f32[8,128]{1,0:T(8,128)S(1)}) custom-call(s32[4]{0:T(128)S(1)} %pad_add_fusion.place_ref, f32[2,32,128]{2,1,0:T(8,128)S(1)} %get-tuple-element.37.after_ref.refs_0_, f32[4096,4096]{1,0:T(8,128)} %gram_ref.5), custom_call_target="tpu_custom_call" | custom-call | bytes 8388608 | tf_op jit(solution)/shard_map/gram_split/pallas_call | solution.py:218
  28.4 1.2 %collective-permute-done.6.refs_4_ = f32[4,32,128]{2,1,0:T(8,128)S(1)} collective-permute-done((f32[4,32,128]{2,1,0:T(8,128)S(1)}, f32[4,32,128]{2,1,0:T(8,128)S(1)}, u32[]{:S(2)}, u32[]{:S(2)}) %collective-permute-start.6) | collective-permute-done | bytes 65568 | tf_op jit(solution)/shard_map/ppermute | solution.py:353
  29.7 3.6 %collective-permute-start.9 = (f16[264,128]{1,0:T(8,128)(2,1)S(1)}, f16[264,128]{1,0:T(8,128)(2,1)S(1)}, u32[]{:S(2)}, u32[]{:S(2)}) collective-permute-start(f16[264,128]{1,0:T(8,128)(2,1)S(1)} %convert_element_type.64), channel_id=1, source_target_pairs={{0,12},{4,8},{8,4},{12,0},{1,13},{5,9},{9,5},{13,1},{2,14},{6,10},... | collective-permute-start | bytes 202760 | tf_op jit(solution)/shard_map/ppermute | solution.py:353
  34.2 4.2 %gram_split.5 = (bf16[1024,2048]{1,0:T(8,128)(2,1)S(1)}, f8e5m2[1024,2048]{1,0:T(32,128)(4,1)S(1)}, f32[8,128]{1,0:T(8,128)S(1)}) custom-call(s32[4]{0:T(128)S(1)} %pad_add_fusion.place_ref, f32[264,128]{1,0:T(8,128)S(1)} %pack.1.after_ref.refs_4_, f32[4096,4096]{1,0:T(8,128)} %gram_ref.5), custom_call_target="tpu_custom_call" | custom-call | bytes 8388608 | tf_op jit(solution)/shard_map/gram_split/pallas_call | solution.py:218
  39.3 4.9 %away.1 = (f32[2,2,32,1024]{3,2,1,0:T(8,128)S(1)}, bf16[2048,128]{1,0:T(8,128)(2,1)S(1)}, f8e5m2[2048,64]{1,0:T(32,128)(4,1)S(1)}, f32[8,64]{1,0:T(8,128)S(1)}) custom-call(s32[4]{0:T(128)S(1)} %pad_add_fusion.place_ref, f32[8,128]{1,0:T(8,128)S(1)} %get-tuple-element.44.after_ref, bf16[1024,2048]{1,0:T(8,128)(2,1)S(1)} %get-tuple-element.45.refs_0_, ...), custom_call_target="tpu_custom_call" | custom-call | flops 2147483648 | bytes 4194304 | tf_op jit(solution)/shard_map/away/pallas_call | solution.py:306
  44.3 2.6 %home.2 = f32[2,32,1024]{2,1,0:T(8,128)S(1)} custom-call(s32[4]{0:T(128)S(1)} %pad_add_fusion.place_ref, bf16[1024,2048]{1,0:T(8,128)(2,1)S(1)} %get-tuple-element.38.high_ref, f8e5m2[1024,2048]{1,0:T(32,128)(4,1)S(1)} %get-tuple-element.39.low_ref, bf16[2048,128]{1,0:T(8,128)(2,1)S(1)} %get-tuple-element.49.terms_ref, ...), custom_call_target="tpu_custom_call" | custom-call | flops 1073741824 | bytes 2097152 | tf_op jit(solution)/shard_map/home/pallas_call | solution.py:323
  47.0 1.6 %collective-permute-start.11 = (bf16[32,1024]{1,0:T(8,128)(2,1)S(1)}, bf16[32,1024]{1,0:T(8,128)(2,1)S(1)}, u32[]{:S(2)}, u32[]{:S(2)}) collective-permute-start(bf16[32,1024]{1,0:T(8,128)(2,1)S(1)} %fusion.7.refs_0_), channel_id=1, source_target_pairs={{0,16},{16,0},{1,17},{17,1},{2,18},{18,2},{3,19},{19,3},{4,20},{20... | collective-permute-start | bytes 196616 | tf_op jit(solution)/shard_map/ppermute | solution.py:353
  48.6 2.6 %home.3.late_ref = f32[2,32,1024]{2,1,0:T(8,128)S(1)} custom-call(s32[4]{0:T(128)S(1)} %pad_add_fusion.place_ref, bf16[1024,2048]{1,0:T(8,128)(2,1)S(1)} %get-tuple-element.53.high_ref, f8e5m2[1024,2048]{1,0:T(32,128)(4,1)S(1)} %get-tuple-element.54.low_ref, bf16[2048,128]{1,0:T(8,128)(2,1)S(1)} %get-tuple-element.49.terms_ref, ...), custom_call_target="tpu_custom_call" | custom-call | flops 1073741824 | bytes 2097152 | tf_op jit(solution)/shard_map/home/pallas_call | solution.py:323
  51.6 1.6 %collective-permute-start.13 = (bf16[32,1024]{1,0:T(8,128)(2,1)S(1)}, bf16[32,1024]{1,0:T(8,128)(2,1)S(1)}, u32[]{:S(2)}, u32[]{:S(2)}) collective-permute-start(bf16[32,1024]{1,0:T(8,128)(2,1)S(1)} %get-tuple-element.58), channel_id=1, source_target_pairs={{0,16},{16,0},{1,17},{17,1},{2,18},{18,2},{3,19},{19,3},{4,20},{20... | collective-permute-start | bytes 196616 | tf_op jit(solution)/shard_map/ppermute | solution.py:353
  53.2 1.5 %collective-permute-start.12 = (bf16[32,1024]{1,0:T(8,128)(2,1)S(1)}, bf16[32,1024]{1,0:T(8,128)(2,1)S(1)}, u32[]{:S(2)}, u32[]{:S(2)}) collective-permute-start(bf16[32,1024]{1,0:T(8,128)(2,1)S(1)} %get-tuple-element.56), channel_id=1, source_target_pairs={{0,2},{2,0},{1,3},{3,1},{4,6},{6,4},{5,7},{7,5},{8,10},{10,8},{9,1... | collective-permute-start | bytes 196616 | tf_op jit(solution)/shard_map/ppermute | solution.py:353
  54.7 1.3 %collective-permute-done.13 = bf16[32,1024]{1,0:T(8,128)(2,1)S(1)} collective-permute-done((bf16[32,1024]{1,0:T(8,128)(2,1)S(1)}, bf16[32,1024]{1,0:T(8,128)(2,1)S(1)}, u32[]{:S(2)}, u32[]{:S(2)}) %collective-permute-start.13) | collective-permute-done | bytes 65568 | tf_op jit(solution)/shard_map/ppermute | solution.py:353
  56.0 1.5 %collective-permute-start.14 = (bf16[32,1024]{1,0:T(8,128)(2,1)S(1)}, bf16[32,1024]{1,0:T(8,128)(2,1)S(1)}, u32[]{:S(2)}, u32[]{:S(2)}) collective-permute-start(bf16[32,1024]{1,0:T(8,128)(2,1)S(1)} %fusion.6), channel_id=1, source_target_pairs={{0,2},{2,0},{1,3},{3,1},{4,6},{6,4},{5,7},{7,5},{8,10},{10,8},{9,1... | collective-permute-start | bytes 196616 | tf_op jit(solution)/shard_map/ppermute | solution.py:353
  57.6 2.7 %collective-permute-done.14 = bf16[32,1024]{1,0:T(8,128)(2,1)S(1)} collective-permute-done((bf16[32,1024]{1,0:T(8,128)(2,1)S(1)}, bf16[32,1024]{1,0:T(8,128)(2,1)S(1)}, u32[]{:S(2)}, u32[]{:S(2)}) %collective-permute-start.14) | collective-permute-done | bytes 65568 | tf_op jit(solution)/shard_map/ppermute | solution.py:353
  62.6 2.8 %collective-permute-start.18 = (f16[40,512]{1,0:T(8,128)(2,1)S(1)}, f16[40,512]{1,0:T(8,128)(2,1)S(1)}, u32[]{:S(2)}, u32[]{:S(2)}) collective-permute-start(f16[40,512]{1,0:T(8,128)(2,1)S(1)} %get-tuple-element.61), channel_id=1, source_target_pairs={{0,12},{4,8},{8,4},{12,0},{1,13},{5,9},{9,5},{13,1},{2,14},{6,10},... | collective-permute-start | bytes 122888 | tf_op jit(solution)/shard_map/ppermute | solution.py:353
  65.4 1.7 %collective-permute-start.16 = (f16[40,512]{1,0:T(8,128)(2,1)S(1)}, f16[40,512]{1,0:T(8,128)(2,1)S(1)}, u32[]{:S(2)}, u32[]{:S(2)}) collective-permute-start(f16[40,512]{1,0:T(8,128)(2,1)S(1)} %get-tuple-element.61), channel_id=1, source_target_pairs={{0,4},{4,0},{8,12},{12,8},{1,5},{5,1},{9,13},{13,9},{2,6},{6,2},{1... | collective-permute-start | bytes 122888 | tf_op jit(solution)/shard_map/ppermute | solution.py:353
  67.1 1.6 %collective-permute-done.18 = f16[40,512]{1,0:T(8,128)(2,1)S(1)} collective-permute-done((f16[40,512]{1,0:T(8,128)(2,1)S(1)}, f16[40,512]{1,0:T(8,128)(2,1)S(1)}, u32[]{:S(2)}, u32[]{:S(2)}) %collective-permute-start.18) | collective-permute-done | bytes 40992 | tf_op jit(solution)/shard_map/ppermute | solution.py:353
  68.6 1.7 %collective-permute-done.17 = f16[40,512]{1,0:T(8,128)(2,1)S(1)} collective-permute-done((f16[40,512]{1,0:T(8,128)(2,1)S(1)}, f16[40,512]{1,0:T(8,128)(2,1)S(1)}, u32[]{:S(2)}, u32[]{:S(2)}) %collective-permute-start.17) | collective-permute-done | bytes 40992 | tf_op jit(solution)/shard_map/ppermute | solution.py:353
  (56 shorter events, 7.9 us)
Async XLA Ops:
  0.0 60.4 %copy-start = (bf16[512,2048]{1,0:T(8,128)(2,1)S(1)}, bf16[512,2048]{1,0:T(8,128)(2,1)}, u32[]{:S(2)}) copy-start(bf16[512,2048]{1,0:T(8,128)(2,1)} %param.11) | copy-start | bytes 6291460
  3.2 15.8 %collective-permute-start.1 = (f16[528,128]{1,0:T(8,128)(2,1)S(1)}, f16[528,128]{1,0:T(8,128)(2,1)S(1)}, u32[]{:S(2)}, u32[]{:S(2)}) collective-permute-start(f16[528,128]{1,0:T(8,128)(2,1)S(1)} %convert_element_type.60), channel_id=1, source_target_pairs={{0,8},{4,12},{8,0},{12,4},{1,9},{5,13},{9,1},{13,5},{2,10},{6,14},... | collective-permute-start | bytes 405512 | tf_op jit(solution)/shard_map/ppermute | solution.py:397
  7.3 11.7 %collective-permute-start = (f16[528,128]{1,0:T(8,128)(2,1)S(1)}, f16[528,128]{1,0:T(8,128)(2,1)S(1)}, u32[]{:S(2)}, u32[]{:S(2)}) collective-permute-start(f16[528,128]{1,0:T(8,128)(2,1)S(1)} %convert_element_type.58), channel_id=1, source_target_pairs={{0,12},{4,8},{8,4},{12,0},{1,13},{5,9},{9,5},{13,1},{2,14},{6,10},... | collective-permute-start | bytes 405512 | tf_op jit(solution)/shard_map/ppermute | solution.py:397
  11.9 7.7 %collective-permute-start.2 = (f16[528,128]{1,0:T(8,128)(2,1)S(1)}, f16[528,128]{1,0:T(8,128)(2,1)S(1)}, u32[]{:S(2)}, u32[]{:S(2)}) collective-permute-start(f16[528,128]{1,0:T(8,128)(2,1)S(1)} %convert_element_type.62), channel_id=1, source_target_pairs={{0,4},{4,0},{8,12},{12,8},{1,5},{5,1},{9,13},{13,9},{2,6},{6,2},{1... | collective-permute-start | bytes 405512 | tf_op jit(solution)/shard_map/ppermute | solution.py:397
  20.5 7.8 %collective-permute-start.3 = (f32[2,32,128]{2,1,0:T(8,128)S(1)}, f32[2,32,128]{2,1,0:T(8,128)S(1)}, u32[]{:S(2)}, u32[]{:S(2)}) collective-permute-start(f32[2,32,128]{2,1,0:T(8,128)S(1)} %get-tuple-element.40), channel_id=1, source_target_pairs={{0,2},{2,0},{16,18},{18,16},{1,3},{3,1},{17,19},{19,17},{4,6},{6,4... | collective-permute-start | bytes 98312 | tf_op jit(solution)/shard_map/ppermute | solution.py:367
  22.1 6.2 %collective-permute-start.4 = (f32[2,32,128]{2,1,0:T(8,128)S(1)}, f32[2,32,128]{2,1,0:T(8,128)S(1)}, u32[]{:S(2)}, u32[]{:S(2)}) collective-permute-start(f32[2,32,128]{2,1,0:T(8,128)S(1)} %get-tuple-element.41), channel_id=1, source_target_pairs={{0,16},{2,18},{16,0},{18,2},{1,17},{3,19},{17,1},{19,3},{4,20},{6,... | collective-permute-start | bytes 98312 | tf_op jit(solution)/shard_map/ppermute | solution.py:367
  23.6 4.8 %collective-permute-start.5 = (f32[2,32,128]{2,1,0:T(8,128)S(1)}, f32[2,32,128]{2,1,0:T(8,128)S(1)}, u32[]{:S(2)}, u32[]{:S(2)}) collective-permute-start(f32[2,32,128]{2,1,0:T(8,128)S(1)} %get-tuple-element.42), channel_id=1, source_target_pairs={{0,18},{2,16},{16,2},{18,0},{1,19},{3,17},{17,3},{19,1},{4,22},{6,... | collective-permute-start | bytes 98312 | tf_op jit(solution)/shard_map/ppermute | solution.py:367
  28.4 1.3 %collective-permute-start.6 = (f32[4,32,128]{2,1,0:T(8,128)S(1)}, f32[4,32,128]{2,1,0:T(8,128)S(1)}, u32[]{:S(2)}, u32[]{:S(2)}) collective-permute-start(f32[4,32,128]{2,1,0:T(8,128)S(1)} %gather.1), channel_id=1, source_target_pairs={{0,1},{1,0},{2,3},{3,2},{4,5},{5,4},{6,7},{7,6},{8,9},{9,8},{10,11... | collective-permute-start | bytes 196616 | tf_op jit(solution)/shard_map/ppermute | solution.py:353
  29.7 8.7 %collective-permute-start.9 = (f16[264,128]{1,0:T(8,128)(2,1)S(1)}, f16[264,128]{1,0:T(8,128)(2,1)S(1)}, u32[]{:S(2)}, u32[]{:S(2)}) collective-permute-start(f16[264,128]{1,0:T(8,128)(2,1)S(1)} %convert_element_type.64), channel_id=1, source_target_pairs={{0,12},{4,8},{8,4},{12,0},{1,13},{5,9},{9,5},{13,1},{2,14},{6,10},... | collective-permute-start | bytes 202760 | tf_op jit(solution)/shard_map/ppermute | solution.py:353
  33.3 6.0 %collective-permute-start.8 = (f16[264,128]{1,0:T(8,128)(2,1)S(1)}, f16[264,128]{1,0:T(8,128)(2,1)S(1)}, u32[]{:S(2)}, u32[]{:S(2)}) collective-permute-start(f16[264,128]{1,0:T(8,128)(2,1)S(1)} %convert_element_type.64), channel_id=1, source_target_pairs={{0,8},{4,12},{8,0},{12,4},{1,9},{5,13},{9,1},{13,5},{2,10},{6,14},... | collective-permute-start | bytes 202760 | tf_op jit(solution)/shard_map/ppermute | solution.py:353
  33.3 6.0 %collective-permute-start.7 = (f16[264,128]{1,0:T(8,128)(2,1)S(1)}, f16[264,128]{1,0:T(8,128)(2,1)S(1)}, u32[]{:S(2)}, u32[]{:S(2)}) collective-permute-start(f16[264,128]{1,0:T(8,128)(2,1)S(1)} %convert_element_type.64), channel_id=1, source_target_pairs={{0,4},{4,0},{8,12},{12,8},{1,5},{5,1},{9,13},{13,9},{2,6},{6,2},{1... | collective-permute-start | bytes 202760 | tf_op jit(solution)/shard_map/ppermute | solution.py:353
  44.2 2.7 %collective-permute-start.10 = (f32[2,2,32,1024]{3,2,1,0:T(8,128)S(1)}, f32[2,2,32,1024]{3,2,1,0:T(8,128)S(1)}, u32[]{:S(2)}, u32[]{:S(2)}) collective-permute-start(f32[2,2,32,1024]{3,2,1,0:T(8,128)S(1)} %get-tuple-element.52), channel_id=1, source_target_pairs={{0,1},{1,0},{2,3},{3,2},{4,5},{5,4},{6,7},{7,6},{8,9},{9,8},{10,11... | collective-permute-start | bytes 1572872 | tf_op jit(solution)/shard_map/ppermute | solution.py:353
  47.0 4.6 %collective-permute-start.11 = (bf16[32,1024]{1,0:T(8,128)(2,1)S(1)}, bf16[32,1024]{1,0:T(8,128)(2,1)S(1)}, u32[]{:S(2)}, u32[]{:S(2)}) collective-permute-start(bf16[32,1024]{1,0:T(8,128)(2,1)S(1)} %fusion.7.refs_0_), channel_id=1, source_target_pairs={{0,16},{16,0},{1,17},{17,1},{2,18},{18,2},{3,19},{19,3},{4,20},{20... | collective-permute-start | bytes 196616 | tf_op jit(solution)/shard_map/ppermute | solution.py:353
  51.6 4.3 %collective-permute-start.13 = (bf16[32,1024]{1,0:T(8,128)(2,1)S(1)}, bf16[32,1024]{1,0:T(8,128)(2,1)S(1)}, u32[]{:S(2)}, u32[]{:S(2)}) collective-permute-start(bf16[32,1024]{1,0:T(8,128)(2,1)S(1)} %get-tuple-element.58), channel_id=1, source_target_pairs={{0,16},{16,0},{1,17},{17,1},{2,18},{18,2},{3,19},{19,3},{4,20},{20... | collective-permute-start | bytes 196616 | tf_op jit(solution)/shard_map/ppermute | solution.py:353
  53.2 4.4 %collective-permute-start.12 = (bf16[32,1024]{1,0:T(8,128)(2,1)S(1)}, bf16[32,1024]{1,0:T(8,128)(2,1)S(1)}, u32[]{:S(2)}, u32[]{:S(2)}) collective-permute-start(bf16[32,1024]{1,0:T(8,128)(2,1)S(1)} %get-tuple-element.56), channel_id=1, source_target_pairs={{0,2},{2,0},{1,3},{3,1},{4,6},{6,4},{5,7},{7,5},{8,10},{10,8},{9,1... | collective-permute-start | bytes 196616 | tf_op jit(solution)/shard_map/ppermute | solution.py:353
  56.0 4.3 %collective-permute-start.14 = (bf16[32,1024]{1,0:T(8,128)(2,1)S(1)}, bf16[32,1024]{1,0:T(8,128)(2,1)S(1)}, u32[]{:S(2)}, u32[]{:S(2)}) collective-permute-start(bf16[32,1024]{1,0:T(8,128)(2,1)S(1)} %fusion.6), channel_id=1, source_target_pairs={{0,2},{2,0},{1,3},{3,1},{4,6},{6,4},{5,7},{7,5},{8,10},{10,8},{9,1... | collective-permute-start | bytes 196616 | tf_op jit(solution)/shard_map/ppermute | solution.py:353
  61.2 1.3 %collective-permute-start.15 = (f32[32,512]{1,0:T(8,128)S(1)}, f32[32,512]{1,0:T(8,128)S(1)}, u32[]{:S(2)}, u32[]{:S(2)}) collective-permute-start(f32[32,512]{1,0:T(8,128)S(1)} %slice_add_fusion), channel_id=1, source_target_pairs={{0,1},{1,0},{2,3},{3,2},{4,5},{5,4},{6,7},{7,6},{8,9},{9,8},{10,11... | collective-permute-start | bytes 196616 | tf_op jit(solution)/shard_map/ppermute | solution.py:353
  62.6 6.0 %collective-permute-start.18 = (f16[40,512]{1,0:T(8,128)(2,1)S(1)}, f16[40,512]{1,0:T(8,128)(2,1)S(1)}, u32[]{:S(2)}, u32[]{:S(2)}) collective-permute-start(f16[40,512]{1,0:T(8,128)(2,1)S(1)} %get-tuple-element.61), channel_id=1, source_target_pairs={{0,12},{4,8},{8,4},{12,0},{1,13},{5,9},{9,5},{13,1},{2,14},{6,10},... | collective-permute-start | bytes 122888 | tf_op jit(solution)/shard_map/ppermute | solution.py:353
  65.4 4.9 %collective-permute-start.17 = (f16[40,512]{1,0:T(8,128)(2,1)S(1)}, f16[40,512]{1,0:T(8,128)(2,1)S(1)}, u32[]{:S(2)}, u32[]{:S(2)}) collective-permute-start(f16[40,512]{1,0:T(8,128)(2,1)S(1)} %get-tuple-element.61), channel_id=1, source_target_pairs={{0,8},{4,12},{8,0},{12,4},{1,9},{5,13},{9,1},{13,5},{2,10},{6,14},... | collective-permute-start | bytes 122888 | tf_op jit(solution)/shard_map/ppermute | solution.py:353
  65.4 4.9 %collective-permute-start.16 = (f16[40,512]{1,0:T(8,128)(2,1)S(1)}, f16[40,512]{1,0:T(8,128)(2,1)S(1)}, u32[]{:S(2)}, u32[]{:S(2)}) collective-permute-start(f16[40,512]{1,0:T(8,128)(2,1)S(1)} %get-tuple-element.61), channel_id=1, source_target_pairs={{0,4},{4,0},{8,12},{12,8},{1,5},{5,1},{9,13},{13,9},{2,6},{6,2},{1... | collective-permute-start | bytes 122888 | tf_op jit(solution)/shard_map/ppermute | solution.py:353
